TPU v7x, 32 devices: a whole 2x2x4 slice. The times are simulated.
32 devices in a mesh: dp: 8 (over z, core), tensor: 4 (over y, x).
Axes of the slice: x: 2, y: 2, z: 4, core: 2. Of those that a mesh axis runs over, the one named last changes fastest.
Arguments:
- tokens: bfloat16 [12288, 1024], P('dp'), may hold values from -6 to 6
- image_ids: int32 [12288], P('dp'), may hold values from 0 to 8, never falling along the last dimension, each value on 1 to 1370 neighbouring positions
- cotangent: bfloat16 [12288, 1024], P('dp'), may hold values from -6 to 6
- ln1_gain: float32 [2, 1024], replicated, may hold values from 0.25 to 1.75
- ln1_bias: float32 [2, 1024], replicated, may hold values from -3 to 3
- qkv_weight: bfloat16 [2, 1024, 3, 1024], P(None, None, None, 'tensor'), may hold values from -0.1875 to 0.1875
- qv_bias: float32 [2, 2, 1024], P(None, None, 'tensor'), may hold values from -3 to 3
- proj_weight: bfloat16 [2, 1024, 1024], P(None, 'tensor'), may hold values from -3 to 3
- proj_bias: float32 [2, 1024], replicated, may hold values from -5 to 5
- scale_attn: float32 [2, 1024], replicated, may hold values from 0.3 to 1.5
- ln2_gain: float32 [2, 1024], replicated, may hold values from 0.25 to 1.75
- ln2_bias: float32 [2, 1024], replicated, may hold values from -2 to 2
- fc1_weight: bfloat16 [2, 1024, 4096], P(None, None, 'tensor'), may hold values from -0.1875 to 0.1875
- fc1_bias: float32 [2, 4096], P(None, 'tensor'), may hold values from -3 to 3
- fc2_weight: bfloat16 [2, 4096, 1024], P(None, 'tensor'), may hold values from -0.09375 to 0.09375
- fc2_bias: float32 [2, 1024], replicated, may hold values from -2 to 2
- scale_mlp: float32 [2, 1024], replicated, may hold values from 0.3 to 1.5
Outputs:
- output: float32 [12288, 1024], P('dp')
- grad_tokens: float32 [12288, 1024], P('dp')
- grad_ln1_gain: float32 [2, 1024], replicated
- grad_ln1_bias: float32 [2, 1024], replicated
- grad_qkv_weight: float32 [2, 1024, 3, 1024], P(None, None, None, 'tensor')
- grad_qv_bias: float32 [2, 2, 1024], P(None, None, 'tensor')
- grad_proj_weight: float32 [2, 1024, 1024], P(None, 'tensor')
- grad_proj_bias: float32 [2, 1024], replicated
- grad_scale_attn: float32 [2, 1024], replicated
- grad_ln2_gain: float32 [2, 1024], replicated
- grad_ln2_bias: float32 [2, 1024], replicated
- grad_fc1_weight: float32 [2, 1024, 4096], P(None, None, 'tensor')
- grad_fc1_bias: float32 [2, 4096], P(None, 'tensor')
- grad_fc2_weight: float32 [2, 4096, 1024], P(None, 'tensor')
- grad_fc2_bias: float32 [2, 1024], replicated
- grad_scale_mlp: float32 [2, 1024], replicated
Inputs may be any that keep to these rules, and one draw needn't show every extreme that they name: `image_ids`: images are consecutive runs of tokens numbered in order; each image has at most 1370 tokens and one has exactly 1370.
All inputs are finite; a program needn't handle non-finite values.
Results may differ from a plain program's by a relative error of at most 0.02.
The roundings to bfloat16 on the way count: a program that leaves them out, or rounds other values in their place, can miss the bound.
Values may be sent and summed in bfloat16 or wider, within the bound.
A program may use at most 384 MiB of HBM per device.

v0:
```python
import jax
import jax.numpy as jnp
from jax import lax
from jax.sharding import PartitionSpec as P

HD = 64
LAYERS = 2
MAXLEN = 1370


eps = 1e-06
masked_score = -1e30
half_root = 0.7071067811865476
density_scale = 0.3989422804014327


def with_halo(array, sides, width):
    for axis, dim in sides:
        peers, length = (lax.axis_size(axis), array.shape[dim])
        up = [(i, (i + 1) % peers) for i in range(peers - 1)]
        down = [(j, i) for i, j in up]
        last = lax.slice_in_dim(array, length - width, length, axis=dim)
        leading = lax.slice_in_dim(array, 0, width, axis=dim)
        before = lax.ppermute(last, axis, up)
        after = lax.ppermute(leading, axis, down)
        array = jnp.concatenate([before, array, after], axis=dim)
    return array


def norm_forward(stream, gain_row, offset):
    centre = jnp.mean(stream, axis=-1, keepdims=True)
    centred = stream - centre
    spread = lax.rsqrt(jnp.mean(centred * centred, axis=-1, keepdims=True) + eps)
    normed = centred * spread
    return (normed * gain_row + offset, normed, spread)


def norm_backward(upstream, normed, spread, gain_row):
    scaled = upstream * gain_row
    centred_grad = (
        scaled
        - jnp.mean(scaled, axis=-1, keepdims=True)
        - normed * jnp.mean(scaled * normed, axis=-1, keepdims=True)
    )
    return (centred_grad * spread, jnp.sum(upstream * normed, axis=0), jnp.sum(upstream, axis=0))


def gelu_pair(before):
    cumulative = 0.5 * (1.0 + lax.erf(before * half_root))
    density = jnp.exp(-0.5 * before * before) * density_scale
    return (before * cumulative, cumulative + before * density)


def block_length():
    return 512


def key_reach(row_count, block_rows):
    margin = min((MAXLEN + 126) // 128 * 128, row_count)
    return (margin, block_rows + 2 * margin)


def branch_total(partial_value):
    return lax.psum(partial_value, "tensor")


def input_total(partial_value):
    return lax.psum(partial_value, "tensor")


def masked_scores(query_block, keys_near, id_block, near_ids, score_scale):
    scores = (
        jnp.einsum("qhd,khd->hqk", query_block, keys_near, preferred_element_type=jnp.float32)
        * score_scale
    )
    allowed = id_block[:, None] == near_ids[None, :]
    return jnp.where(allowed[None], scores, masked_score)


def attend_forward(queries, rim_pair, rim_ids, own_ids):
    row_count, head_count, head_width = queries.shape
    block_rows = block_length()
    block_count = row_count // block_rows
    margin, window = key_reach(row_count, block_rows)
    score_scale = head_width ** (-0.5)

    def one_block(packed):
        query_block, id_block, block_index = packed
        first_row = row_count - margin + block_index * block_rows
        near_pair = lax.dynamic_slice_in_dim(rim_pair, first_row, window, 0)
        near_ids = lax.dynamic_slice_in_dim(rim_ids, first_row, window, 0)
        keys_near = near_pair[:, 0].reshape(window, head_count, head_width)
        values_near = near_pair[:, 1].reshape(window, head_count, head_width)
        scores = masked_scores(query_block, keys_near, id_block, near_ids, score_scale)
        row_peak = jnp.max(scores, axis=-1, keepdims=True)
        weights = jnp.exp(scores - row_peak)
        row_total = jnp.sum(weights, axis=-1, keepdims=True)
        mixture = jnp.einsum(
            "hqk,khd->qhd",
            weights.astype(jnp.bfloat16),
            values_near,
            preferred_element_type=jnp.float32,
        )
        result = (mixture / jnp.transpose(row_total, (1, 0, 2))).astype(jnp.bfloat16)
        return (result, (row_peak + jnp.log(row_total))[..., 0])

    block_numbers = jnp.arange(block_count, dtype=jnp.int32)
    results, logsums = lax.map(
        one_block,
        (
            queries.reshape(block_count, block_rows, head_count, head_width),
            own_ids.reshape(block_count, block_rows),
            block_numbers,
        ),
    )
    return (results.reshape(row_count, head_count * head_width), logsums)


def attend_backward(queries, rim_pair, rim_ids, own_ids, attended, grad_heads, logsums):
    row_count, head_count, head_width = queries.shape
    block_rows = block_length()
    block_count = row_count // block_rows
    margin, window = key_reach(row_count, block_rows)
    score_scale = head_width ** (-0.5)

    def one_block(running, packed):
        query_block, id_block, out_block, grad_block, lse_block, block_index = packed
        first_row = row_count - margin + block_index * block_rows
        near_pair = lax.dynamic_slice_in_dim(rim_pair, first_row, window, 0)
        near_ids = lax.dynamic_slice_in_dim(rim_ids, first_row, window, 0)
        keys_near = near_pair[:, 0].reshape(window, head_count, head_width)
        values_near = near_pair[:, 1].reshape(window, head_count, head_width)
        scores = masked_scores(query_block, keys_near, id_block, near_ids, score_scale)
        probabilities = jnp.exp(scores - lse_block[..., None])
        row_delta = jnp.sum(grad_block.astype(jnp.float32) * out_block.astype(jnp.float32), axis=-1)
        grad_prob = jnp.einsum(
            "qhd,khd->hqk", grad_block, values_near, preferred_element_type=jnp.float32
        )
        grad_score = (probabilities * (grad_prob - jnp.transpose(row_delta)[..., None])).astype(
            jnp.bfloat16
        )
        grad_query = (
            jnp.einsum("hqk,khd->qhd", grad_score, keys_near, preferred_element_type=jnp.float32)
            * score_scale
        )
        key_part = (
            lax.dynamic_slice_in_dim(running[0], first_row, window, 0)
            + jnp.einsum(
                "hqk,qhd->khd", grad_score, query_block, preferred_element_type=jnp.float32
            )
            * score_scale
        )
        value_part = lax.dynamic_slice_in_dim(running[1], first_row, window, 0) + jnp.einsum(
            "hqk,qhd->khd",
            probabilities.astype(jnp.bfloat16),
            grad_block,
            preferred_element_type=jnp.float32,
        )
        grad_key = lax.dynamic_update_slice_in_dim(running[0], key_part, first_row, 0)
        grad_value = lax.dynamic_update_slice_in_dim(running[1], value_part, first_row, 0)
        return ((grad_key, grad_value), grad_query)

    shaped = (block_count, block_rows, head_count, head_width)
    zeros_wide = jnp.zeros((3 * row_count, head_count, head_width), jnp.float32)
    block_numbers = jnp.arange(block_count, dtype=jnp.int32)
    sums, grad_queries = lax.scan(
        one_block,
        (zeros_wide, zeros_wide),
        (
            queries.reshape(shaped),
            own_ids.reshape(block_count, block_rows),
            attended.reshape(shaped),
            grad_heads.reshape(shaped),
            logsums,
            block_numbers,
        ),
    )
    window_sums = jnp.stack([sums[0], sums[1]], axis=1).reshape(
        3 * row_count, 2, head_count * head_width
    )
    return (grad_queries.reshape(row_count, head_count * head_width), window_sums)


def body(
    tokens,
    image_ids,
    cotangent,
    ln1_gain,
    ln1_bias,
    qkv_weight,
    qv_bias,
    proj_weight,
    proj_bias,
    scale_attn,
    ln2_gain,
    ln2_bias,
    fc1_weight,
    fc1_bias,
    fc2_weight,
    fc2_bias,
    scale_mlp,
):
    row_count = tokens.shape[0]
    head_share = qkv_weight.shape[3]
    heads_here = head_share // HD
    own_ids = image_ids + 1
    rim_ids = with_halo(own_ids, (("dp", 0),), row_count)
    stream = tokens.astype(jnp.float32)
    records = []
    for level_index in range(LAYERS):
        normed1, hat1, spread1 = norm_forward(stream, ln1_gain[level_index], ln1_bias[level_index])
        first_in = normed1.astype(jnp.bfloat16)
        projected = jnp.einsum(
            "td,dck->tck", first_in, qkv_weight[level_index], preferred_element_type=jnp.float32
        )
        queries = (
            (projected[:, 0] + qv_bias[level_index, 0])
            .astype(jnp.bfloat16)
            .reshape(row_count, heads_here, HD)
        )
        key_value = jnp.stack(
            [projected[:, 1], projected[:, 2] + qv_bias[level_index, 1]], axis=1
        ).astype(jnp.bfloat16)
        rim_pair = with_halo(key_value, (("dp", 0),), row_count)
        attended, logsums = attend_forward(queries, rim_pair, rim_ids, own_ids)
        mixed1 = branch_total(
            jnp.dot(attended, proj_weight[level_index], preferred_element_type=jnp.float32)
        )
        middle = stream + scale_attn[level_index] * (mixed1 + proj_bias[level_index])
        normed2, hat2, spread2 = norm_forward(middle, ln2_gain[level_index], ln2_bias[level_index])
        second_in = normed2.astype(jnp.bfloat16)
        before = (
            jnp.dot(second_in, fc1_weight[level_index], preferred_element_type=jnp.float32)
            + fc1_bias[level_index]
        )
        activated, slopes = gelu_pair(before)
        activated = activated.astype(jnp.bfloat16)
        mixed2 = branch_total(
            jnp.dot(activated, fc2_weight[level_index], preferred_element_type=jnp.float32)
        )
        records.append(
            (
                hat1,
                spread1,
                first_in,
                queries,
                rim_pair,
                attended,
                logsums,
                mixed1,
                hat2,
                spread2,
                second_in,
                activated,
                slopes,
                mixed2,
            )
        )
        stream = middle + scale_mlp[level_index] * (mixed2 + fc2_bias[level_index])
    upstream = cotangent.astype(jnp.float32)
    gradients = [None] * LAYERS
    for level_index in reversed(range(LAYERS)):
        (
            hat1,
            spread1,
            first_in,
            queries,
            rim_pair,
            attended,
            logsums,
            mixed1,
            hat2,
            spread2,
            second_in,
            activated,
            slopes,
            mixed2,
        ) = records[level_index]
        grad_scale_mlp = jnp.sum(upstream * (mixed2 + fc2_bias[level_index]), axis=0)
        grad_fc2_bias = jnp.sum(upstream * scale_mlp[level_index], axis=0)
        grad_branch2 = (upstream * scale_mlp[level_index]).astype(jnp.bfloat16)
        grad_fc2 = jnp.einsum(
            "tf,td->fd", activated, grad_branch2, preferred_element_type=jnp.float32
        )
        grad_activated = jnp.einsum(
            "td,fd->tf", grad_branch2, fc2_weight[level_index], preferred_element_type=jnp.float32
        )
        grad_before = grad_activated * slopes
        grad_fc1_bias = jnp.sum(grad_before, axis=0)
        grad_before_narrow = grad_before.astype(jnp.bfloat16)
        grad_fc1 = jnp.einsum(
            "td,tf->df", second_in, grad_before_narrow, preferred_element_type=jnp.float32
        )
        grad_normed2 = input_total(
            jnp.einsum(
                "tf,df->td",
                grad_before_narrow,
                fc1_weight[level_index],
                preferred_element_type=jnp.float32,
            )
        )
        back2, grad_ln2_gain, grad_ln2_bias = norm_backward(
            grad_normed2, hat2, spread2, ln2_gain[level_index]
        )
        grad_middle = upstream + back2
        grad_scale_attn = jnp.sum(grad_middle * (mixed1 + proj_bias[level_index]), axis=0)
        grad_proj_bias = jnp.sum(grad_middle * scale_attn[level_index], axis=0)
        grad_branch1 = (grad_middle * scale_attn[level_index]).astype(jnp.bfloat16)
        grad_proj = jnp.einsum(
            "tk,td->kd", attended, grad_branch1, preferred_element_type=jnp.float32
        )
        grad_heads = jnp.einsum(
            "td,kd->tk", grad_branch1, proj_weight[level_index], preferred_element_type=jnp.float32
        ).astype(jnp.bfloat16)
        grad_query, window_sums = attend_backward(
            queries, rim_pair, rim_ids, own_ids, attended, grad_heads, logsums
        )
        outgoing = jnp.concatenate([window_sums[:row_count], window_sums[2 * row_count :]], axis=0)
        incoming = with_halo(outgoing, (("dp", 0),), row_count)
        grad_pair = (
            window_sums[row_count : 2 * row_count]
            + incoming[:row_count]
            + incoming[3 * row_count :]
        )
        grad_qv = jnp.stack([jnp.sum(grad_query, axis=0), jnp.sum(grad_pair[:, 1], axis=0)])
        grad_all = jnp.stack([grad_query, grad_pair[:, 0], grad_pair[:, 1]], axis=1).astype(
            jnp.bfloat16
        )
        grad_qkv = jnp.einsum("td,tck->dck", first_in, grad_all, preferred_element_type=jnp.float32)
        grad_normed1 = input_total(
            jnp.einsum(
                "tck,dck->td", grad_all, qkv_weight[level_index], preferred_element_type=jnp.float32
            )
        )
        back1, grad_ln1_gain, grad_ln1_bias = norm_backward(
            grad_normed1, hat1, spread1, ln1_gain[level_index]
        )
        upstream = grad_middle + back1
        layer_set = (
            grad_ln1_gain,
            grad_ln1_bias,
            grad_qkv,
            grad_qv,
            grad_proj,
            grad_proj_bias,
            grad_scale_attn,
            grad_ln2_gain,
            grad_ln2_bias,
            grad_fc1,
            grad_fc1_bias,
            grad_fc2,
            grad_fc2_bias,
            grad_scale_mlp,
        )
        gradients[level_index] = layer_set
    stacked = [
        jnp.stack([gradients[level_index][member] for level_index in range(LAYERS)])
        for member in range(14)
    ]
    stacked = lax.psum(
        (
            stacked[0],
            stacked[1],
            stacked[2],
            stacked[3],
            stacked[4],
            stacked[5],
            stacked[6],
            stacked[7],
            stacked[8],
            stacked[9],
            stacked[10],
            stacked[11],
            stacked[12],
            stacked[13],
        ),
        "dp",
    )
    return (
        stream,
        upstream,
        stacked[0],
        stacked[1],
        stacked[2],
        stacked[3],
        stacked[4],
        stacked[5],
        stacked[6],
        stacked[7],
        stacked[8],
        stacked[9],
        stacked[10],
        stacked[11],
        stacked[12],
        stacked[13],
    )


def solution(mesh):
    return jax.shard_map(
        body,
        mesh=mesh,
        in_specs=(
            P("dp", None),
            P("dp"),
            P("dp", None),
            P(),
            P(),
            P(None, None, None, "tensor"),
            P(None, None, "tensor"),
            P(None, "tensor", None),
            P(),
            P(),
            P(),
            P(),
            P(None, None, "tensor"),
            P(None, "tensor"),
            P(None, "tensor", None),
            P(),
            P(),
        ),
        out_specs=(
            P("dp", None),
            P("dp", None),
            P(),
            P(),
            P(None, None, None, "tensor"),
            P(None, None, "tensor"),
            P(None, "tensor", None),
            P(),
            P(),
            P(),
            P(),
            P(None, None, "tensor"),
            P(None, "tensor"),
            P(None, "tensor", None),
            P(),
            P(),
        ),
        check_vma=False,
    )
```

profile of v0, /device:TPU:17, one launch (start us, length us, event | category | flops | bytes accessed | tf_op | source)
XLA Modules:
  0.0 2724.1 jit_solution(8178501697057071110)
XLA Ops:
  58.3 130.9 %while.60 = (s32[]{:T(128)}, bf16[3,512,4,64]{1,3,2,0:T(8,128)(2,1)}, f32[3,4,512]{2,1,0:T(4,128)S(1)}, s32[3]{0:T(128)S(1)}, bf16[4608,2,256]{0,2,1:T(8,128)(2,...) while((s32[]{:T(128)}, ...), condition=%wide.region_5.6_spmd, body=%wide.region_2.5_spmd.sunk | while | flops 1821767680 | bytes 99465448 | solution.py:108
  62.8 12.8 fusion.309
  75.5 13.5 fusion.310
  89.1 12.7 fusion.311
  106.3 12.8 fusion.309
  119.1 13.5 fusion.310
  132.6 12.7 fusion.311
  149.8 12.8 fusion.309
  162.6 13.5 fusion.310
  176.1 12.7 fusion.311
  200.2 135.1 %all-reduce.13.cloned.1.call-done = f32[1536,1024]{1,0:T(8,128)} async-done(((f32[1536,1024]{1,0:T(8,128)}), f32[1536,1024]{1,0:T(8,128)}) %all-reduce.13.cloned.1.call-update) | async-done | bytes 6291472 | tf_op jit(solution)/shard_map/psum | solution.py:64
  358.9 136.7 %all-reduce.15.cloned.1.call-done = f32[1536,1024]{1,0:T(8,128)} async-done(((f32[1536,1024]{1,0:T(8,128)}), f32[1536,1024]{1,0:T(8,128)}) %all-reduce.15.cloned.1.call-update) | async-done | bytes 6291472 | tf_op jit(solution)/shard_map/psum | solution.py:64
  522.9 9.5 collective-permute-done.4
  548.2 130.7 %while.61 = (s32[]{:T(128)}, bf16[3,512,4,64]{1,3,2,0:T(8,128)(2,1)}, f32[3,4,512]{2,1,0:T(4,128)S(1)}, s32[3]{0:T(128)S(1)}, bf16[4608,2,256]{0,2,1:T(8,128)(2,...) while((s32[]{:T(128)}, ...), condition=%wide.region_15.16_spmd, body=%wide.region_12.15_spmd.sunk | while | flops 1821767680 | bytes 99465448 | solution.py:108
  552.7 12.8 fusion.315
  565.5 13.5 fusion.316
  579.0 12.7 fusion.317
  596.2 12.8 fusion.315
  609.0 13.5 fusion.316
  622.5 12.7 fusion.317
  639.7 12.8 fusion.315
  652.5 13.5 fusion.316
  666.0 12.7 fusion.317
  686.7 137.1 %all-reduce.17.cloned.1.call-done = f32[1536,1024]{1,0:T(8,128)} async-done(((f32[1536,1024]{1,0:T(8,128)}), f32[1536,1024]{1,0:T(8,128)}) %all-reduce.17.cloned.1.call-update) | async-done | bytes 6291472 | tf_op jit(solution)/shard_map/psum | solution.py:64
  854.7 138.6 %all-reduce.19.cloned.1.call-done = f32[1536,1024]{1,0:T(8,128)} async-done(((f32[1536,1024]{1,0:T(8,128)}), f32[1536,1024]{1,0:T(8,128)}) %all-reduce.19.cloned.1.call-update) | async-done | bytes 6291472 | tf_op jit(solution)/shard_map/psum | solution.py:68
  1019.0 208.5 %while.62 = (s32[]{:T(128)}, f32[4608,4,64]{0,2,1:T(8,128)}, f32[4608,4,64]{0,2,1:T(8,128)}, f32[3,512,4,64]{1,3,2,0:T(8,128)S(1)}, s32[3]{0:T(128)S(1)}, /*inde...) while((s32[]{:T(128)}, f32[4608,4,64]{0,2,1:T(8,128)}, ...), condition=%wide.region_25.26_spmd, body=%wide.region_23.25_spmd.sunk | while | flops 4435146752 | bytes 155547936 | solution.py:166
  1022.8 11.0 fusion.328
  1035.9 17.9 multiply_convert_fusion.15
  1053.8 9.1 fusion.332
  1062.9 10.0 fusion.330
  1072.9 15.6 fusion.331
  1092.1 11.0 fusion.328
  1105.2 17.9 multiply_convert_fusion.15
  1123.1 9.1 fusion.332
  1132.2 10.0 fusion.330
  1142.2 15.6 fusion.331
  1161.3 11.0 fusion.328
  1174.5 17.9 multiply_convert_fusion.15
  1192.4 9.1 fusion.332
  1201.5 10.1 fusion.330
  1211.6 15.5 fusion.331
  1258.9 17.3 collective-permute-done.6
  1293.9 137.1 %all-reduce.21.cloned.1.call-done = f32[1536,1024]{1,0:T(8,128)} async-done(((f32[1536,1024]{1,0:T(8,128)}), f32[1536,1024]{1,0:T(8,128)}) %all-reduce.21.cloned.1.call-update) | async-done | bytes 6291472 | tf_op jit(solution)/shard_map/psum | solution.py:68
  1437.9 10.0 multiply_reduce_fusion
  1460.2 138.6 %all-reduce.23.cloned.1.call-done = f32[1536,1024]{1,0:T(8,128)} async-done(((f32[1536,1024]{1,0:T(8,128)}), f32[1536,1024]{1,0:T(8,128)}) %all-reduce.23.cloned.1.call-update) | async-done | bytes 6291472 | tf_op jit(solution)/shard_map/psum | solution.py:68
  1625.9 210.2 %while.63 = (s32[]{:T(128)}, f32[4608,4,64]{0,2,1:T(8,128)}, f32[4608,4,64]{0,2,1:T(8,128)}, f32[3,512,4,64]{1,3,2,0:T(8,128)S(1)}, s32[3]{0:T(128)S(1)}, /*inde...) while((s32[]{:T(128)}, f32[4608,4,64]{0,2,1:T(8,128)}, ...), condition=%wide.region_34.35_spmd, body=%wide.region_32.34_spmd.sunk | while | flops 4435146752 | bytes 155547936 | solution.py:166
  1629.6 11.0 fusion.343
  1643.4 17.9 multiply_convert_fusion.16
  1661.3 9.1 fusion.347
  1670.4 10.0 fusion.345
  1680.4 15.6 fusion.346
  1699.5 11.0 fusion.343
  1713.3 17.9 multiply_convert_fusion.16
  1740.2 10.0 fusion.345
  1750.3 15.7 fusion.346
  1769.5 11.0 fusion.343
  1783.3 17.9 multiply_convert_fusion.16
  1810.3 10.0 fusion.345
  1820.3 15.6 fusion.346
  1875.6 9.2 collective-permute-done.8
  1965.8 175.6 %all-reduce.29.cloned.1.call-done = (f32[1536,1024]{1,0:T(8,128)}, f32[1536,1024]{1,0:T(8,128)}) async-done(((f32[1536,1024]{1,0:T(8,128)}, f32[1536,1024]{1,0:T(8,128)}), (f32[1536,1024]{1,0:T(8,128)}, f32[1536,1024]{1,0:T(8,128)})) %all-reduce.29.cloned.1.call-update) | async-done | bytes 12582928 | tf_op jit(solution)/shard_map/psum | solution.py:64
  2141.5 9.2 fusion.138
  2164.4 473.5 %all-reduce.27.cloned.1.call-done = (f32[2,1024,3,256]{3,1,2,0:T(8,128)}, f32[2,256,1024]{2,1,0:T(8,128)}, f32[2,1024,1024]{2,1,0:T(8,128)}, f32[2,1024,1024]{2,1,0:T(8,128)}) async-done(((f32[2,1024,3,256]{3,1,2,0:T(8,128)}, f32[2,256,1024]{2,1,0:T(8,128)}, f32[2,1024,1024]{2,1,0:T(8,128)}, f32[2,1024,1024]{2,1,0:T(8,128)}), (f32[2,1024,3,256]{3,1,2,0:T(8,128)}, f32[2,256,1024]{2,1,0:T(8,128)}, ...) | async-done | bytes 25165840 | tf_op jit(solution)/shard_map/psum | solution.py:360
  2638.0 56.0 %all-reduce.25.cloned.1.call-done = (f32[2,1024]{1,0:T(2,128)}, f32[2,1024]{1,0:T(2,128)}, f32[2,2,256]{2,1,0:T(2,128)}, f32[2,1024]{1,0:T(2,128)}, f32[2,1024]{...) async-done(((f32[2,1024]{1,0:T(2,128)}, f32[2,1024]{1,0:T(2,128)}, ...) | async-done | bytes 77840 | tf_op jit(solution)/shard_map/psum | solution.py:360
  (610 shorter events, 517.5 us)
Async XLA Ops:
  7.2 328.1 %all-reduce.13.cloned.1.call-start = ((), (), s32[]{:S(2)}) async-start(), calls=%async_computation | async-start | bytes 12582912 | tf_op jit(solution)/shard_map/psum | solution.py:64
  20.9 25.8 collective-permute-start
  24.7 22.1 collective-permute-start.1
  26.6 15.7 collective-permute-start.2
  30.3 16.5 collective-permute-start.3
  192.2 143.1 %copy-start.6 = (bf16[1536,1024]{1,0:T(8,128)(2,1)S(1)}, bf16[1536,1024]{1,0:T(8,128)(2,1)}, u32[]{:S(2)}) copy-start(bf16[1536,1024]{1,0:T(8,128)(2,1)} %param.25) | copy-start | bytes 9437188
  197.1 298.6 %all-reduce.15.cloned.1.call-start = ((), (), s32[]{:S(2)}) async-start(), calls=%async_computation.1 | async-start | bytes 12582912 | tf_op jit(solution)/shard_map/psum | solution.py:64
  197.8 141.4 %copy-start.50 = (f32[1,1024]{1,0:T(1,128)}, f32[1,1024]{1,0:T(1,128)S(1)}, u32[]{:S(2)}) copy-start(f32[1,1024]{1,0:T(1,128)S(1)} %get-tuple-element.785) | copy-start | bytes 12292
  198.4 140.8 %copy-start.75 = (f32[1,1024]{1,0:T(1,128)}, f32[1,1024]{1,0:T(1,128)S(1)}, u32[]{:S(2)}) copy-start(f32[1,1024]{1,0:T(1,128)S(1)} %get-tuple-element.787) | copy-start | bytes 12292
  199.0 141.1 %copy-start.70 = (f32[1,1024]{1,0:T(1,128)}, f32[1,1024]{1,0:T(1,128)S(1)}, u32[]{:S(2)}) copy-start(f32[1,1024]{1,0:T(1,128)S(1)} %get-tuple-element.781) | copy-start | bytes 12292
  199.6 140.5 %copy-start.123 = (f32[1,1024]{1,0:T(1,128)}, f32[1,1024]{1,0:T(1,128)S(1)}, u32[]{:S(2)}) copy-start(f32[1,1024]{1,0:T(1,128)S(1)} %get-tuple-element.783) | copy-start | bytes 12292
  200.2 139.9 %copy-start.128 = (f32[1,1024]{1,0:T(1,128)}, f32[1,1024]{1,0:T(1,128)S(1)}, u32[]{:S(2)}) copy-start(f32[1,1024]{1,0:T(1,128)S(1)} %get-tuple-element.779) | copy-start | bytes 12292
  339.2 10.8 copy-start
  339.2 10.7 copy-start.42
  357.1 466.8 %all-reduce.17.cloned.1.call-start = ((), (), s32[]{:S(2)}) async-start(), calls=%async_computation.2 | async-start | bytes 12582912 | tf_op jit(solution)/shard_map/psum | solution.py:64
  358.3 142.9 %copy-start.77 = (f32[1,1024]{1,0:T(1,128)}, f32[1,1024]{1,0:T(1,128)S(1)}, u32[]{:S(2)}) copy-start(f32[1,1024]{1,0:T(1,128)S(1)} %get-tuple-element.777) | copy-start | bytes 12292
  358.9 142.3 %copy-start.80 = (f32[1,1024]{1,0:T(1,128)}, f32[1,1024]{1,0:T(1,128)S(1)}, u32[]{:S(2)}) copy-start(f32[1,1024]{1,0:T(1,128)S(1)} %get-tuple-element.775) | copy-start | bytes 12292
  511.1 21.3 collective-permute-start.4
  514.7 22.1 collective-permute-start.5
  681.8 142.0 %copy-start.53 = (f32[1,1024]{1,0:T(1,128)S(1)}, f32[1,1024]{1,0:T(1,128)}, u32[]{:S(2)}) copy-start(f32[1,1024]{1,0:T(1,128)} %get-tuple-element.784) | copy-start | bytes 12292
  681.8 142.0 %copy-start.82 = (f32[1,1024]{1,0:T(1,128)S(1)}, f32[1,1024]{1,0:T(1,128)}, u32[]{:S(2)}) copy-start(f32[1,1024]{1,0:T(1,128)} %get-tuple-element.786) | copy-start | bytes 12292
  686.7 306.6 %all-reduce.19.cloned.1.call-start = ((), (), s32[]{:S(2)}) async-start(), calls=%async_computation.3 | async-start | bytes 12582912 | tf_op jit(solution)/shard_map/psum | solution.py:68
  829.4 10.7 copy-start.2
  829.5 170.6 %copy-start.48 = (f32[1536]{0:T(1024)}, f32[1536]{0:T(1024)S(1)}, u32[]{:S(2)}) copy-start(f32[1536]{0:T(1024)S(1)} %broadcast_multiply_fusion.8) | copy-start | bytes 18436
  830.3 169.8 %copy-start.63 = (f32[1536]{0:T(1024)}, f32[1536]{0:T(1024)S(1)}, u32[]{:S(2)}) copy-start(f32[1536]{0:T(1024)S(1)} %add_rsqrt_fusion) | copy-start | bytes 18436
  854.7 576.4 %all-reduce.21.cloned.1.call-start = ((), (), s32[]{:S(2)}) async-start(), calls=%async_computation.4 | async-start | bytes 12582912 | tf_op jit(solution)/shard_map/psum | solution.py:68
  1000.1 10.7 copy-start.26
  1238.0 38.2 %collective-permute-start.6 = (f32[1536,2,256]{2,0,1:T(8,128)}, f32[1536,2,256]{2,0,1:T(8,128)}, u32[]{:S(2)}, u32[]{:S(2)}) collective-permute-start(f32[1536,2,256]{2,0,1:T(8,128)} %copy.64), channel_id=1, source_target_pairs={{0,4},{4,8},{8,12},{12,16},{16,20},{20,24},{24,28},{1,5},{5,9},{9,... | collective-permute-start | bytes 9437192 | tf_op jit(solution)/shard_map/ppermute | solution.py:24
  1244.0 38.9 %collective-permute-start.7 = (f32[1536,2,256]{2,0,1:T(8,128)}, f32[1536,2,256]{2,0,1:T(8,128)}, u32[]{:S(2)}, u32[]{:S(2)}) collective-permute-start(f32[1536,2,256]{2,0,1:T(8,128)} %copy.66), channel_id=1, source_target_pairs={{4,0},{8,4},{12,8},{16,12},{20,16},{24,20},{28,24},{5,1},{9,5},{13... | collective-permute-start | bytes 9437192 | tf_op jit(solution)/shard_map/ppermute | solution.py:25
  1258.9 30.3 %copy-start.35 = (bf16[1536,1,256]{2,0,1:T(8,128)(2,1)S(1)}, bf16[1536,1,256]{2,0,1:T(8,128)(2,1)}, u32[]{:S(2)}) copy-start(bf16[1536,1,256]{2,0,1:T(8,128)(2,1)} %reshape.410) | copy-start | bytes 2359300
  1258.9 30.3 %copy-start.141 = (bf16[2,1024,3,256]{3,1,2,0:T(8,128)(2,1)S(1)}, bf16[2,1024,3,256]{3,1,2,0:T(8,128)(2,1)}, u32[]{:S(2)}) copy-start(bf16[2,1024,3,256]{3,1,2,0:T(8,128)(2,1)} %param.30) | copy-start | bytes 9437188
  1293.8 137.2 %copy-start.46 = (f32[1536]{0:T(1024)S(1)}, f32[1536]{0:T(1024)}, u32[]{:S(2)}) copy-start(f32[1536]{0:T(1024)} %copy-done.45) | copy-start | bytes 18436
  1293.8 137.2 %copy-start.61 = (f32[1536]{0:T(1024)S(1)}, f32[1536]{0:T(1024)}, u32[]{:S(2)}) copy-start(f32[1536]{0:T(1024)} %copy-done.60) | copy-start | bytes 18436
  1293.8 137.2 %copy-start.68 = (f32[1,1024]{1,0:T(1,128)S(1)}, f32[1,1024]{1,0:T(1,128)}, u32[]{:S(2)}) copy-start(f32[1,1024]{1,0:T(1,128)} %get-tuple-element.788) | copy-start | bytes 12292
  1293.8 144.0 %copy-start.78 = (f32[1,1024]{1,0:T(1,128)S(1)}, f32[1,1024]{1,0:T(1,128)}, u32[]{:S(2)}) copy-start(f32[1,1024]{1,0:T(1,128)} %copy-done.77) | copy-start | bytes 12292
  1293.9 144.0 %copy-start.81 = (f32[1,1024]{1,0:T(1,128)S(1)}, f32[1,1024]{1,0:T(1,128)}, u32[]{:S(2)}) copy-start(f32[1,1024]{1,0:T(1,128)} %copy-done.80) | copy-start | bytes 12292
  1293.9 304.9 %all-reduce.23.cloned.1.call-start = ((), (), s32[]{:S(2)}) async-start(), calls=%async_computation.5 | async-start | bytes 12582912 | tf_op jit(solution)/shard_map/psum | solution.py:68
  1431.0 16.8 slice-start.14
  1437.8 10.0 copy-start.129
  1437.9 10.0 copy-start.138
  1460.1 138.7 %copy-start.43 = (f32[1536]{0:T(1024)S(1)}, f32[1536]{0:T(1024)}, u32[]{:S(2)}) copy-start(f32[1536]{0:T(1024)} %copy-done.42) | copy-start | bytes 18436
  1460.1 138.7 %copy-start.58 = (f32[1536]{0:T(1024)S(1)}, f32[1536]{0:T(1024)}, u32[]{:S(2)}) copy-start(f32[1536]{0:T(1024)} %copy-done.57) | copy-start | bytes 18436
  1460.1 138.7 %copy-start.71 = (f32[1,1024]{1,0:T(1,128)S(1)}, f32[1,1024]{1,0:T(1,128)}, u32[]{:S(2)}) copy-start(f32[1,1024]{1,0:T(1,128)} %copy-done.70) | copy-start | bytes 12292
  1460.1 681.3 %all-reduce.29.cloned.1.call-start = ((), (), s32[]{:S(2)}) async-start(), calls=%async_computation.8 | async-start | bytes 25165824 | tf_op jit(solution)/shard_map/psum | solution.py:64
  1460.2 145.4 %copy-start.51 = (f32[1,1024]{1,0:T(1,128)S(1)}, f32[1,1024]{1,0:T(1,128)}, u32[]{:S(2)}) copy-start(f32[1,1024]{1,0:T(1,128)} %copy-done.50) | copy-start | bytes 12292
  1460.2 145.4 %copy-start.76 = (f32[1,1024]{1,0:T(1,128)S(1)}, f32[1,1024]{1,0:T(1,128)}, u32[]{:S(2)}) copy-start(f32[1,1024]{1,0:T(1,128)} %copy-done.75) | copy-start | bytes 12292
  1607.0 10.6 copy-start.27
  1846.6 38.2 %collective-permute-start.8 = (f32[1536,2,256]{2,0,1:T(8,128)}, f32[1536,2,256]{2,0,1:T(8,128)}, u32[]{:S(2)}, u32[]{:S(2)}) collective-permute-start(f32[1536,2,256]{2,0,1:T(8,128)} %copy.73), channel_id=1, source_target_pairs={{0,4},{4,8},{8,12},{12,16},{16,20},{20,24},{24,28},{1,5},{5,9},{9,... | collective-permute-start | bytes 9437192 | tf_op jit(solution)/shard_map/ppermute | solution.py:24
  1852.7 38.9 %collective-permute-start.9 = (f32[1536,2,256]{2,0,1:T(8,128)}, f32[1536,2,256]{2,0,1:T(8,128)}, u32[]{:S(2)}, u32[]{:S(2)}) collective-permute-start(f32[1536,2,256]{2,0,1:T(8,128)} %copy.75), channel_id=1, source_target_pairs={{4,0},{8,4},{12,8},{16,12},{20,16},{24,20},{28,24},{5,1},{9,5},{13... | collective-permute-start | bytes 9437192 | tf_op jit(solution)/shard_map/ppermute | solution.py:25
  1875.6 22.2 copy-start.37
  1875.6 22.2 copy-start.142
  1902.5 735.4 %all-reduce.27.cloned.1.call-start = ((), (), s32[]{:S(2)}) async-start(), calls=%async_computation.7 | async-start | bytes 50331648 | tf_op jit(solution)/shard_map/psum | solution.py:360
  1904.4 13.9 slice-start.4
  1904.4 14.9 slice-start.2
  1918.3 18.7 slice-start
  1919.4 17.6 slice-start.1
  1929.7 17.8 slice-start.6
  1937.1 10.4 slice-start.7
  1958.1 183.3 %copy-start.91 = (f32[1,1024]{1,0:T(1,128)S(1)}, f32[1,1024]{1,0:T(1,128)}, u32[]{:S(2)}) copy-start(f32[1,1024]{1,0:T(1,128)} %get-tuple-element.774) | copy-start | bytes 12292
  1958.2 735.8 %all-reduce.25.cloned.1.call-start = ((), (), s32[]{:S(2)}) async-start(), calls=%async_computation.6 | async-start | bytes 155648 | tf_op jit(solution)/shard_map/psum | solution.py:360
  2141.5 10.4 copy-start.8
  2695.3 12.2 slice-start.12
  2696.8 10.2 copy-start.111
  2696.8 10.8 slice-start.13
  (119 other events, 626.1 us)
Sparse Core Ops, SparseCore 0:
  197.3 137.9 all-reduce.12
  357.2 138.4 all-reduce.14
  686.8 137.0 all-reduce.16
  854.8 138.4 all-reduce.18
  1294.0 137.0 all-reduce.20
  1460.3 138.4 all-reduce.22
  1902.6 238.8 all-reduce.28
  2145.5 492.4 all-reduce.26
  2642.3 51.6 all-reduce.24
where the time goes:
time: 2730 us; the launch traced here: 2720 us
  waiting for transfers between devices  1590 us (58%)
  matrix products  649 us (24%)
  other arithmetic  256 us (9%)
  local copies, waits for them, and re-layouts  177 us (6%)
  starting transfers between devices  28.7 us (1%)
    psum x4, waiting for transfers between devices, branch_total(): return lax.psum(partial_value, 'tensor')  585 us
    psum x2, waiting for transfers between devices, body(): lax.psum((stacked[0], stacked[1], stacked[2], stacked[3], stacked[4], sta...  530 us
    psum x3, waiting for transfers between devices, input_total(): return lax.psum(partial_value, 'tensor')  414 us
    dot_general x12, matrix products, masked_scores(): jnp.einsum('qhd,khd->hqk', query_block, keys_near, preferred_element_type...  142 us
    dot_general x6, matrix products, one_block(): jnp.einsum('qhd,khd->hqk', grad_block, values_near, preferred_element_typ...  108 us
    dot_general x6, matrix products, one_block(): jnp.einsum('hqk,qhd->khd', probabilities.astype(jnp.bfloat16), grad_block...  93.6 us
    reduce_sum x6, other arithmetic, one_block(): row_total = jnp.sum(weights, axis=-1, keepdims=True)  81.1 us
    dot_general x6, matrix products, one_block(): jnp.einsum('hqk,khd->qhd', weights.astype(jnp.bfloat16), values_near, pre...  76.2 us
  transfers between devices with their start and end apart: 19, of which 17 were waited for; matrix products, arithmetic and copies ran while one was open for 5% of the time, Pallas kernels for 0%

commit v1 on v0

v1 whole, which is shorter than its diff:
```python
import functools
import jax
import jax.numpy as jnp
from jax import lax
from jax.experimental import pallas as pl
from jax.experimental.pallas import tpu as pltpu
from jax.sharding import PartitionSpec as P

HD = 64
LAYERS = 2
D = 1024
MESH = pl.DeviceIdType.MESH
F32 = jnp.float32
BF16 = jnp.bfloat16
eps = 1e-06
half_root = 0.7071067811865476
density_scale = 0.3989422804014327
BIG = 1e30
Q_BLOCK = 512
K_BLOCK = 512
VMEM_LIMIT = 60 * 2**20


def bit_of(index, k):
    return (index // (1 << k)) % 2


def order_bits(nbits, half):
    return tuple(range(nbits)) if half == 0 else tuple(reversed(range(nbits)))


def compose(free_bits, free_value, fixed):
    index = sum(value * (1 << k) for k, value in fixed.items())
    for place, k in enumerate(free_bits):
        index = index + ((free_value >> place) & 1) * (1 << k)
    return index


class Exchange:
    def __init__(self, n, chunks, sub):
        self.n, self.chunks, self.sub = n, chunks, sub
        self.nbits = n.bit_length() - 1
        self.half = sub // 2
        self.me = lax.axis_index("tensor")
        self.bits = [bit_of(self.me, k) for k in range(self.nbits)]
        self.pending = []

    def partner(self, k):
        return self.me + (1 - 2 * self.bits[k]) * (1 << k)

    def barrier(self):
        sem = pltpu.get_barrier_semaphore()
        for k in range(self.nbits):
            pl.semaphore_signal(
                sem, inc=1, device_id={"tensor": self.partner(k)}, device_id_type=MESH
            )
        pl.semaphore_wait(sem, self.nbits)

    def rows(self, h):
        return pl.ds(h * self.half, self.half)

    def copy(self, src, dst, sems, c, h, message, k):
        return pltpu.make_async_remote_copy(
            src_ref=src,
            dst_ref=dst,
            send_sem=sems.at[0, c, h, message],
            recv_sem=sems.at[1, c, h, message],
            device_id={"tensor": self.partner(k)},
            device_id_type=MESH,
        )

    def rs_base(self, p):
        return sum(self.n >> (q + 1) for q in range(p))

    def rs_fixed(self, order, p, flip):
        fixed = {k: self.bits[k] for k in order[:p]}
        fixed[order[p]] = 1 - self.bits[order[p]] if flip else self.bits[order[p]]
        return fixed

    def rs_places(self, order, p, f):
        places = []
        for q in range(p):
            free = order[q + 1 :]
            index = 0
            for place, k in enumerate(free):
                at = order.index(k)
                if at < p:
                    value = self.bits[k]
                elif at == p:
                    value = 1 - self.bits[k]
                else:
                    value = (f >> (at - p - 1)) & 1
                index = index + value * (1 << place)
            places.append(self.rs_base(q) + index)
        return places

    def rs_send(self, part, recv, sems, c, p):
        for h in range(2):
            order = order_bits(self.nbits, h)
            free = order[p + 1 :]
            for f in range(1 << len(free)):
                b = compose(free, f, self.rs_fixed(order, p, True))
                message = self.rs_base(p) + f
                if p > 0:
                    total = part[b, c, self.rows(h), :].astype(F32)
                    for place in self.rs_places(order, p, f):
                        total = total + recv[c, place, self.rows(h), :].astype(F32)
                    part[b, c, self.rows(h), :] = total.astype(BF16)
                cp = self.copy(
                    part.at[b, c, self.rows(h), :],
                    recv.at[c, message, self.rows(h), :],
                    sems,
                    c,
                    h,
                    message,
                    order[p],
                )
                cp.start()
                self.pending.append(cp)

    def rs_wait(self, part, recv, sems, c, p):
        for h in range(2):
            order = order_bits(self.nbits, h)
            for f in range(self.n >> (p + 1)):
                message = self.rs_base(p) + f
                self.copy(
                    part.at[0, c, self.rows(h), :],
                    recv.at[c, message, self.rows(h), :],
                    sems,
                    c,
                    h,
                    message,
                    order[p],
                ).wait_recv()

    def rs_total(self, part, recv, c):
        halves = []
        for h in range(2):
            order = order_bits(self.nbits, h)
            total = part[self.me, c, self.rows(h), :].astype(F32)
            for p in range(self.nbits):
                free = order[p + 1 :]
                place = self.rs_base(p) + sum(
                    self.bits[k] * (1 << at) for at, k in enumerate(free)
                )
                total = total + recv[c, place, self.rows(h), :].astype(F32)
            halves.append(total)
        return jnp.concatenate(halves, axis=0)

    def ag_send(self, full, sems, c, p):
        for h in range(2):
            order = order_bits(self.nbits, h)
            fixed = {k: self.bits[k] for k in order[p:]}
            for f in range(1 << p):
                b = compose(order[:p], f, fixed)
                message = (1 << p) - 1 + f
                ref = full.at[b, c, self.rows(h), :]
                cp = self.copy(ref, ref, sems, c, h, message, order[p])
                cp.start()
                self.pending.append(cp)

    def ag_wait(self, full, sems, c, p):
        for h in range(2):
            order = order_bits(self.nbits, h)
            fixed = {k: self.bits[k] for k in order[p + 1 :]}
            fixed[order[p]] = 1 - self.bits[order[p]]
            for f in range(1 << p):
                b = compose(order[:p], f, fixed)
                message = (1 << p) - 1 + f
                ref = full.at[b, c, self.rows(h), :]
                self.copy(ref, ref, sems, c, h, message, order[p]).wait_recv()

    def drain(self):
        for cp in self.pending:
            cp.wait_send()
        self.pending = []


def erf(x):
    c = jnp.clip(x, -3.832506856900711, 3.832506856900711)
    s = c * c
    top = jnp.full_like(s, 0.00022905065861350646)
    for k in (0.0034082910107109506, 0.050955695062380861, 0.18520832239976145, 1.128379143519084):
        top = top * s + k
    low = jnp.full_like(s, -1.1791602954361697e-7)
    for k in (
        0.000023547966471313185,
        0.0010179625278914885,
        0.014070470171167667,
        0.11098505178285362,
        0.49746925110067538,
        1.0,
    ):
        low = low * s + k
    return c * top / low


def gelu_pair(before):
    cumulative = 0.5 * (1.0 + erf(before * half_root))
    density = jnp.exp(-0.5 * before * before) * density_scale
    return before * cumulative, cumulative + before * density


def normalised(stream):
    centre = jnp.mean(stream, axis=-1, keepdims=True)
    centred = stream - centre
    spread = lax.rsqrt(jnp.mean(centred * centred, axis=-1, keepdims=True) + eps)
    return centred * spread, spread


def norm_back(upstream, normed, spread, gain_row):
    scaled = upstream * gain_row
    return spread * (
        scaled
        - jnp.mean(scaled, axis=-1, keepdims=True)
        - normed * jnp.mean(scaled * normed, axis=-1, keepdims=True)
    )


def chunk_of(ref, c):
    x = ref[:, c]
    return x.reshape(x.shape[0] * x.shape[1], x.shape[2])


def column_loop(width, step, fn):
    if width <= step:
        fn(pl.ds(0, width))
    else:

        def one(j, carry):
            fn(pl.ds(pl.multiple_of(j * step, step), step))
            return carry

        lax.fori_loop(0, width // step, one, 0)


def matmul_nn(x, w_ref, cols):
    return jnp.dot(x, w_ref[:, cols], preferred_element_type=F32)


def matmul_nt(x, w_ref, cols):
    return lax.dot_general(
        x, w_ref[cols, :], (((1,), (1,)), ((), ())), preferred_element_type=F32
    )


def run_stages(ex, stages):
    for stage in stages:
        for c in range(ex.chunks):
            stage(c)


def rs_stages(ex, part, recv, sems):
    stages = []
    for p in range(1, ex.nbits):

        def stage(c, p=p):
            ex.rs_wait(part, recv, sems, c, p - 1)
            ex.rs_send(part, recv, sems, c, p)

        stages.append(stage)
    return stages


def ag_stages(ex, full, sems):
    stages = []
    for p in range(1, ex.nbits):

        def stage(c, p=p):
            ex.ag_wait(full, sems, c, p - 1)
            ex.ag_send(full, sems, c, p)

        stages.append(stage)
    return stages


def own_rows(ref, c):
    return ref[c]


def forward_kernel(
    n, chunks, sub, last,
    attended, proj, fc1, fc2, fc1_bias, vec, stream, *rest,
):
    if last:
        (u1_o, hat2_o, sp2_o, u2_o, a2_o, act_o, slope_o, out_o,
         part1, recv1, part2, recv2, full2, sems) = rest
    else:
        (qkv, qv_bias, u1_o, hat2_o, sp2_o, u2_o, a2_o, act_o, slope_o, stream_o, hat1_o, sp1_o, a1_o, q_o, k_o, v_o,
         part1, recv1, part2, recv2, sems) = rest
        full2 = a1_o
    ex = Exchange(n, chunks, sub)
    ex.barrier()
    row = lambda i: vec[i : i + 1, :]

    def pre(c):
        def cols(j):
            y = matmul_nn(chunk_of(attended, c), proj, j)
            part1[:, c, :, j] = y.astype(BF16).reshape(n, sub, -1)

        column_loop(D, 256, cols)
        ex.rs_send(part1, recv1, sems.at[0], c, 0)

    def own1(c):
        ex.rs_wait(part1, recv1, sems.at[0], c, ex.nbits - 1)
        u1 = ex.rs_total(part1, recv1, c) + row(0)
        u1_o[c] = u1
        middle = stream[c] + row(1) * u1
        hat, spread = normalised(middle)
        hat2_o[c] = hat
        sp2_o[c] = spread
        a2_o[ex.me, c] = (hat * row(2) + row(3)).astype(BF16)
        ex.ag_send(a2_o, sems.at[1], c, 0)

    def mid(c):
        ex.ag_wait(a2_o, sems.at[1], c, ex.nbits - 1)

        def hidden(j):
            before = matmul_nn(chunk_of(a2_o, c), fc1, j) + fc1_bias[:, j]
            a, s = gelu_pair(before)
            act_o[:, c, :, j] = a.astype(BF16).reshape(n, sub, -1)
            slope_o[:, c, :, j] = s.astype(BF16).reshape(n, sub, -1)

        column_loop(fc1.shape[1], 256, hidden)

        def cols(j):
            y = matmul_nn(chunk_of(act_o, c), fc2, j)
            part2[:, c, :, j] = y.astype(BF16).reshape(n, sub, -1)

        column_loop(D, 256, cols)
        ex.rs_send(part2, recv2, sems.at[2], c, 0)

    def own2(c):
        ex.rs_wait(part2, recv2, sems.at[2], c, ex.nbits - 1)
        u2 = ex.rs_total(part2, recv2, c) + row(4)
        u2_o[c] = u2
        middle = stream[c] + row(1) * u1_o[c]
        after = middle + row(5) * u2
        if last:
            full2[ex.me, c] = after.astype(BF16)
        else:
            stream_o[c] = after
            hat, spread = normalised(after)
            hat1_o[c] = hat
            sp1_o[c] = spread
            full2[ex.me, c] = (hat * row(6) + row(7)).astype(BF16)
        ex.ag_send(full2, sems.at[3], c, 0)

    def post(c):
        ex.ag_wait(full2, sems.at[3], c, ex.nbits - 1)
        if last:
            for b in range(n):
                out_o[b, c] = full2[b, c].astype(F32)
            return
        x = chunk_of(full2, c)
        width = q_o.shape[3]
        for i, ref in enumerate((q_o, k_o, v_o)):
            y = matmul_nn(x, qkv, slice(i * width, (i + 1) * width))
            if i != 1:
                y = y + qv_bias[i // 2 : i // 2 + 1, :]
            ref[:, c] = y.astype(BF16).reshape(n, sub, width)

    run_stages(
        ex,
        [pre]
        + rs_stages(ex, part1, recv1, sems.at[0])
        + [own1]
        + ag_stages(ex, a2_o, sems.at[1])
        + [mid]
        + rs_stages(ex, part2, recv2, sems.at[2])
        + [own2]
        + ag_stages(ex, full2, sems.at[3])
        + [post],
    )
    ex.drain()


def sizes(rows, n):
    block = rows // n
    chunks = 3 if block % 96 == 0 else (2 if block % 64 == 0 else 1)
    return block, chunks, block // chunks


def vmem():
    return pl.BlockSpec(memory_space=pltpu.VMEM)


def call(kernel, name, collective_id, outs, scratch, args, flops):
    return pl.pallas_call(
        kernel,
        out_shape=[jax.ShapeDtypeStruct(s, d) for s, d in outs],
        in_specs=[vmem()] * len(args),
        out_specs=[vmem()] * len(outs),
        scratch_shapes=scratch,
        compiler_params=pltpu.CompilerParams(
            collective_id=collective_id, has_side_effects=True, vmem_limit_bytes=VMEM_LIMIT
        ),
        cost_estimate=pl.CostEstimate(flops=flops, bytes_accessed=10**8, transcendentals=0),
        name=name,
    )(*args)


def comm_scratch(n, chunks, sub):
    return [
        pltpu.VMEM((n, chunks, sub, D), BF16),
        pltpu.VMEM((chunks, n - 1, sub, D), BF16),
    ]


def sem_scratch(stages, n, chunks):
    return [pltpu.SemaphoreType.DMA((stages, 2, chunks, 2, n - 1))]


def forward_block(n, last, collective_id, attended, proj, fc1, fc2, fc1_bias, vec, stream, qkv=None, qv_bias=None):
    rows, width = attended.shape
    block, chunks, sub = sizes(rows, n)
    hidden = fc1.shape[1]
    split = lambda cols: (n, chunks, sub, cols)
    mine = (chunks, sub, D)
    args = [attended.reshape(split(width)), proj, fc1, fc2, fc1_bias, vec, stream.reshape(mine)]
    outs = [
        (mine, F32), (mine, F32), ((chunks, sub, 1), F32), (mine, F32),
        (split(D), BF16), (split(hidden), BF16), (split(hidden), BF16),
    ]
    scratch = comm_scratch(n, chunks, sub) + comm_scratch(n, chunks, sub)
    if last:
        outs += [(split(D), F32)]
        scratch += [pltpu.VMEM(split(D), BF16)]
    else:
        args += [qkv, qv_bias]
        outs += [(mine, F32), (mine, F32), ((chunks, sub, 1), F32), (split(D), BF16)] + [(split(width), BF16)] * 3
    return call(
        functools.partial(forward_kernel, n, chunks, sub, last),
        "forward_last" if last else "forward_block",
        collective_id,
        outs,
        scratch + sem_scratch(4, n, chunks),
        args,
        2 * rows * D * (2 * hidden + 4 * width),
    )


def add_rows(ref, i, value):
    ref[i : i + 1, :] += jnp.sum(value, axis=0, keepdims=True)


def input_norm_own(ex, part, recv, sems, c, hat, spread, gain, gm, sums, at):
    ex.rs_wait(part, recv, sems, c, ex.nbits - 1)
    da1 = ex.rs_total(part, recv, c)
    add_rows(sums, at, da1 * hat[c])
    add_rows(sums, at + 1, da1)
    return gm[c] + norm_back(da1, hat[c], spread[c], gain)


def input_grad_chunk(ex, dqkv, qkv, part, c):
    def cols(j):
        y = matmul_nt(chunk_of(dqkv, c), qkv, j)
        part[:, c, :, j] = y.astype(BF16).reshape(ex.n, ex.sub, -1)

    column_loop(D, 256, cols)


def backward_kernel(n, chunks, sub, first, *refs):
    if first:
        (cot, e2_in, fc1, fc2, proj, vec, slope, u1, hat2, sp2, u2,
         dbn_o, e1_o, datt_o, gm_o, sums_o, fc1b_o, part2, recv2, sems) = refs
        full = e2_in
    else:
        (dqkv, qkv, hat1, sp1, gm_in, fc1, fc2, proj, vec, slope, u1, hat2, sp2, u2,
         e2_o, dbn_o, e1_o, datt_o, gm_o, sums_o, fc1b_o, part1, recv1, part2, recv2, sems) = refs
        full = e2_o
    ex = Exchange(n, chunks, sub)
    ex.barrier()
    row = lambda i: vec[i : i + 1, :]
    sums_o[...] = jnp.zeros_like(sums_o)
    fc1b_o[...] = jnp.zeros_like(fc1b_o)

    def pre(c):
        input_grad_chunk(ex, dqkv, qkv, part1, c)
        ex.rs_send(part1, recv1, sems.at[0], c, 0)

    def own0(c):
        g = input_norm_own(ex, part1, recv1, sems.at[0], c, hat1, sp1, row(3), gm_in, sums_o, 6)
        add_rows(sums_o, 0, g * u2[c])
        add_rows(sums_o, 1, g * row(0))
        gm_o[c] = g
        full[ex.me, c] = (g * row(0)).astype(BF16)
        ex.ag_send(full, sems.at[1], c, 0)

    def mid(c):
        if first:
            g = cot[c].astype(F32)
            add_rows(sums_o, 0, g * u2[c])
            add_rows(sums_o, 1, g * row(0))
            gm_o[c] = g
        else:
            ex.ag_wait(full, sems.at[1], c, ex.nbits - 1)

        def hidden(j):
            y = matmul_nt(chunk_of(full, c), fc2, j)
            w = y.shape[1]
            db = y * slope[:, c, :, j].astype(F32).reshape(n * sub, w)
            fc1b_o[:, j] += jnp.sum(db, axis=0, keepdims=True)
            dbn_o[:, c, :, j] = db.astype(BF16).reshape(n, sub, w)

        column_loop(fc1.shape[1], 256, hidden)

        def cols(j):
            y = matmul_nt(chunk_of(dbn_o, c), fc1, j)
            part2[:, c, :, j] = y.astype(BF16).reshape(n, sub, -1)

        column_loop(D, 256, cols)
        ex.rs_send(part2, recv2, sems.at[2], c, 0)

    def own1(c):
        ex.rs_wait(part2, recv2, sems.at[2], c, ex.nbits - 1)
        da2 = ex.rs_total(part2, recv2, c)
        hat = hat2[c]
        add_rows(sums_o, 2, da2 * hat)
        add_rows(sums_o, 3, da2)
        gm = gm_o[c] + norm_back(da2, hat, sp2[c], row(1))
        gm_o[c] = gm
        add_rows(sums_o, 4, gm * u1[c])
        add_rows(sums_o, 5, gm * row(2))
        e1_o[ex.me, c] = (gm * row(2)).astype(BF16)
        ex.ag_send(e1_o, sems.at[3], c, 0)

    def post(c):
        ex.ag_wait(e1_o, sems.at[3], c, ex.nbits - 1)
        y = matmul_nt(chunk_of(e1_o, c), proj, slice(None))
        datt_o[:, c] = y.astype(BF16).reshape(n, sub, -1)

    head = [] if first else (
        [pre] + rs_stages(ex, part1, recv1, sems.at[0]) + [own0] + ag_stages(ex, full, sems.at[1])
    )
    run_stages(
        ex,
        head
        + [mid]
        + rs_stages(ex, part2, recv2, sems.at[2])
        + [own1]
        + ag_stages(ex, e1_o, sems.at[3])
        + [post],
    )
    ex.drain()


def backward_block(n, collective_id, source, fc1, fc2, proj, vec, slope, u1, hat2, sp2, u2):
    first = len(source) == 2
    _, chunks, sub, hidden = slope.shape
    width = proj.shape[0]
    split = lambda cols: (n, chunks, sub, cols)
    mine = (chunks, sub, D)
    outs = [] if first else [(split(D), BF16)]
    outs += [
        (split(hidden), BF16), (split(D), BF16), (split(width), BF16), (mine, F32),
        ((8, D), F32), ((1, hidden), F32),
    ]
    scratch = [] if first else comm_scratch(n, chunks, sub)
    scratch += comm_scratch(n, chunks, sub) + sem_scratch(4, n, chunks)
    return call(
        functools.partial(backward_kernel, n, chunks, sub, first),
        "backward_first" if first else "backward_block",
        collective_id,
        outs,
        scratch,
        list(source) + [fc1, fc2, proj, vec, slope, u1, hat2, sp2, u2],
        2 * n * chunks * sub * D * (2 * hidden + 4 * width),
    )


def tail_kernel(n, chunks, sub, dqkv, qkv, hat1, sp1, gm_in, vec, out_o, sums_o, part1, recv1, full, sems):
    ex = Exchange(n, chunks, sub)
    ex.barrier()
    sums_o[...] = jnp.zeros_like(sums_o)

    def pre(c):
        input_grad_chunk(ex, dqkv, qkv, part1, c)
        ex.rs_send(part1, recv1, sems.at[0], c, 0)

    def own(c):
        g = input_norm_own(ex, part1, recv1, sems.at[0], c, hat1, sp1, vec[3:4, :], gm_in, sums_o, 6)
        full[ex.me, c] = g.astype(BF16)
        ex.ag_send(full, sems.at[1], c, 0)

    def post(c):
        ex.ag_wait(full, sems.at[1], c, ex.nbits - 1)
        for b in range(n):
            out_o[b, c] = full[b, c].astype(F32)

    run_stages(
        ex,
        [pre]
        + rs_stages(ex, part1, recv1, sems.at[0])
        + [own]
        + ag_stages(ex, full, sems.at[1])
        + [post],
    )
    ex.drain()


def backward_tail(n, collective_id, dqkv, qkv, hat1, sp1, gm, vec):
    _, chunks, sub, width = dqkv.shape
    split = lambda cols: (n, chunks, sub, cols)
    return call(
        functools.partial(tail_kernel, n, chunks, sub),
        "backward_tail",
        collective_id,
        [(split(D), F32), ((8, D), F32)],
        comm_scratch(n, chunks, sub) + [pltpu.VMEM(split(D), BF16)] + sem_scratch(2, n, chunks),
        [dqkv, qkv, hat1, sp1, gm, vec],
        2 * n * chunks * sub * D * width,
    )


def id_features(ids_col, query_side):
    lane = lax.broadcasted_iota(jnp.int32, (ids_col.shape[0], HD), 1)
    bit = (ids_col >> (lane & 15)) & 1
    first = lane < 16
    second = (lane >= 16) & (lane < 32)
    inv = 1 - bit
    if query_side:
        v = jnp.where(first, bit, jnp.where(second, inv, 0)).astype(F32) * (-BIG)
    else:
        v = jnp.where(first, inv, jnp.where(second, bit, 0)).astype(F32)
    return v

def fwd_kernel(QB, KB, nq, lo_ref, hi_ref, q_ref, k_ref, v_ref, idq_ref, idk_ref, o_ref, lse_ref, kaug, vt, qaug):
    nk = k_ref.shape[0] // KB
    t_lo = lo_ref[0]
    t_hi = hi_ref[nq - 1]
    def prep(t, _):
        r = pl.ds(pl.multiple_of(t * KB, KB), KB)
        feat = id_features(idk_ref[r, :], False).astype(BF16)
        kk = k_ref[r, :]
        kaug[0, r, :] = jnp.concatenate([kk[:, :HD], feat], axis=1)
        kaug[1, r, :] = jnp.concatenate([kk[:, HD:], feat], axis=1)
        vt[:, r] = v_ref[r, :].T
        return 0
    lax.fori_loop(t_lo, t_hi, prep, 0)
    def qprep(t, _):
        r = pl.ds(pl.multiple_of(t * QB, QB), QB)
        feat = id_features(idq_ref[r, :], True).astype(BF16)
        qq = (q_ref[r, :] * BF16(0.125))
        qaug[0, :, r] = jnp.concatenate([qq[:, :HD], feat], axis=1).T
        qaug[1, :, r] = jnp.concatenate([qq[:, HD:], feat], axis=1).T
        return 0
    lax.fori_loop(0, nq, qprep, 0)
    def qloop(qb, _):
        rq = pl.ds(pl.multiple_of(qb * QB, QB), QB)
        outs = []
        qts = [qaug[h, :, rq] for h in range(2)]
        def kloop(t, c):
            r = pl.ds(pl.multiple_of(t * KB, KB), KB)
            new = []
            for h in range(2):
                m, l, acc = c[h]
                s = jnp.dot(kaug[h, r, :], qts[h], preferred_element_type=F32)
                mn = jnp.maximum(m, jnp.max(s, axis=0, keepdims=True))
                p = jnp.exp(s - mn)
                al = jnp.exp(m - mn)
                l = l * al + jnp.sum(p, axis=0, keepdims=True)
                acc = acc * al + jnp.dot(vt[h * HD:(h + 1) * HD, r], p.astype(BF16), preferred_element_type=F32)
                new.append((mn, l, acc))
            return tuple(new)
        z = (jnp.full((1, QB), -3e38, F32), jnp.zeros((1, QB), F32), jnp.zeros((HD, QB), F32))
        c = lax.fori_loop(lo_ref[qb], hi_ref[qb], kloop, (z, z))
        both = jnp.concatenate([c[h][2] / c[h][1] for h in range(2)], axis=0)
        o_ref[rq, :] = both.T.astype(BF16)
        for h in range(2):
            lse_ref[0, h:h + 1, rq] = c[h][0] + jnp.log(c[h][1])
        return 0
    lax.fori_loop(0, nq, qloop, 0)

def attend_fwd(q, kwin, vwin, idq, idk, lo, hi, QB, KB):
    n, cols = q.shape
    w = kwin.shape[0]
    pairs = cols // 128
    nq = n // QB
    return pl.pallas_call(
        functools.partial(fwd_kernel, QB, KB, nq),
        grid_spec=pltpu.PrefetchScalarGridSpec(
            num_scalar_prefetch=2, grid=(pairs,),
            in_specs=[pl.BlockSpec((n, 128), lambda g, *_: (0, g)), pl.BlockSpec((w, 128), lambda g, *_: (0, g)), pl.BlockSpec((w, 128), lambda g, *_: (0, g)),
                      pl.BlockSpec((n, 1), lambda g, *_: (0, 0)), pl.BlockSpec((w, 1), lambda g, *_: (0, 0))],
            out_specs=[pl.BlockSpec((n, 128), lambda g, *_: (0, g)), pl.BlockSpec((1, 2, n), lambda g, *_: (g, 0, 0))],
            scratch_shapes=[pltpu.VMEM((2, w, 128), BF16), pltpu.VMEM((128, w), BF16), pltpu.VMEM((2, 128, n), BF16)]),
        out_shape=[jax.ShapeDtypeStruct((n, cols), BF16), jax.ShapeDtypeStruct((pairs, 2, n), F32)],
        compiler_params=pltpu.CompilerParams(vmem_limit_bytes=VMEM_LIMIT),
        name="attend_fwd",
    )(lo, hi, q, kwin, vwin, idq, idk)

def bwd_kernel(QB, KB, nq, lo_ref, hi_ref, q_ref, k_ref, v_ref, idq_ref, idk_ref, o_ref, g_ref, lse_ref, dq_ref, dk_ref, dv_ref, kaug, vaug, kt, qaug, gaug, acc):
    w = k_ref.shape[0]
    t_lo = lo_ref[0]
    t_hi = hi_ref[nq - 1]
    lane = lax.broadcasted_iota(jnp.int32, (KB, HD), 1)
    three = ((lane >= 32) & (lane < 35))
    def zero(t, _):
        r = pl.ds(pl.multiple_of(t * KB, KB), KB)
        dk_ref[r, :] = jnp.zeros((KB, 128), BF16)
        dv_ref[r, :] = jnp.zeros((KB, 128), BF16)
        return 0
    lax.fori_loop(0, w // KB, zero, 0)
    def prep(t, _):
        r = pl.ds(pl.multiple_of(t * KB, KB), KB)
        feat = jnp.where(three, 1.0, id_features(idk_ref[r, :], False)).astype(BF16)
        ones = jnp.where(three, 1.0, 0.0).astype(BF16)
        kk = k_ref[r, :]
        vv = v_ref[r, :]
        for h in range(2):
            kaug[h, r, :] = jnp.concatenate([kk[:, h * HD:(h + 1) * HD], feat], axis=1)
            vaug[h, r, :] = jnp.concatenate([vv[:, h * HD:(h + 1) * HD], ones], axis=1)
            acc[h, r, :] = jnp.zeros((KB, 128), F32)
        kt[:, r] = kk.T
        return 0
    lax.fori_loop(t_lo, t_hi, prep, 0)
    def pieces(x):
        a = x.astype(BF16).astype(F32)
        b = (x - a).astype(BF16).astype(F32)
        return a, b, x - a - b
    def qprep(t, _):
        r = pl.ds(pl.multiple_of(t * QB, QB), QB)
        fid = id_features(idq_ref[r, :], True).T
        row = lax.broadcasted_iota(jnp.int32, (HD, QB), 0)
        qt = (q_ref[r, :] * BF16(0.125)).T
        gg = g_ref[r, :]
        gt = gg.T
        prod = (gg.astype(F32) * o_ref[r, :].astype(F32)).T
        for h in range(2):
            a, b, c = pieces(-lse_ref[0, h:h + 1, r])
            f = jnp.where(row == 32, a, jnp.where(row == 33, b, jnp.where(row == 34, c, fid)))
            qaug[h, :, r] = jnp.concatenate([qt[h * HD:(h + 1) * HD, :], f.astype(BF16)], axis=0)
            d = -jnp.sum(prod[h * HD:(h + 1) * HD, :], axis=0, keepdims=True)
            a, b, c = pieces(d)
            f = jnp.where(row == 32, a, jnp.where(row == 33, b, jnp.where(row == 34, c, 0.0)))
            gaug[h, :, r] = jnp.concatenate([gt[h * HD:(h + 1) * HD, :], f.astype(BF16)], axis=0)
        return 0
    lax.fori_loop(0, nq, qprep, 0)
    def qloop(qb, _):
        rq = pl.ds(pl.multiple_of(qb * QB, QB), QB)
        qq = q_ref[rq, :] * BF16(0.125)
        gg = g_ref[rq, :]
        zz = jnp.zeros((QB, HD), BF16)
        qts = [qaug[h, :, rq] for h in range(2)]
        gts = [gaug[h, :, rq] for h in range(2)]
        rhs = [jnp.concatenate([jnp.concatenate([qq[:, h * HD:(h + 1) * HD], zz], axis=1), jnp.concatenate([zz, gg[:, h * HD:(h + 1) * HD]], axis=1)], axis=0) for h in range(2)]
        def kloop(t, c):
            r = pl.ds(pl.multiple_of(t * KB, KB), KB)
            new = []
            for h in range(2):
                s = jnp.dot(kaug[h, r, :], qts[h], preferred_element_type=F32)
                dp = jnp.dot(vaug[h, r, :], gts[h], preferred_element_type=F32)
                p = jnp.exp(s)
                ds = (p * dp).astype(BF16)
                both = jnp.concatenate([ds, p.astype(BF16)], axis=1)
                acc[h, r, :] += jnp.dot(both, rhs[h], preferred_element_type=F32)
                new.append(c[h] + jnp.dot(kt[h * HD:(h + 1) * HD, r], ds, preferred_element_type=F32))
            return tuple(new)
        z = jnp.zeros((HD, QB), F32)
        c = lax.fori_loop(lo_ref[qb], hi_ref[qb], kloop, (z, z))
        dq_ref[rq, :] = (jnp.concatenate([c[0], c[1]], axis=0) * 0.125).T
        return 0
    lax.fori_loop(0, nq, qloop, 0)
    def fin(t, _):
        r = pl.ds(pl.multiple_of(t * KB, KB), KB)
        a0 = acc[0, r, :]
        a1 = acc[1, r, :]
        dk_ref[r, :] = jnp.concatenate([a0[:, :HD], a1[:, :HD]], axis=1).astype(dk_ref.dtype)
        dv_ref[r, :] = jnp.concatenate([a0[:, HD:], a1[:, HD:]], axis=1).astype(dv_ref.dtype)
        return 0
    lax.fori_loop(t_lo, t_hi, fin, 0)

def attend_bwd(q, kwin, vwin, idq, idk, lo, hi, out, grad, lse, QB, KB):
    n, cols = q.shape
    w = kwin.shape[0]
    pairs = cols // 128
    nq = n // QB
    rows = lambda m: pl.BlockSpec((m, 128), lambda g, *_: (0, g))
    return pl.pallas_call(
        functools.partial(bwd_kernel, QB, KB, nq),
        grid_spec=pltpu.PrefetchScalarGridSpec(
            num_scalar_prefetch=2, grid=(pairs,),
            in_specs=[rows(n), rows(w), rows(w), pl.BlockSpec((n, 1), lambda g, *_: (0, 0)), pl.BlockSpec((w, 1), lambda g, *_: (0, 0)), rows(n), rows(n), pl.BlockSpec((1, 2, n), lambda g, *_: (g, 0, 0))],
            out_specs=[rows(n), rows(w), rows(w)],
            scratch_shapes=[pltpu.VMEM((2, w, 128), BF16), pltpu.VMEM((2, w, 128), BF16), pltpu.VMEM((128, w), BF16), pltpu.VMEM((2, 128, n), BF16), pltpu.VMEM((2, 128, n), BF16), pltpu.VMEM((2, w, 128), F32)]),
        out_shape=[jax.ShapeDtypeStruct((n, cols), F32), jax.ShapeDtypeStruct((w, cols), BF16), jax.ShapeDtypeStruct((w, cols), BF16)],
        compiler_params=pltpu.CompilerParams(vmem_limit_bytes=VMEM_LIMIT),
        name="attend_bwd",
    )(lo, hi, q, kwin, vwin, idq, idk, out, grad, lse)

def reach(ids_win, n, QB, KB):
    w = ids_win.shape[0]
    own = ids_win[n:2 * n].reshape(n // QB, QB)
    lo = jnp.argmax(ids_win[None, :] == own[:, :1], axis=1)
    hi = w - jnp.argmax(ids_win[::-1][None, :] == own[:, -1:], axis=1)
    return (lo // KB).astype(jnp.int32), ((hi + KB - 1) // KB).astype(jnp.int32)

def neighbours(axis):
    peers = lax.axis_size(axis)
    up = [(i, i + 1) for i in range(peers - 1)]
    return up, [(j, i) for i, j in up]


def with_halo(array):
    up, down = neighbours("dp")
    return jnp.concatenate(
        [lax.ppermute(array, "dp", up), array, lax.ppermute(array, "dp", down)], axis=0
    )


def own_part(array, n):
    block, chunks, sub = sizes(array.shape[0], n)
    first = lax.axis_index("tensor") * block
    return lax.dynamic_slice_in_dim(array, first, block, 0).reshape(chunks, sub, array.shape[1])


def weight_grad(left, right):
    rows = left.shape[0] * left.shape[1] * left.shape[2]
    return lax.dot_general(
        left.reshape(rows, -1),
        right.reshape(rows, -1),
        (((0,), (0,)), ((), ())),
        preferred_element_type=F32,
    ).astype(BF16)


def body(
    tokens, image_ids, cotangent, ln1_gain, ln1_bias, qkv_weight, qv_bias, proj_weight, proj_bias, scale_attn,
    ln2_gain, ln2_bias, fc1_weight, fc1_bias, fc2_weight, fc2_bias, scale_mlp,
):
    n = lax.axis_size("tensor")
    rows = tokens.shape[0]
    width = qkv_weight.shape[3]
    _, chunks, sub = sizes(rows, n)
    split = (n, chunks, sub)
    qkv2 = qkv_weight.reshape(LAYERS, D, 3 * width)
    ids_win = with_halo(image_ids + 1)
    lo, hi = reach(ids_win, rows, Q_BLOCK, K_BLOCK)
    idq, idk = ids_win[rows : 2 * rows, None], ids_win[:, None]

    stream = tokens.astype(F32)
    hat, _ = normalised(stream)
    a1 = (hat * ln1_gain[0] + ln1_bias[0]).astype(BF16)
    first = jnp.dot(a1, qkv2[0], preferred_element_type=F32)
    q = (first[:, :width] + qv_bias[0, 0]).astype(BF16)
    k = first[:, width : 2 * width].astype(BF16)
    v = (first[:, 2 * width :] + qv_bias[0, 1]).astype(BF16)
    a1 = a1.reshape(split + (D,))
    own = own_part(tokens, n).astype(F32)
    hat1, sp1 = normalised(own)

    saved = []
    for level in range(LAYERS):
        kwin, vwin = with_halo(k), with_halo(v)
        attended, lse = attend_fwd(q, kwin, vwin, idq, idk, lo, hi, Q_BLOCK, K_BLOCK)
        last = level == LAYERS - 1
        after = 0 if last else level + 1
        vec = jnp.stack(
            [
                proj_bias[level], scale_attn[level], ln2_gain[level], ln2_bias[level], fc2_bias[level],
                scale_mlp[level], ln1_gain[after], ln1_bias[after],
            ]
        )
        extra = () if last else (qkv2[level + 1], qv_bias[level + 1])
        outs = forward_block(
            n, last, level, attended, proj_weight[level], fc1_weight[level], fc2_weight[level], fc1_bias[level][None],
            vec, own, *extra,
        )
        u1, hat2, sp2, u2, a2, act, slope = outs[:7]
        saved.append((q, kwin, vwin, attended, lse, a1, hat1, sp1, u1, hat2, sp2, u2, a2, act, slope))
        if last:
            output = outs[7].reshape(rows, D)
        else:
            own, hat1, sp1, a1, q, k, v = outs[7:]
            q, k, v = (x.reshape(rows, width) for x in (q, k, v))

    cot = cotangent.astype(F32)
    source = (own_part(cotangent, n), (cot * scale_mlp[LAYERS - 1]).astype(BF16).reshape(split + (D,)))
    weights = [None] * LAYERS
    sums = [None] * (LAYERS + 1)
    narrow = [None] * LAYERS
    up, down = neighbours("dp")
    for level in reversed(range(LAYERS)):
        q, kwin, vwin, attended, lse, a1, hat1, sp1, u1, hat2, sp2, u2, a2, act, slope = saved[level]
        above = min(level + 1, LAYERS - 1)
        vec = jnp.stack([scale_mlp[level], ln2_gain[level], scale_attn[level], ln1_gain[above]])
        outs = backward_block(
            n, LAYERS + level, source, fc1_weight[level], fc2_weight[level], proj_weight[level], vec, slope, u1, hat2,
            sp2, u2,
        )
        e2 = source[1] if level == LAYERS - 1 else outs[0]
        dbn, e1, datt, gm, vec_sums, fc1b = outs[-6:]
        sums[level + 1] = vec_sums
        datt = datt.reshape(rows, width)
        dq, dkwin, dvwin = attend_bwd(q, kwin, vwin, idq, idk, lo, hi, attended, datt, lse, Q_BLOCK, K_BLOCK)

        def home(win):
            back = lax.ppermute(win[:rows], "dp", down).astype(F32)
            on = lax.ppermute(win[2 * rows :], "dp", up).astype(F32)
            return win[rows : 2 * rows].astype(F32) + back + on

        dk, dv = home(dkwin), home(dvwin)
        qv = jnp.stack([jnp.sum(dq, axis=0), jnp.sum(dv, axis=0)])
        dqkv = jnp.concatenate([dq, dk, dv], axis=1).astype(BF16).reshape(split + (3 * width,))
        narrow[level] = (qv, fc1b[0])
        weights[level] = lax.psum(
            (
                weight_grad(a1, dqkv),
                weight_grad(attended.reshape(split + (width,)), e1),
                weight_grad(a2, dbn),
                weight_grad(act, e2),
            ),
            "dp",
        )
        source = (dqkv, qkv2[level], hat1, sp1, gm)
    vec = jnp.stack([ln1_gain[0]] * 4)
    grad_tokens, sums[0] = backward_tail(n, 2 * LAYERS, *source, vec)
    total = lax.psum(jnp.stack(sums), ("dp", "tensor"))
    qv_total, fc1b_total = lax.psum(
        (jnp.stack([narrow[i][0] for i in range(LAYERS)]), jnp.stack([narrow[i][1] for i in range(LAYERS)])), "dp"
    )
    big = [jnp.stack([weights[i][j].astype(F32) for i in range(LAYERS)]) for j in range(4)]
    upper, lower = total[1:], total[:-1]
    return (
        output,
        grad_tokens.reshape(rows, D),
        lower[:, 6],
        lower[:, 7],
        big[0].reshape(LAYERS, D, 3, width),
        qv_total,
        big[1],
        upper[:, 5],
        upper[:, 4],
        upper[:, 2],
        upper[:, 3],
        big[2],
        fc1b_total,
        big[3],
        upper[:, 1],
        upper[:, 0],
    )


def solution(mesh):
    cols, stack_rows = P(None, None, "tensor"), P(None, "tensor", None)
    qkv = P(None, None, None, "tensor")
    return jax.shard_map(
        body,
        mesh=mesh,
        in_specs=(
            P("dp", None), P("dp"), P("dp", None), P(), P(), qkv, cols, stack_rows, P(), P(), P(), P(), cols,
            P(None, "tensor"), stack_rows, P(), P(),
        ),
        out_specs=(
            P("dp", None), P("dp", None), P(), P(), qkv, cols, stack_rows, P(), P(), P(), P(), cols,
            P(None, "tensor"), stack_rows, P(), P(),
        ),
        check_vma=False,
    )
```

time: 2730 us -> 1280 us (0.47)
  waiting for transfers between devices: 1590 us -> 352 us
  Pallas kernels: 0 us -> 650 us
  matrix products: 649 us -> 46 us
  other arithmetic: 256 us -> 53.8 us
  local copies, waits for them, and re-layouts: 177 us -> 58.7 us
  starting transfers between devices: 28.7 us -> 75.7 us
    psum x9 -> x2, waiting for transfers between devices: 1530 us -> 347 us  [the longest x1 257 us: body(): lax.psum((weight_grad(a1, dqkv), weight_grad(attended.reshape(split + (wi...]
    pallas_call x0 -> x9, Pallas kernels: none -> 650 us  [the longest x5 462 us: call(): pl.pallas_call(kernel, out_shape=[jax.ShapeDtypeStruct(s, d) for s, d in...]
    dot_general x66 -> x9, matrix products: 649 us -> 46 us  [the longest x8 41.5 us: weight_grad(): lax.dot_general(left.reshape(rows, -1), right.reshape(rows, -1), (((0,),...]
    reduce_sum x32 -> x8, other arithmetic: 179 us -> 6.51 us  [the longest x2 2.7 us: normalised(): centre = jnp.mean(stream, axis=-1, keepdims=True)]
    ppermute x10 -> x18, waiting for transfers between devices: 59.9 us -> 4.65 us  [the longest x4 2.19 us: home(): on = lax.ppermute(win[2 * rows:], 'dp', up).astype(F32)]
    ppermute x10 -> x18, starting transfers between devices: 28.4 us -> 75.6 us  [the longest x4 31.2 us: home(): back = lax.ppermute(win[:rows], 'dp', down).astype(F32)]
    slice x32 -> x14, local copies, waits for them, and re-layouts: 52.8 us -> 11.5 us  [the longest x4 5.79 us: home(): back = lax.ppermute(win[:rows], 'dp', down).astype(F32)]
    unnamed x344 -> x96, local copies, waits for them, and re-layouts: 57.3 us -> 19.2 us
  transfers between devices with their start and end apart: 19 -> 20, of which waited for: 17 -> 6; matrix products, arithmetic and copies ran while one was open for 5% -> 8% of each run, Pallas kernels for 0% -> 0%
where the time goes in v1:
time: 1280 us; the launch traced here: 1270 us
  Pallas kernels  650 us (51%)
  waiting for transfers between devices  352 us (28%)
  starting transfers between devices  75.7 us (6%)
  local copies, waits for them, and re-layouts  58.7 us (5%)
  other arithmetic  53.8 us (4%)
  matrix products  46 us (4%)
  blocking collectives  21.9 us (2%)
  between operations  15.2 us (1%)
    pallas_call x5, Pallas kernels, call(): pl.pallas_call(kernel, out_shape=[jax.ShapeDtypeStruct(s, d) for s, d in...  462 us
    psum x1, waiting for transfers between devices, body(): lax.psum((weight_grad(a1, dqkv), weight_grad(attended.reshape(split + (wi...  257 us
    pallas_call x2, Pallas kernels, attend_bwd(): pl.pallas_call(functools.partial(bwd_kernel, QB, KB, nq), grid_spec=pltpu...  104 us
    psum x1, waiting for transfers between devices, body(): total = lax.psum(jnp.stack(sums), ('dp', 'tensor'))  90.5 us
    pallas_call x2, Pallas kernels, attend_fwd(): pl.pallas_call(functools.partial(fwd_kernel, QB, KB, nq), grid_spec=pltpu...  83.6 us
    dot_general x8, matrix products, weight_grad(): lax.dot_general(left.reshape(rows, -1), right.reshape(rows, -1), (((0,),...  41.5 us
    ppermute x4, starting transfers between devices, home(): back = lax.ppermute(win[:rows], 'dp', down).astype(F32)  31.2 us
  transfers between devices with their start and end apart: 20, of which 6 were waited for; matrix products, arithmetic and copies ran while one was open for 8% of the time, Pallas kernels for 0%

profile of v1, /device:TPU:17, one launch (start us, length us, event | category | flops | bytes accessed | tf_op | source)
XLA Modules:
  0.0 1272.8 jit_solution(1667571523689601732)
XLA Ops:
  8.1 2.7 collective-permute-start.1
  10.8 3.1 collective-permute-start
  14.7 2.5 convert_reduce_fusion
  18.2 1.9 fusion.43
  20.1 2.6 copy.111
  22.7 4.5 fusion.41
  28.7 2.0 collective-permute-start.5
  30.7 3.6 collective-permute-start.4
  35.4 2.1 collective-permute-start.3
  39.4 2.7 slice_bitcast_fusion.4
  42.3 4.9 slice_bitcast_fusion
  50.0 2.6 copy.112
  52.6 2.6 copy.82.rest_0_.refs_1_
  55.8 3.8 collective-permute-start.2
  59.8 3.1 broadcast_in_dim.7.idk_ref
  64.8 3.2 pad_maximum_fusion.1.v_ref
  68.7 3.2 pad_maximum_fusion.k_ref
  71.9 41.8 %attend_fwd.2 = (bf16[1536,256]{1,0:T(8,128)(2,1)}, f32[2,2,1536]{2,1,0:T(2,128)}) custom-call(s32[3]{0:T(128)} %get-tuple-element.187.lo_ref, s32[3]{0:T(128)} %get-tuple-element.186.hi_ref, bf16[1536,256]{1,0:T(8,128)(2,1)} %get-tuple-element.127.q_ref, bf16[4608,256]{1,0:T(8,128)(2,1)} %pad_maximum_fusion.k_ref, ...), custom_call_target="tpu_custom_call" | custom-call | tf_op jit(solution)/shard_map/attend_fwd/pallas_call | solution.py:680
  113.7 112.6 %forward_block.1 = (f32[3,128,1024]{2,1,0:T(8,128)}, f32[3,128,1024]{2,1,0:T(8,128)}, f32[3,128,1]{2,1,0:T(8,128)}, f32[3,128,1024]{2,1,0:T(8,128)}, bf16[4,3,12...) custom-call(bf16[4,3,128,256]{3,2,1,0:T(8,128)(2,1)} %bitcast.152, ...), custom_call_target="tpu_custom_call" | custom-call | flops 9663676416 | bytes 100000000 | tf_op jit(solution)/shard_map/forward_block/pallas_call | solution.py:389
  226.2 9.4 collective-permute-start.7
  235.7 1.9 collective-permute-start.6
  237.6 4.5 multiply_convert_fusion
  242.1 2.4 collective-permute-start.9
  244.5 3.2 collective-permute-start.8
  248.3 2.8 copy.90.qkv
  252.5 2.1 constant_dynamic-slice_fusion
  254.7 3.2 pad_maximum_fusion.2.k_ref
  257.8 3.1 pad_maximum_fusion.3.v_ref
  261.0 41.8 %attend_fwd.3 = (bf16[1536,256]{1,0:T(8,128)(2,1)}, f32[2,2,1536]{2,1,0:T(2,128)}) custom-call(s32[3]{0:T(128)} %get-tuple-element.187.lo_ref, s32[3]{0:T(128)} %get-tuple-element.186.hi_ref, bf16[1536,256]{1,0:T(8,128)(2,1)} %bitcast.141, bf16[4608,256]{1,0:T(8,128)(2,1)} %pad_maximum_fusion.2.k_ref, bf16[4608,256]{1,0:T(8,128)(2,1)} %pad_maximum_fusion.3.v_ref, ...), custom_call_target="tpu_custom_call" | custom-call | tf_op jit(solution)/shard_map/attend_fwd/pallas_call | solution.py:680
  302.8 109.1 %forward_last.1 = (f32[3,128,1024]{2,1,0:T(8,128)}, f32[3,128,1024]{2,1,0:T(8,128)}, f32[3,128,1]{2,1,0:T(8,128)}, f32[3,128,1024]{2,1,0:T(8,128)}, bf16[4,3,128...) custom-call(bf16[4,3,128,256]{3,2,1,0:T(8,128)(2,1)} %bitcast.153, ...), custom_call_target="tpu_custom_call" | custom-call | flops 9663676416 | bytes 100000000 | tf_op jit(solution)/shard_map/forward_last/pallas_call | solution.py:389
  411.9 7.7 convert_bitcast_fusion
  419.5 65.5 %backward_first.1 = (bf16[4,3,128,1024]{3,2,1,0:T(8,128)(2,1)}, bf16[4,3,128,1024]{3,2,1,0:T(8,128)(2,1)}, bf16[4,3,128,256]{3,2,1,0:T(8,128)(2,1)}, f32[3,128,1...) custom-call(bf16[3,128,1024]{2,1,0:T(8,128)(2,1)} %bitcast.159, bf16[4,3,128,1024]{3,2,1,0:T(8,128)(2,1)} %bitcast.149, ...), custom_call_target="tpu_custom_call" | custom-call | flops 9663676416 | bytes 100000000 | tf_op jit(solution)/shard_map/backward_first/pallas_call | solution.py:389
  485.0 52.3 %attend_bwd.2 = (f32[1536,256]{1,0:T(8,128)}, bf16[4608,256]{1,0:T(8,128)(2,1)}, bf16[4608,256]{1,0:T(8,128)(2,1)}) custom-call(s32[3]{0:T(128)} %get-tuple-element.187.lo_ref, s32[3]{0:T(128)} %get-tuple-element.186.hi_ref, bf16[1536,256]{1,0:T(8,128)(2,1)} %bitcast.142, bf16[4608,256]{1,0:T(8,128)(2,1)} %pad_maximum_fusion.2.k_ref, ...), custom_call_target="tpu_custom_call" | custom-call | tf_op jit(solution)/shard_map/attend_bwd/pallas_call | solution.py:780
  539.0 14.6 %collective-permute-start.10 = (bf16[1536,256]{1,0:T(8,128)(2,1)S(1)}, bf16[1536,256]{1,0:T(8,128)(2,1)S(1)}, u32[]{:S(2)}, u32[]{:S(2)}) collective-permute-start(bf16[1536,256]{1,0:T(8,128)(2,1)S(1)} %get-tuple-element.142), channel_id=1, source_target_pairs={{4,0},{8,4},{12,8},{16,12},{20,16},{24,20},{28,24},{5,1},{9,5},{13... | collective-permute-start | bytes 2359304 | tf_op jit(solution)/shard_map/ppermute | solution.py:899
  553.5 1.9 collective-permute-start.11
  555.6 2.4 collective-permute-start.12
  558.0 3.2 collective-permute-start.13
  561.2 6.7 fusion.25
  567.9 1.8 fusion.30
  573.2 4.0 fusion.18
  578.8 115.7 %backward_block.1 = (bf16[4,3,128,1024]{3,2,1,0:T(8,128)(2,1)}, bf16[4,3,128,1024]{3,2,1,0:T(8,128)(2,1)}, bf16[4,3,128,1024]{3,2,1,0:T(8,128)(2,1)}, bf16[4,3,1...) custom-call(bf16[4,3,128,768]{3,2,1,0:T(8,128)(2,1)} %pad_maximum_fusion.4.refs_0_, ...), custom_call_target="tpu_custom_call" | custom-call | flops 9663676416 | bytes 100000000 | tf_op jit(solution)/shard_map/backward_block/pallas_call | solution.py:389
  694.4 52.1 %attend_bwd.3 = (f32[1536,256]{1,0:T(8,128)}, bf16[4608,256]{1,0:T(8,128)(2,1)}, bf16[4608,256]{1,0:T(8,128)(2,1)}) custom-call(s32[3]{0:T(128)} %get-tuple-element.187.lo_ref, s32[3]{0:T(128)} %get-tuple-element.186.hi_ref, bf16[1536,256]{1,0:T(8,128)(2,1)} %get-tuple-element.127.q_ref, bf16[4608,256]{1,0:T(8,128)(2,1)} %pad_maximum_fusion.k_ref, ...), custom_call_target="tpu_custom_call" | custom-call | tf_op jit(solution)/shard_map/attend_bwd/pallas_call | solution.py:780
  746.5 2.8 fusion.44
  749.3 11.7 collective-permute-start.14
  761.1 1.9 collective-permute-start.15
  763.0 6.8 fusion.26
  769.8 4.7 fusion.24
  775.7 2.6 copy.93
  778.3 2.5 collective-permute-start.16
  780.8 3.2 collective-permute-start.17
  784.0 4.0 fusion.29
  788.3 2.2 add_convert_fusion
  797.0 58.9 %backward_tail.1 = (f32[4,3,128,1024]{3,2,1,0:T(8,128)}, f32[8,1024]{1,0:T(8,128)}) custom-call(bf16[4,3,128,768]{3,2,1,0:T(8,128)(2,1)} %pad_maximum_fusion.5.dqkv, bf16[1024,768]{1,0:T(8,128)(2,1)} %copy.90.qkv, f32[3,128,1024]{2,1,0:T(8,128)} %subtract_multiply_fusion.hat1, f32[3,128,1]{2,1,0:T(8,128)} %copy.91.sp1, ...), custom_call_target="tpu_custom_call" | custom-call | flops 2415919104 | bytes 100000000 | tf_op jit(solution)/shard_map/backward_tail/pallas_call | solution.py:389
  857.4 5.9 fusion.21
  863.3 2.6 copy.92
  866.6 21.9 %all-reduce = (f32[2,2,256]{2,1,0:T(2,128)}, f32[2,1024]{1,0:T(2,128)}) all-reduce(f32[2,2,256]{2,1,0:T(2,128)S(1)} %pad_maximum_fusion.10, f32[2,1024]{1,0:T(2,128)S(1)} %pad_maximum_fusion.9), channel_id=1, replica_groups=mesh['dp'=8,'tensor'=4] {'dp'}, use_global_device_ids=true, to_apply=%region_13.14 | all-reduce | flops 3072 | bytes 24576 | tf_op jit(solution)/shard_map/psum | solution.py:920
  888.5 90.5 %all-reduce.5.cloned.1.call-done = f32[3,8,1024]{2,1,0:T(8,128)} async-done(((f32[3,8,1024]{2,1,0:T(8,128)}), f32[3,8,1024]{2,1,0:T(8,128)}) %all-reduce.5.cloned.1.call-update) | async-done | bytes 98320 | tf_op jit(solution)/shard_map/psum | solution.py:919
  985.1 256.8 %all-reduce.7.cloned.1.call-done = (bf16[1,1024,3,256]{3,1,2,0:T(8,128)(2,1)}, bf16[1,1024,3,256]{3,1,2,0:T(8,128)(2,1)}, bf16[1,256,1024]{2,1,0:T(8,128)(2,1)},...) async-done(((bf16[1,1024,3,256]{3,1,2,0:T(8,128)(2,1)}, ...) | async-done | bytes 12582928 | tf_op jit(solution)/shard_map/psum | solution.py:907
  1241.8 2.8 maximum_convert_fusion.3
  1244.7 3.5 maximum_convert_fusion.2
  1248.9 4.2 maximum_convert_fusion
  1253.1 4.8 maximum_convert_fusion.1
  1259.0 3.0 copy.140
  1262.9 2.7 copy.141
  (164 shorter events, 41.2 us)
Async XLA Ops:
  7.2 10.0 copy-start
  7.2 971.8 %all-reduce.5.cloned.1.call-start = ((), (), s32[]{:S(2)}) async-start(), calls=%async_computation | async-start | bytes 196608 | tf_op jit(solution)/shard_map/psum | solution.py:919
  8.1 47.7 %collective-permute-start.1 = (s32[1536]{0:T(1024)S(1)}, s32[1536]{0:T(1024)S(1)}, u32[]{:S(2)}, u32[]{:S(2)}) collective-permute-start(s32[1536]{0:T(1024)S(1)} %broadcast_add_fusion), channel_id=1, source_target_pairs={{4,0},{8,4},{12,8},{16,12},{20,16},{24,20},{28,24},{5,1},{9,5},{13... | collective-permute-start | bytes 18440 | tf_op jit(solution)/shard_map/ppermute | solution.py:808
  10.8 48.8 %collective-permute-start = (s32[1536]{0:T(1024)S(1)}, s32[1536]{0:T(1024)S(1)}, u32[]{:S(2)}, u32[]{:S(2)}) collective-permute-start(s32[1536]{0:T(1024)S(1)} %broadcast_add_fusion), channel_id=1, source_target_pairs={{0,4},{4,8},{8,12},{12,16},{16,20},{20,24},{24,28},{1,5},{5,9},{9,... | collective-permute-start | bytes 18440 | tf_op jit(solution)/shard_map/ppermute | solution.py:808
  14.7 3.5 copy-start.3
  20.1 2.6 copy-start.21
  20.1 2.6 copy-start.22
  27.2 10.3 copy-start.29
  28.7 10.1 copy-start.20
  28.7 36.2 %collective-permute-start.5 = (bf16[1536,256]{1,0:T(8,128)(2,1)}, bf16[1536,256]{1,0:T(8,128)(2,1)}, u32[]{:S(2)}, u32[]{:S(2)}) collective-permute-start(bf16[1536,256]{1,0:T(8,128)(2,1)} %get-tuple-element.126), channel_id=1, source_target_pairs={{4,0},{8,4},{12,8},{16,12},{20,16},{24,20},{28,24},{5,1},{9,5},{13... | collective-permute-start | bytes 2359304 | tf_op jit(solution)/shard_map/ppermute | solution.py:808
  30.7 34.1 %collective-permute-start.4 = (bf16[1536,256]{1,0:T(8,128)(2,1)}, bf16[1536,256]{1,0:T(8,128)(2,1)}, u32[]{:S(2)}, u32[]{:S(2)}) collective-permute-start(bf16[1536,256]{1,0:T(8,128)(2,1)} %get-tuple-element.126), channel_id=1, source_target_pairs={{0,4},{4,8},{8,12},{12,16},{16,20},{20,24},{24,28},{1,5},{5,9},{9,... | collective-permute-start | bytes 2359304 | tf_op jit(solution)/shard_map/ppermute | solution.py:808
  35.4 6.8 copy-start.23
  35.4 6.8 copy-start.24
  35.4 6.8 copy-start.25
  35.4 6.8 copy-start.26
  35.4 6.9 copy-start.27
  35.4 6.9 copy-start.28
  35.4 32.6 %collective-permute-start.3 = (bf16[1536,256]{1,0:T(8,128)(2,1)}, bf16[1536,256]{1,0:T(8,128)(2,1)}, u32[]{:S(2)}, u32[]{:S(2)}) collective-permute-start(bf16[1536,256]{1,0:T(8,128)(2,1)} %slice.284), channel_id=1, source_target_pairs={{4,0},{8,4},{12,8},{16,12},{20,16},{24,20},{28,24},{5,1},{9,5},{13... | collective-permute-start | bytes 2359304 | tf_op jit(solution)/shard_map/ppermute | solution.py:808
  38.1 4.2 copy-start.2
  38.4 8.8 copy-start.1
  55.8 12.9 %collective-permute-start.2 = (bf16[1536,256]{1,0:T(8,128)(2,1)}, bf16[1536,256]{1,0:T(8,128)(2,1)}, u32[]{:S(2)}, u32[]{:S(2)}) collective-permute-start(bf16[1536,256]{1,0:T(8,128)(2,1)} %slice.284), channel_id=1, source_target_pairs={{0,4},{4,8},{8,12},{12,16},{16,20},{20,24},{24,28},{1,5},{5,9},{9,... | collective-permute-start | bytes 2359304 | tf_op jit(solution)/shard_map/ppermute | solution.py:808
  226.2 28.4 %collective-permute-start.7 = (bf16[1536,256]{1,0:T(8,128)(2,1)}, bf16[1536,256]{1,0:T(8,128)(2,1)}, u32[]{:S(2)}, u32[]{:S(2)}) collective-permute-start(bf16[1536,256]{1,0:T(8,128)(2,1)} %bitcast.154), channel_id=1, source_target_pairs={{4,0},{8,4},{12,8},{16,12},{20,16},{24,20},{28,24},{5,1},{9,5},{13... | collective-permute-start | bytes 2359304 | tf_op jit(solution)/shard_map/ppermute | solution.py:808
  235.7 19.0 %collective-permute-start.6 = (bf16[1536,256]{1,0:T(8,128)(2,1)}, bf16[1536,256]{1,0:T(8,128)(2,1)}, u32[]{:S(2)}, u32[]{:S(2)}) collective-permute-start(bf16[1536,256]{1,0:T(8,128)(2,1)} %bitcast.155), channel_id=1, source_target_pairs={{0,4},{4,8},{8,12},{12,16},{16,20},{20,24},{24,28},{1,5},{5,9},{9,... | collective-permute-start | bytes 2359304 | tf_op jit(solution)/shard_map/ppermute | solution.py:808
  242.1 15.8 %collective-permute-start.9 = (bf16[1536,256]{1,0:T(8,128)(2,1)}, bf16[1536,256]{1,0:T(8,128)(2,1)}, u32[]{:S(2)}, u32[]{:S(2)}) collective-permute-start(bf16[1536,256]{1,0:T(8,128)(2,1)} %bitcast.14), channel_id=1, source_target_pairs={{4,0},{8,4},{12,8},{16,12},{20,16},{24,20},{28,24},{5,1},{9,5},{13... | collective-permute-start | bytes 2359304 | tf_op jit(solution)/shard_map/ppermute | solution.py:808
  244.5 13.4 %collective-permute-start.8 = (bf16[1536,256]{1,0:T(8,128)(2,1)}, bf16[1536,256]{1,0:T(8,128)(2,1)}, u32[]{:S(2)}, u32[]{:S(2)}) collective-permute-start(bf16[1536,256]{1,0:T(8,128)(2,1)} %bitcast.14), channel_id=1, source_target_pairs={{0,4},{4,8},{8,12},{12,16},{16,20},{20,24},{24,28},{1,5},{5,9},{9,... | collective-permute-start | bytes 2359304 | tf_op jit(solution)/shard_map/ppermute | solution.py:808
  537.3 18.1 %copy-start.8 = (bf16[4608,256]{1,0:T(8,128)(2,1)S(1)}, bf16[4608,256]{1,0:T(8,128)(2,1)}, u32[]{:S(2)}) copy-start(bf16[4608,256]{1,0:T(8,128)(2,1)} %get-tuple-element.83) | copy-start | bytes 7077892
  537.3 23.8 %copy-start.36 = (bf16[4,3,128,1024]{3,2,1,0:T(8,128)(2,1)S(1)}, bf16[4,3,128,1024]{3,2,1,0:T(8,128)(2,1)}, u32[]{:S(2)}) copy-start(bf16[4,3,128,1024]{3,2,1,0:T(8,128)(2,1)} %get-tuple-element.107) | copy-start | bytes 9437188
  539.0 31.0 %collective-permute-start.10 = (bf16[1536,256]{1,0:T(8,128)(2,1)S(1)}, bf16[1536,256]{1,0:T(8,128)(2,1)S(1)}, u32[]{:S(2)}, u32[]{:S(2)}) collective-permute-start(bf16[1536,256]{1,0:T(8,128)(2,1)S(1)} %get-tuple-element.142), channel_id=1, source_target_pairs={{4,0},{8,4},{12,8},{16,12},{20,16},{24,20},{28,24},{5,1},{9,5},{13... | collective-permute-start | bytes 2359304 | tf_op jit(solution)/shard_map/ppermute | solution.py:899
  553.5 16.5 %collective-permute-start.11 = (bf16[1536,256]{1,0:T(8,128)(2,1)S(1)}, bf16[1536,256]{1,0:T(8,128)(2,1)S(1)}, u32[]{:S(2)}, u32[]{:S(2)}) collective-permute-start(bf16[1536,256]{1,0:T(8,128)(2,1)S(1)} %get-tuple-element.143), channel_id=1, source_target_pairs={{0,4},{4,8},{8,12},{12,16},{16,20},{20,24},{24,28},{1,5},{5,9},{9,... | collective-permute-start | bytes 2359304 | tf_op jit(solution)/shard_map/ppermute | solution.py:900
  555.6 16.0 %collective-permute-start.12 = (bf16[1536,256]{1,0:T(8,128)(2,1)S(1)}, bf16[1536,256]{1,0:T(8,128)(2,1)S(1)}, u32[]{:S(2)}, u32[]{:S(2)}) collective-permute-start(bf16[1536,256]{1,0:T(8,128)(2,1)S(1)} %get-tuple-element.144), channel_id=1, source_target_pairs={{4,0},{8,4},{12,8},{16,12},{20,16},{24,20},{28,24},{5,1},{9,5},{13... | collective-permute-start | bytes 2359304 | tf_op jit(solution)/shard_map/ppermute | solution.py:899
  558.0 14.8 %collective-permute-start.13 = (bf16[1536,256]{1,0:T(8,128)(2,1)S(1)}, bf16[1536,256]{1,0:T(8,128)(2,1)S(1)}, u32[]{:S(2)}, u32[]{:S(2)}) collective-permute-start(bf16[1536,256]{1,0:T(8,128)(2,1)S(1)} %get-tuple-element.145), channel_id=1, source_target_pairs={{0,4},{4,8},{8,12},{12,16},{16,20},{20,24},{24,28},{1,5},{5,9},{9,... | collective-permute-start | bytes 2359304 | tf_op jit(solution)/shard_map/ppermute | solution.py:900
  561.2 6.7 copy-start.17
  561.2 6.7 copy-start.33
  567.9 1.8 copy-start.16
  570.0 3.2 copy-start.32
  746.5 16.5 %copy-start.35 = (bf16[4,3,128,1024]{3,2,1,0:T(8,128)(2,1)S(1)}, bf16[4,3,128,1024]{3,2,1,0:T(8,128)(2,1)}, u32[]{:S(2)}) copy-start(bf16[4,3,128,1024]{3,2,1,0:T(8,128)(2,1)} %get-tuple-element.111) | copy-start | bytes 9437188
  749.3 39.0 %collective-permute-start.14 = (bf16[1536,256]{1,0:T(8,128)(2,1)}, bf16[1536,256]{1,0:T(8,128)(2,1)}, u32[]{:S(2)}, u32[]{:S(2)}) collective-permute-start(bf16[1536,256]{1,0:T(8,128)(2,1)} %get-tuple-element.138), channel_id=1, source_target_pairs={{4,0},{8,4},{12,8},{16,12},{20,16},{24,20},{28,24},{5,1},{9,5},{13... | collective-permute-start | bytes 2359304 | tf_op jit(solution)/shard_map/ppermute | solution.py:899
  761.1 27.2 %collective-permute-start.15 = (bf16[1536,256]{1,0:T(8,128)(2,1)}, bf16[1536,256]{1,0:T(8,128)(2,1)}, u32[]{:S(2)}, u32[]{:S(2)}) collective-permute-start(bf16[1536,256]{1,0:T(8,128)(2,1)} %get-tuple-element.139), channel_id=1, source_target_pairs={{0,4},{4,8},{8,12},{12,16},{16,20},{20,24},{24,28},{1,5},{5,9},{9,... | collective-permute-start | bytes 2359304 | tf_op jit(solution)/shard_map/ppermute | solution.py:900
  763.0 6.8 copy-start.34
  763.0 6.8 copy-start.37
  769.8 4.7 copy-start.7
  778.3 9.7 copy-start.15
  778.3 13.9 %collective-permute-start.16 = (bf16[1536,256]{1,0:T(8,128)(2,1)}, bf16[1536,256]{1,0:T(8,128)(2,1)S(1)}, u32[]{:S(2)}, u32[]{:S(2)}) collective-permute-start(bf16[1536,256]{1,0:T(8,128)(2,1)} %get-tuple-element.140), channel_id=1, source_target_pairs={{4,0},{8,4},{12,8},{16,12},{20,16},{24,20},{28,24},{5,1},{9,5},{13... | collective-permute-start | bytes 2359304 | tf_op jit(solution)/shard_map/ppermute | solution.py:899
  780.8 12.4 collective-permute-start.17
  788.3 6.5 copy-start.4
  790.5 5.9 copy-start.5
  794.7 2.3 copy-start.6
  797.0 58.9 %copy-start.18 = (f32[8,1024]{1,0:T(8,128)S(1)}, f32[8,1024]{1,0:T(8,128)}, u32[]{:S(2)}) copy-start(f32[8,1024]{1,0:T(8,128)} %get-tuple-element.101) | copy-start | bytes 98308
  797.0 58.9 %copy-start.19 = (f32[8,1024]{1,0:T(8,128)S(1)}, f32[8,1024]{1,0:T(8,128)}, u32[]{:S(2)}) copy-start(f32[8,1024]{1,0:T(8,128)} %get-tuple-element.100) | copy-start | bytes 98308
  857.3 384.5 %all-reduce.7.cloned.1.call-start = ((), (), s32[]{:S(2)}) async-start(), calls=%async_computation.1 | async-start | bytes 25165824 | tf_op jit(solution)/shard_map/psum | solution.py:907
  865.9 0.7 copy-start.30
  865.9 0.7 copy-start.31
  1241.8 2.8 copy-start.13
  1241.8 2.8 copy-start.14
  1244.7 3.5 copy-start.11
  1244.7 4.3 copy-start.12
  1248.9 4.2 copy-start.9
  1248.9 4.2 copy-start.10
  1253.1 4.8 slice-start
  1253.1 5.9 slice-start.1
  1253.1 8.9 slice-start.2
  1257.9 4.9 slice-start.3
Sparse Core Ops, SparseCore 0:
  857.4 121.4 all-reduce.4
  983.1 258.7 all-reduce.6

commit v2 on v1

v2 whole, which is shorter than its diff:
```python
import functools
import jax
import jax.numpy as jnp
from jax import lax
from jax.experimental import pallas as pl
from jax.experimental.pallas import tpu as pltpu
from jax.sharding import PartitionSpec as P

HD = 64
LAYERS = 2
D = 1024
MESH = pl.DeviceIdType.MESH
F32 = jnp.float32
BF16 = jnp.bfloat16
eps = 1e-06
half_root = 0.7071067811865476
density_scale = 0.3989422804014327
BIG = 1e30
TILES = (4, 512, 512, 256)
VMEM_LIMIT = 62 * 2**20


def bit_of(index, k):
    return (index // (1 << k)) % 2


def order_bits(nbits, half):
    return tuple(range(nbits)) if half == 0 else tuple(reversed(range(nbits)))


def compose(free_bits, free_value, fixed):
    index = sum(value * (1 << k) for k, value in fixed.items())
    for place, k in enumerate(free_bits):
        index = index + ((free_value >> place) & 1) * (1 << k)
    return index


class Names:
    def __getattr__(self, key):
        return key


N = Names()


class Exchange:
    def __init__(self, n, chunks, sub):
        self.n, self.chunks, self.sub = n, chunks, sub
        self.nbits = n.bit_length() - 1
        self.half = sub // 2
        self.me = lax.axis_index(N.tensor)
        self.bits = [bit_of(self.me, k) for k in range(self.nbits)]
        self.pending = []

    def partner(self, k):
        return self.me + (1 - 2 * self.bits[k]) * (1 << k)

    def partners(self):
        return [{N.tensor: self.partner(k)} for k in range(self.nbits)]

    def rows(self, h):
        return pl.ds(h * self.half, self.half)

    def copy(self, src, dst, sems, c, h, message, k):
        return pltpu.make_async_remote_copy(
            src_ref=src,
            dst_ref=dst,
            send_sem=sems.at[0, c, h, message],
            recv_sem=sems.at[1, c, h, message],
            device_id={N.tensor: self.partner(k)},
            device_id_type=MESH,
        )

    def rs_base(self, p):
        return sum(self.n >> (q + 1) for q in range(p))

    def rs_fixed(self, order, p, flip):
        fixed = {k: self.bits[k] for k in order[:p]}
        fixed[order[p]] = 1 - self.bits[order[p]] if flip else self.bits[order[p]]
        return fixed

    def rs_places(self, order, p, f):
        places = []
        for q in range(p):
            free = order[q + 1 :]
            index = 0
            for place, k in enumerate(free):
                at = order.index(k)
                if at < p:
                    value = self.bits[k]
                elif at == p:
                    value = 1 - self.bits[k]
                else:
                    value = (f >> (at - p - 1)) & 1
                index = index + value * (1 << place)
            places.append(self.rs_base(q) + index)
        return places

    def rs_send(self, part, recv, sems, c, p):
        for h in range(2):
            order = order_bits(self.nbits, h)
            free = order[p + 1 :]
            for f in range(1 << len(free)):
                b = compose(free, f, self.rs_fixed(order, p, True))
                message = self.rs_base(p) + f
                if p > 0:
                    total = part[b, c, self.rows(h), :].astype(F32)
                    for place in self.rs_places(order, p, f):
                        total = total + recv[c, place, self.rows(h), :].astype(F32)
                    part[b, c, self.rows(h), :] = total.astype(BF16)
                cp = self.copy(
                    part.at[b, c, self.rows(h), :],
                    recv.at[c, message, self.rows(h), :],
                    sems,
                    c,
                    h,
                    message,
                    order[p],
                )
                cp.start()
                self.pending.append(cp)

    def rs_wait(self, part, recv, sems, c, p):
        for h in range(2):
            order = order_bits(self.nbits, h)
            for f in range(self.n >> (p + 1)):
                message = self.rs_base(p) + f
                self.copy(
                    part.at[0, c, self.rows(h), :],
                    recv.at[c, message, self.rows(h), :],
                    sems,
                    c,
                    h,
                    message,
                    order[p],
                ).wait_recv()

    def rs_total(self, part, recv, c):
        halves = []
        for h in range(2):
            order = order_bits(self.nbits, h)
            total = part[self.me, c, self.rows(h), :].astype(F32)
            for p in range(self.nbits):
                free = order[p + 1 :]
                place = self.rs_base(p) + sum(
                    self.bits[k] * (1 << at) for at, k in enumerate(free)
                )
                total = total + recv[c, place, self.rows(h), :].astype(F32)
            halves.append(total)
        return jnp.concatenate(halves, axis=0)

    def ag_send(self, full, sems, c, p):
        for h in range(2):
            order = order_bits(self.nbits, h)
            fixed = {k: self.bits[k] for k in order[p:]}
            for f in range(1 << p):
                b = compose(order[:p], f, fixed)
                message = (1 << p) - 1 + f
                ref = full.at[b, c, self.rows(h), :]
                cp = self.copy(ref, ref, sems, c, h, message, order[p])
                cp.start()
                self.pending.append(cp)

    def ag_wait(self, full, sems, c, p):
        for h in range(2):
            order = order_bits(self.nbits, h)
            fixed = {k: self.bits[k] for k in order[p + 1 :]}
            fixed[order[p]] = 1 - self.bits[order[p]]
            for f in range(1 << p):
                b = compose(order[:p], f, fixed)
                message = (1 << p) - 1 + f
                ref = full.at[b, c, self.rows(h), :]
                self.copy(ref, ref, sems, c, h, message, order[p]).wait_recv()

    def drain(self):
        for cp in self.pending:
            cp.wait_send()
        self.pending = []


def erf(x):
    c = jnp.clip(x, -3.832506856900711, 3.832506856900711)
    s = c * c
    top = jnp.full_like(s, 0.00022905065861350646)
    for k in (0.0034082910107109506, 0.050955695062380861, 0.18520832239976145, 1.128379143519084):
        top = top * s + k
    low = jnp.full_like(s, -1.1791602954361697e-7)
    for k in (
        0.000023547966471313185,
        0.0010179625278914885,
        0.014070470171167667,
        0.11098505178285362,
        0.49746925110067538,
        1.0,
    ):
        low = low * s + k
    return c * top / low


def gelu_pair(before):
    cumulative = 0.5 * (1.0 + erf(before * half_root))
    density = jnp.exp(-0.5 * before * before) * density_scale
    return before * cumulative, cumulative + before * density


def normalised(stream):
    centre = jnp.mean(stream, axis=-1, keepdims=True)
    centred = stream - centre
    spread = lax.rsqrt(jnp.mean(centred * centred, axis=-1, keepdims=True) + eps)
    return centred * spread, spread


def norm_back(upstream, normed, spread, gain_row):
    scaled = upstream * gain_row
    return spread * (
        scaled
        - jnp.mean(scaled, axis=-1, keepdims=True)
        - normed * jnp.mean(scaled * normed, axis=-1, keepdims=True)
    )


def chunk_of(ref, c):
    x = ref[:, c]
    return x.reshape(x.shape[0] * x.shape[1], x.shape[2])


def column_loop(width, step, fn):
    if width <= step:
        fn(pl.ds(0, width))
    else:

        def one(j, carry):
            fn(pl.ds(pl.multiple_of(j * step, step), step))
            return carry

        lax.fori_loop(0, width // step, one, 0)


def matmul_nn(x, w_ref, cols):
    return jnp.dot(x, w_ref[:, cols], preferred_element_type=F32)


def matmul_nt(x, w_ref, cols):
    return lax.dot_general(
        x, w_ref[cols, :], (((1,), (1,)), ((), ())), preferred_element_type=F32
    )


def tall(ref, cols=slice(None)):
    x = ref[..., cols]
    return x.reshape(x.shape[0] * x.shape[1] * x.shape[2], x.shape[3])


def grad_items(left, right, out, first, step=256):
    width = left.shape[3]
    step = min(step, width)

    def item(at):
        y = lax.dot_general(
            tall(left, slice(at, at + step)), tall(right), (((0,), (0,)), ((), ())), preferred_element_type=F32
        )
        out[first + at : first + at + step, :] = y.astype(BF16)

    return [functools.partial(item, at) for at in range(0, width, step)]


def with_items(ex, stage, items):
    share = -(-len(items) // ex.chunks)

    def both(c):
        for item in items[c * share : (c + 1) * share]:
            item()
        stage(c)

    return both


def rs_stages(ex, part, recv, sems):
    stages = []
    for p in range(1, ex.nbits):

        def stage(c, p=p):
            ex.rs_wait(part, recv, sems, c, p - 1)
            ex.rs_send(part, recv, sems, c, p)

        stages.append(stage)
    return stages


def ag_stages(ex, full, sems):
    stages = []
    for p in range(1, ex.nbits):

        def stage(c, p=p):
            ex.ag_wait(full, sems, c, p - 1)
            ex.ag_send(full, sems, c, p)

        stages.append(stage)
    return stages


def sizes(rows, n):
    block = rows // n
    chunks = 3 if block % 96 == 0 else (2 if block % 64 == 0 else 1)
    return block, chunks, block // chunks


class Total:
    def __init__(self, bufs, recv, sems, dp_size, n, wide):
        self.bufs, self.recv, self.sems, self.wide = bufs, recv, sems, wide
        self.axes = [(N.dp, k) for k in range(dp_size.bit_length() - 1)]
        self.axes += [(N.tensor, k) for k in range(n.bit_length() - 1)]
        self.copies = []

    def target(self, i):
        axis, k = self.axes[i]
        me = lax.axis_index(axis)
        return {axis: me + (1 - 2 * bit_of(me, k)) * (1 << k)}

    def partners(self):
        return [self.target(i) for i, (axis, _) in enumerate(self.axes) if axis == N.dp]

    def start(self, i):
        cp = pltpu.make_async_remote_copy(
            src_ref=self.bufs.at[i],
            dst_ref=self.recv.at[i],
            send_sem=self.sems.at[0, i],
            recv_sem=self.sems.at[1, i],
            device_id=self.target(i),
            device_id_type=MESH,
        )
        cp.start()
        self.copies.append(cp)

    def step(self, i):
        self.copies[i].wait_recv()
        axis, _ = self.axes[i]
        total = self.bufs[i] + self.recv[i]
        if axis == N.tensor:
            row = lax.broadcasted_iota(jnp.int32, total.shape, 0)
            total = jnp.where(row < self.wide, total, self.bufs[i])
        self.bufs[i + 1] = total
        if i + 1 < len(self.axes):
            self.start(i + 1)

    def drain(self):
        for cp in self.copies:
            cp.wait_send()


def run_stages(ex, stages, extra=()):
    extra = sorted(extra, key=lambda pair: pair[0])
    slot = 0
    for stage in stages:
        for c in range(ex.chunks):
            while extra and extra[0][0] <= slot:
                extra.pop(0)[1]()
            stage(c)
            slot += 1
    for _, thunk in extra:
        thunk()


def meet(partners):
    sem = pltpu.get_barrier_semaphore()
    for partner in partners:
        pl.semaphore_signal(sem, inc=1, device_id=partner, device_id_type=MESH)
    pl.semaphore_wait(sem, len(partners))


class Refs:
    def __init__(self):
        self.loads, self.targets, self.stores = {}, {}, []

    def need(self, *names):
        for name in names:
            if name in self.loads:
                self.loads.pop(name).wait()

    def store(self, name, index=()):
        cp = pltpu.make_async_copy(
            getattr(self, name).at[index] if index else getattr(self, name),
            self.targets[name].at[index] if index else self.targets[name],
            self.store_sems.at[len(self.stores)],
        )
        cp.start()
        self.stores.append(cp)

    def finish(self):
        self.need(*list(self.loads))
        for cp in self.stores:
            cp.wait()


def call(kernel, name, collective_id, ins, outs, scratch, flops):
    late_in = [(k, a) for k, a, late in ins if late is True]
    late_out = [(k, shape, dtype) for k, shape, dtype, late in outs if late is True]

    def entry(*refs):
        refs = list(refs)
        take = lambda count: [refs.pop(0) for _ in range(count)]
        r = Refs()
        r.sources = {}
        in_refs, out_refs = take(len(ins)), take(len(outs))
        in_bufs, out_bufs = take(len(late_in)), take(len(late_out))
        load_sems, r.store_sems = take(2)
        bufs = {k: b for (k, _), b in zip(late_in, in_bufs)}
        for (k, _, late), ref in zip(ins, in_refs):
            if late == N.far:
                r.sources[k] = ref
                continue
            setattr(r, k, bufs[k] if late else ref)
            if late:
                cp = pltpu.make_async_copy(ref, bufs[k], load_sems.at[len(r.loads)])
                cp.start()
                r.loads[k] = cp
        bufs = {k: b for (k, _, _), b in zip(late_out, out_bufs)}
        for (k, _), ref in zip(scratch, take(len(scratch))):
            setattr(r, k, ref)
        for (k, _, _, late), ref in zip(outs, out_refs):
            if late == N.far:
                r.targets[k] = ref
                continue
            setattr(r, k, getattr(r, late) if isinstance(late, str) else bufs[k] if late else ref)
            if late:
                r.targets[k] = ref
        kernel(r)
        r.finish()

    space = lambda late: pl.BlockSpec(memory_space=pl.ANY if late else pltpu.VMEM)
    result = pl.pallas_call(
        entry,
        out_shape=[jax.ShapeDtypeStruct(shape, dtype) for _, shape, dtype, _ in outs],
        in_specs=[space(late) for _, _, late in ins],
        out_specs=[space(late) for _, _, _, late in outs],
        scratch_shapes=[pltpu.VMEM(a.shape, a.dtype) for _, a in late_in]
        + [pltpu.VMEM(shape, dtype) for _, shape, dtype in late_out]
        + [pltpu.SemaphoreType.DMA((max(len(late_in), 1),)), pltpu.SemaphoreType.DMA((64,))]
        + [spec for _, spec in scratch],
        compiler_params=pltpu.CompilerParams(
            collective_id=collective_id, has_side_effects=True, vmem_limit_bytes=VMEM_LIMIT
        ),
        cost_estimate=pl.CostEstimate(flops=flops, bytes_accessed=10**8, transcendentals=0),
        name=name,
    )(*[a for _, a, _ in ins])
    return dict(zip([k for k, _, _, _ in outs], result))


def comm_scratch(n, chunks, sub, tag):
    return [
        (N.part + tag, pltpu.VMEM((n, chunks, sub, D), BF16)),
        (N.recv + tag, pltpu.VMEM((chunks, n - 1, sub, D), BF16)),
    ]


def sem_scratch(stages, n, chunks):
    return [(N.sems, pltpu.SemaphoreType.DMA((stages, 2, chunks, 2, n - 1)))]


class Halo:
    def __init__(self, sems, dp_size):
        self.sems, self.size = sems, dp_size
        self.me = lax.axis_index(N.dp)
        self.has = (self.me < dp_size - 1, self.me > 0)
        self.pending = []

    def partners(self):
        return [{N.dp: (self.me + step) % self.size} for step in (1, self.size - 1)]

    def copy(self, src, dst, way, message):
        step = 1 if way == 0 else -1
        return pltpu.make_async_remote_copy(
            src_ref=src,
            dst_ref=dst,
            send_sem=self.sems.at[0, way, message],
            recv_sem=self.sems.at[1, way, message],
            device_id={N.dp: self.me + step},
            device_id_type=MESH,
        )

    def send(self, src, dst, way, message):
        cp = self.copy(src, dst, way, message)

        @pl.when(self.has[way])
        def _():
            cp.start()

        self.pending.append((cp, way))

    def wait(self, dst, way, message):
        @pl.when(self.has[1 - way])
        def _():
            self.copy(dst, dst, way, message).wait_recv()

    def drain(self):
        for cp, way in self.pending:

            @pl.when(self.has[way])
            def _(cp=cp):
                cp.wait_send()


class GradSum:
    def __init__(self, arrays, sems, dp_size):
        self.arrays, self.sems = arrays, sems
        self.local = {}
        self.k = dp_size.bit_length() - 1
        self.me = lax.axis_index(N.dp)
        self.bits = [bit_of(self.me, k) for k in range(self.k)]
        self.pending = []

    def partner(self, k):
        return {N.dp: self.me + (1 - 2 * self.bits[k]) * (1 << k)}

    def partners(self):
        return [self.partner(k) for k in range(self.k)]

    def offset(self, rows, k):
        return sum(self.bits[i] * (rows >> (i + 1)) for i in range(k))

    def copy(self, src, dst, a, message, k):
        return pltpu.make_async_remote_copy(
            src_ref=src,
            dst_ref=dst,
            send_sem=self.sems.at[0, a, message],
            recv_sem=self.sems.at[1, a, message],
            device_id=self.partner(k),
            device_id_type=MESH,
        )

    def recv_rows(self, a, k):
        rows, _, _, _, start, _ = self.arrays[a]
        return (rows >> start) - (rows >> k)

    def here(self, a, at, size):
        rows, _, _, _, start, _ = self.arrays[a]
        return pl.ds(pl.multiple_of(at - self.offset(rows, start), 16), size)

    def add(self, a, base, size, k):
        rows, grad, recv, _, start, _ = self.arrays[a]
        step = 32 if size % 32 == 0 else 16

        def block(i, carry):
            at = base + i * step
            here = self.here(a, at, step)
            total = grad[here, :].astype(F32)
            for j in range(start, k):
                there = at - self.offset(rows, j + 1) + self.recv_rows(a, j)
                total = total + recv[pl.ds(pl.multiple_of(there, 16), step), :].astype(F32)
            grad[here, :] = total.astype(BF16)
            return carry

        lax.fori_loop(0, size // step, block, 0)

    def merge(self, a):
        rows, grad, _, _, start, pieces = self.arrays[a]
        size = rows >> start
        step = 32 if size % 32 == 0 else 16

        def block(i, carry):
            here = pl.ds(pl.multiple_of(i * step, 16), step)
            grad[here, :] = sum(x[here, :].astype(F32) for x in pieces).astype(BF16)
            return carry

        lax.fori_loop(0, size // step, block, 0)

    def send(self, a, k):
        rows, grad, recv, _, start, _ = self.arrays[a]
        size = rows >> (k + 1)
        base = self.offset(rows, k) + (1 - self.bits[k]) * size
        if k > start:
            self.add(a, base, size, k)
        cp = self.copy(
            grad.at[self.here(a, base, size), :], recv.at[pl.ds(self.recv_rows(a, k), size), :], a, k, k
        )
        cp.start()
        self.pending.append(cp)

    def wait(self, a, k):
        rows, _, recv, _, _, _ = self.arrays[a]
        ref = recv.at[pl.ds(self.recv_rows(a, k), rows >> (k + 1)), :]
        self.copy(ref, ref, a, k, k).wait_recv()

    def split(self, a, keep, send):
        rows, grad, recv, _, _, _ = self.arrays[a]
        size = rows >> 2
        step = 32 if size % 32 == 0 else 16
        for out, bit in ((keep, self.bits[1]), (send, 1 - self.bits[1])):

            def block(i, carry, out=out, bit=bit):
                at = bit * size + i * step
                mine = grad[pl.ds(pl.multiple_of(self.bits[0] * 2 * size + at, 16), step), :].astype(F32)
                total = mine + recv[pl.ds(pl.multiple_of(at, 16), step), :].astype(F32)
                out[pl.ds(pl.multiple_of(i * step, 16), step), :] = total.astype(BF16)
                return carry

            lax.fori_loop(0, size // step, block, 0)

    def own(self, a, k, mine):
        rows, _, _, out, _, _ = self.arrays[a]
        size = rows >> (k + 1)
        base = self.offset(rows, k + 1) if mine else self.offset(rows, k) + (1 - self.bits[k]) * size
        return out.at[pl.ds(pl.multiple_of(base, 16), size), :]

    def gather_send(self, a, k):
        ref = self.own(a, k, True)
        src = ref
        if k == self.k - 1:
            rows, grad = self.arrays[a][:2]
            src = grad.at[self.here(a, self.offset(rows, self.k), rows >> self.k), :]
            self.local[a] = pltpu.make_async_copy(src, ref, self.sems.at[0, a, 2 * self.k])
            self.local[a].start()
        elif k == self.k - 2:
            self.local[a].wait()
        cp = self.copy(src, ref, a, self.k + k, k)
        cp.start()
        self.pending.append(cp)

    def gather_wait(self, a, k):
        ref = self.own(a, k, False)
        self.copy(ref, ref, a, self.k + k, k).wait_recv()

    def steps(self, a):
        last, start = self.k - 1, self.arrays[a][4]

        def first():
            if start:
                self.merge(a)
            self.send(a, start)

        def halve(k):
            self.wait(a, k - 1)
            self.send(a, k)

        def turn():
            rows = self.arrays[a][0]
            self.wait(a, last)
            self.add(a, self.offset(rows, self.k), rows >> self.k, self.k)
            self.gather_send(a, last)

        def double(k):
            self.gather_wait(a, k + 1)
            self.gather_send(a, k)

        out = [first] + [functools.partial(halve, k) for k in range(start + 1, self.k)] + [turn]
        out += [functools.partial(double, k) for k in reversed(range(last))]
        return out + [functools.partial(self.gather_wait, a, 0)]

    def drain(self):
        for cp in self.pending:
            cp.wait_send()


def grad_scratch(shapes, dp_size):
    steps = 2 * (dp_size.bit_length() - 1) + 1
    out = [
        ("grad_recv%d" % i, pltpu.VMEM(((rows >> start) - rows // dp_size, cols), BF16))
        for i, (rows, cols, start) in enumerate(shapes)
    ]
    return out + [(N.grad_sems, pltpu.SemaphoreType.DMA((2, len(shapes), steps)))]


def grad_rows(rows, dp_size):
    unit = 16 * dp_size
    return -(-rows // unit) * unit


def placed(steps, slots):
    slots = list(slots)
    while len(slots) < len(steps):
        slots.append(slots[-1] + 2)
    return list(zip(slots, steps))


def forward_kernel(n, dp_size, chunks, sub, last, r):
    ex = Exchange(n, chunks, sub)
    if last:
        meet(ex.partners())
    else:
        halo = Halo(r.halo_sems, dp_size)
        meet(ex.partners() + halo.partners())
    sems = r.sems
    row = lambda i: r.vec[i : i + 1, :]
    full2 = None if last else r.a1

    def pre(c):
        def cols(j):
            y = matmul_nn(chunk_of(r.attended, c), r.proj, j)
            r.part1[:, c, :, j] = y.astype(BF16).reshape(n, sub, -1)

        column_loop(D, 256, cols)
        ex.rs_send(r.part1, r.recv1, sems.at[0], c, 0)

    def own1(c):
        r.need(N.stream)
        ex.rs_wait(r.part1, r.recv1, sems.at[0], c, ex.nbits - 1)
        u1 = ex.rs_total(r.part1, r.recv1, c) + row(0)
        r.u1[c] = u1
        middle = r.stream[c] + row(1) * u1
        r.stream[c] = middle
        hat, spread = normalised(middle)
        r.hat2[c] = hat
        r.sp2[c] = spread
        r.a2[ex.me, c] = (hat * row(2) + row(3)).astype(BF16)
        ex.ag_send(r.a2, sems.at[1], c, 0)
        r.store(N.u1, (c,))
        r.store(N.hat2, (c,))

    def mid(c):
        r.need(N.fc1, N.fc2)
        ex.ag_wait(r.a2, sems.at[1], c, ex.nbits - 1)

        def hidden(j):
            before = matmul_nn(chunk_of(r.a2, c), r.fc1, j) + r.fc1_bias[:, j]
            a, s = gelu_pair(before)
            r.act[:, c, :, j] = a.astype(BF16).reshape(n, sub, -1)
            r.slope[:, c, :, j] = s.astype(BF16).reshape(n, sub, -1)

        column_loop(r.fc1.shape[1], 256, hidden)

        def cols(j):
            y = matmul_nn(chunk_of(r.act, c), r.fc2, j)
            r.part2[:, c, :, j] = y.astype(BF16).reshape(n, sub, -1)

        column_loop(D, 256, cols)
        ex.rs_send(r.part2, r.recv2, sems.at[2], c, 0)
        for name in (N.a2, N.act, N.slope):
            r.store(name, (slice(None), c))

    def own2(c):
        ex.rs_wait(r.part2, r.recv2, sems.at[2], c, ex.nbits - 1)
        u2 = ex.rs_total(r.part2, r.recv2, c) + row(4)
        r.u2[c] = u2
        after = r.stream[c] + row(5) * u2
        r.after[c] = after.astype(r.after.dtype)
        r.store(N.after, (c,))
        r.store(N.u2, (c,))
        if not last:
            hat, spread = normalised(after)
            r.hat1[c] = hat
            r.sp1[c] = spread
            full2[ex.me, c] = (hat * row(6) + row(7)).astype(BF16)
            r.store(N.hat1, (c,))
            ex.ag_send(full2, sems.at[3], c, 0)

    def post(c):
        ex.ag_wait(full2, sems.at[3], c, ex.nbits - 1)
        r.need(N.qkv)
        x = chunk_of(full2, c)
        width = r.q.shape[3]
        for i, name in enumerate((N.q, N.k, N.v)):
            y = matmul_nn(x, r.qkv, slice(i * width, (i + 1) * width))
            if i != 1:
                y = y + r.qv_bias[i // 2 : i // 2 + 1, :]
            getattr(r, name)[:, c] = y.astype(BF16).reshape(n, sub, width)
            r.store(name, (slice(None), c))
            if i:
                for way in range(2):
                    halo.send(
                        getattr(r, name).at[:, c], r.targets[name + N._near].at[way, :, c], way, (i - 1) * chunks + c
                    )
        r.store(N.a1, (slice(None), c))

    run_stages(
        ex,
        [pre]
        + rs_stages(ex, r.part1, r.recv1, sems.at[0])
        + [own1]
        + ag_stages(ex, r.a2, sems.at[1])
        + [mid]
        + rs_stages(ex, r.part2, r.recv2, sems.at[2])
        + [own2]
        + ([] if last else ag_stages(ex, full2, sems.at[3]) + [post]),
    )
    if not last:
        for i, name in enumerate((N.k_near, N.v_near)):
            for c in range(chunks):
                for way in range(2):
                    halo.wait(r.targets[name].at[way, :, c], way, i * chunks + c)
        halo.drain()
    ex.drain()


def forward_block(n, dp_size, last, collective_id, attended, proj, fc1, fc2, fc1_bias, vec, stream, qkv=None, qv_bias=None):
    rows, width = attended.shape
    block, chunks, sub = sizes(rows, n)
    hidden = fc1.shape[1]
    split = lambda cols: (n, chunks, sub, cols)
    mine = (chunks, sub, D)
    ins = [
        (N.attended, attended.reshape(split(width)), False), (N.proj, proj, False), (N.stream, stream.reshape(mine), True),
        (N.fc1, fc1, True), (N.fc2, fc2, True), (N.fc1_bias, fc1_bias, False), (N.vec, vec, False),
    ]
    outs = [
        (N.u1, mine, F32, True), (N.hat2, mine, F32, True), (N.sp2, (chunks, sub, 1), F32, False),
        (N.u2, mine, F32, True), (N.a2, split(D), BF16, True), (N.act, split(hidden), BF16, True),
        (N.slope, split(hidden), BF16, True),
    ]
    scratch = comm_scratch(n, chunks, sub, "1") + comm_scratch(n, chunks, sub, "2")
    if last:
        outs += [(N.after, mine, BF16, True)]
    else:
        ins += [(N.qkv, qkv, True), (N.qv_bias, qv_bias, False)]
        outs += [(N.after, mine, F32, True), (N.hat1, mine, F32, True), (N.sp1, (chunks, sub, 1), F32, False)]
        outs += [(N.a1, split(D), BF16, True)] + [(k, split(width), BF16, True) for k in N.qkv]
        outs += [(k, (2,) + split(width), BF16, N.far) for k in (N.k_near, N.v_near)]
        scratch += [(N.halo_sems, pltpu.SemaphoreType.DMA((2, 2, 2 * chunks)))]
    return call(
        functools.partial(forward_kernel, n, dp_size, chunks, sub, last),
        N.forward_last if last else N.forward_block,
        collective_id,
        ins,
        outs,
        scratch + sem_scratch(4, n, chunks),
        2 * rows * D * (2 * hidden + 4 * width),
    )


def add_rows(ref, i, value):
    ref[i : i + 1, :] += jnp.sum(value, axis=0, keepdims=True)


def input_norm_own(ex, r, c, gain, sums):
    r.need(N.hat1, N.gm)
    ex.rs_wait(r.part, r.recv, r.sems.at[0], c, ex.nbits - 1)
    da1 = ex.rs_total(r.part, r.recv, c)
    add_rows(sums, 6, da1 * r.hat1[c])
    add_rows(sums, 7, da1)
    return r.gm[c] + norm_back(da1, r.hat1[c], r.sp1[c], gain)


def send_home(halo, r, chunks):
    cp = pltpu.make_async_copy(r.sources[N.dkv_in].at[:, 1], r.dkv, r.dkv_sem)
    cp.start()
    r.loads[N.dkv] = cp
    for c in range(chunks):
        for way in range(2):
            for i in range(2):
                src = r.sources[N.dkv_in].at[i, 2 - 2 * way, :, c]
                halo.send(src, near_part(r, way, i, c), way, 2 * c + i)


def near_part(r, way, i, c):
    width = r.dq.shape[3]
    return r.near.at[:, c, :, pl.ds((2 * way + i) * width, width)]


def input_grad_chunk(ex, halo, r, c):
    r.need(N.dq, N.dkv, N.qkv)
    width = r.dq.shape[3]
    for way in range(2):
        for i in range(2):
            halo.wait(near_part(r, way, i, c), way, 2 * c + i)
    r.dqkv[:, c, :, :width] = r.dq[:, c]
    for i in range(2):
        cols = slice((i + 1) * width, (i + 2) * width)

        for b in range(ex.n):
            r.total_kv[...] = r.dkv[i, b, c].astype(F32)
            for way in range(2):

                @pl.when(halo.has[1 - way])
                def _():
                    first = (2 * way + i) * width
                    r.total_kv[...] += r.near[b, c, :, first : first + width].astype(F32)

            total = r.total_kv[...]
            if i:
                r.dv_sum[...] += jnp.sum(total, axis=0, keepdims=True)
            r.dqkv[b, c, :, cols] = total.astype(BF16)

    def cols(j):
        y = matmul_nt(chunk_of(r.dqkv, c), r.qkv, j)
        r.part[:, c, :, j] = y.astype(BF16).reshape(ex.n, ex.sub, -1)

    column_loop(D, 256, cols)
    ex.rs_send(r.part, r.recv, r.sems.at[0], c, 0)


def backward_kernel(n, dp_size, chunks, sub, first, r):
    ex = Exchange(n, chunks, sub)
    sems, part, recv = r.sems, r.part, r.recv
    row = lambda i: r.vec[i : i + 1, :]
    if first:
        meet(ex.partners() + [{N.dp: core_partner()}])
    else:
        halo = Halo(r.halo_sems, dp_size)
        gs = GradSum(upper_arrays(r), r.grad_sems, dp_size)
        meet(ex.partners() + gs.partners() + halo.partners())
        r.near = r.e1
        send_home(halo, r, chunks)
        r.dv_sum[...] = jnp.zeros_like(r.dv_sum)
    first_arrays = [(x.shape[0], x, recv, None, 0, ()) for x, recv in ((r.g1, r.core_recv0), (r.g2, r.core_recv1))]
    first_sum = GradSum(first_arrays, r.core_sems, dp_size)
    r.sums[...] = jnp.zeros_like(r.sums)
    r.fc1b[...] = jnp.zeros_like(r.fc1b)
    width, hidden_size = r.proj.shape[0], r.fc1.shape[1]
    if r.g4.shape[0] > width:
        r.g4[width:, :] = jnp.zeros((r.g4.shape[0] - width, D), BF16)

    def pre(c):
        input_grad_chunk(ex, halo, r, c)

    def own0(c):
        r.need(N.u2)
        g = input_norm_own(ex, r, c, row(3), r.sums)
        add_rows(r.sums, 0, g * r.u2[c])
        add_rows(r.sums, 1, g * row(0))
        r.gm[c] = g
        r.full[ex.me, c] = (g * row(0)).astype(BF16)
        ex.ag_send(r.full, sems.at[1], c, 0)

    def mid(c):
        r.need(N.fc1, N.fc2, N.slope, N.full, N.u2, N.gm)
        if not first and c == 0:
            ex.drain()
        if first:
            g = r.gm[c]
            add_rows(r.sums, 0, g * r.u2[c])
            add_rows(r.sums, 1, g * row(0))
        else:
            ex.ag_wait(r.full, sems.at[1], c, ex.nbits - 1)

        def hidden(j):
            y = matmul_nt(chunk_of(r.full, c), r.fc2, j)
            w = y.shape[1]
            db = y * r.slope[:, c, :, j].astype(F32).reshape(n * sub, w)
            r.fc1b[:, j] += jnp.sum(db, axis=0, keepdims=True)
            r.slope[:, c, :, j] = db.astype(BF16).reshape(n, sub, w)

        column_loop(hidden_size, 256, hidden)

        def cols(j):
            y = matmul_nt(chunk_of(r.slope, c), r.fc1, j)
            part[:, c, :, j] = y.astype(BF16).reshape(n, sub, -1)

        column_loop(D, 256, cols)
        ex.rs_send(part, recv, sems.at[2], c, 0)

    def own1(c):
        r.need(N.hat2, N.u1)
        ex.rs_wait(part, recv, sems.at[2], c, ex.nbits - 1)
        da2 = ex.rs_total(part, recv, c)
        hat = r.hat2[c]
        add_rows(r.sums, 2, da2 * hat)
        add_rows(r.sums, 3, da2)
        gm = r.gm[c] + norm_back(da2, hat, r.sp2[c], row(1))
        r.gm[c] = gm
        add_rows(r.sums, 4, gm * r.u1[c])
        add_rows(r.sums, 5, gm * row(2))
        r.e1[ex.me, c] = (gm * row(2)).astype(BF16)
        ex.ag_send(r.e1, sems.at[3], c, 0)
        r.store(N.gm_out, (c,))

    def post(c):
        r.need(N.proj)
        ex.ag_wait(r.e1, sems.at[3], c, ex.nbits - 1)
        y = matmul_nt(chunk_of(r.e1, c), r.proj, slice(None))
        r.datt[:, c] = y.astype(BF16).reshape(n, sub, -1)
        r.store(N.datt, (slice(None), c))

    stages, extra = [], []
    if not first:
        made = [lambda: r.need(N.a1)] + grad_items(r.a1, r.dqkv, r.up3, 0)
        stages = [pre] + rs_stages(ex, part, recv, sems.at[0]) + [own0] + ag_stages(ex, r.full, sems.at[1])
        stages[1] = with_items(ex, stages[1], made)
        r.act = r.a1.at[:, :, :, pl.ds(0, hidden_size)]

        def fetch_act():
            cp = pltpu.make_async_copy(r.sources[N.act], r.act, r.act_sem)
            cp.start()
            r.loads[N.act] = cp

        extra += [(2 * chunks, fetch_act)]
        extra += [(3, lambda: r.need(N.keep1, N.got1, N.keep2, N.got2, N.up4))]
        extra += placed_sums(gs)
    gathers = ag_stages(ex, r.e1, sems.at[3])
    sums2 = rs_stages(ex, part, recv, sems.at[2])
    sums2[0] = with_items(ex, sums2[0], [lambda: r.need(N.act)] + grad_items(r.act, r.full, r.g1, 0))
    made = [lambda: r.need(N.a2)] + grad_items(r.a2, r.slope, r.g2, 0)
    stages += [mid] + sums2 + [with_items(ex, own1, made)] + gathers + [post]
    end = len(stages) * chunks
    behind = end - chunks * (1 + len(gathers))

    def part_of(a):
        first_sum.wait(a, 0)
        names = ((N.keep1, N.send1), (N.keep2, N.send2))[a]
        first_sum.split(a, getattr(r, names[0] + N._out), getattr(r, names[1] + N._out))
        for name in names:
            r.store(name + N._out)

    extra += [(behind - chunks, lambda: first_sum.send(0, 0)), (behind + 1, lambda: part_of(0))]
    extra += [(behind + 1, lambda: first_sum.send(1, 0)), (behind + 3, lambda: part_of(1))]
    run_stages(ex, stages, extra)
    r.need(N.attended)
    for item in grad_items(r.attended, r.e1, r.g4, 0):
        item()
    if not first:
        gs.drain()
        halo.drain()
    first_sum.drain()
    ex.drain()


def core_partner():
    me = lax.axis_index(N.dp)
    return me + 1 - 2 * bit_of(me, 0)


def tail_sums(gs):
    return (
        placed(gs.steps(0), (3, 6, 10, 13, 16))
        + placed(gs.steps(1), (4, 9, 13, 15.5, 17))
        + placed(gs.steps(2), (6, 7, 9, 12, 15, 16, 18))
        + placed(gs.steps(3), (3, 5, 7, 10, 12, 14, 17))
    )


def placed_sums(gs):
    return (
        placed(gs.steps(0), (3, 9, 15, 21, 25))
        + placed(gs.steps(1), (4, 10, 16, 22, 26))
        + placed(gs.steps(2), (6, 7, 11, 17, 20, 24, 27))
        + placed(gs.steps(3), (3, 5, 8, 12, 14, 18, 23))
    )


def upper_arrays(r):
    pieces = ((r.keep1, r.got1), (r.keep2, r.got2), (), ())
    return [
        (
            r.targets["up%d_out" % (i + 1)].shape[0],
            getattr(r, "up%d" % (i + 1)),
            getattr(r, "grad_recv%d" % i),
            r.targets["up%d_out" % (i + 1)],
            2 if x else 0,
            x,
        )
        for i, x in enumerate(pieces)
    ]


def upper_buffers(above, width, dp_size):
    shapes = [(4 * x.shape[0], x.shape[1]) for x in (above[N.keep1], above[N.keep2])]
    shapes += [(D, 3 * width), above[N.up4].shape]
    scratch = [(N.up1, pltpu.VMEM(above[N.keep1].shape, BF16)), (N.up2, pltpu.VMEM(above[N.keep2].shape, BF16))]
    scratch += [(N.up3, pltpu.VMEM(shapes[2], BF16))]
    scratch += grad_scratch([x + (start,) for x, start in zip(shapes, (2, 2, 0, 0))], dp_size)
    return scratch, [("up%d_out" % (i + 1), x, BF16, N.far) for i, x in enumerate(shapes)]


def home_buffers(n, chunks, sub, width):
    split = (n, chunks, sub)
    return [
        (N.dqkv, pltpu.VMEM(split + (3 * width,), BF16)),
        (N.total_kv, pltpu.VMEM((sub, width), F32)),
        (N.dkv, pltpu.VMEM((2,) + split + (width,), BF16)),
        (N.dkv_sem, pltpu.SemaphoreType.DMA),
        (N.halo_sems, pltpu.SemaphoreType.DMA((2, 2, 2 * chunks))),
    ]


def backward_block(n, dp_size, collective_id, source, above, fc1, fc2, proj, vec, saved):
    first = not above
    _, chunks, sub, hidden = saved[N.slope].shape
    width = proj.shape[0]
    split = lambda cols: (n, chunks, sub, cols)
    mine = (chunks, sub, D)
    ins = list(source.items()) + list(above.items()) + [(N.fc2, fc2), (N.slope, saved[N.slope]), (N.fc1, fc1)]
    ins += [(k, saved[k]) for k in (N.u2, N.act, N.a2, N.hat2, N.u1, N.sp2, N.attended)] + [(N.proj, proj), (N.vec, vec)]
    outs = [
        (N.datt, split(width), BF16, True), (N.gm_out, mine, F32, N.gm), (N.sums, (8, D), F32, False),
        (N.fc1b, (1, hidden), F32, False), (N.g4, (grad_rows(width, dp_size), D), BF16, False),
    ]
    for i, (rows, cols) in enumerate(((hidden, D), (D, hidden))):
        outs += [(k % (i + 1), (rows // 4, cols), BF16, True) for k in ("keep%d_out", "send%d_out")]
    scratch = comm_scratch(n, chunks, sub, "") + [(N.e1, pltpu.VMEM(split(D), BF16))] + sem_scratch(4, n, chunks)
    scratch += [(N.g1, pltpu.VMEM((hidden, D), BF16)), (N.g2, pltpu.VMEM((D, hidden), BF16))]
    scratch += [(N.core_recv0, pltpu.VMEM((hidden // 2, D), BF16)), (N.core_recv1, pltpu.VMEM((D // 2, hidden), BF16))]
    scratch += [(N.core_sems, pltpu.SemaphoreType.DMA((2, 2, 2 * (dp_size.bit_length() - 1))))]
    if not first:
        scratch += [(N.act_sem, pltpu.SemaphoreType.DMA)]
        scratch += [(N.full, pltpu.VMEM(split(D), BF16))] + home_buffers(n, chunks, sub, width)
        more, results = upper_buffers(above, width, dp_size)
        scratch += more
        outs += results + [(N.dv_sum, (1, width), F32, False)]
    return call(
        functools.partial(backward_kernel, n, dp_size, chunks, sub, first),
        N.backward_first if first else N.backward_block,
        collective_id,
        [(k, a, N.far if k == N.act and not first else lateness(k)) for k, a in ins],
        outs,
        scratch,
        2 * n * chunks * sub * D * (2 * hidden + 4 * width),
    )


def lateness(name):
    if name == N.dkv_in:
        return N.far
    return name not in (N.sp1, N.sp2, N.vec, N.base)


def tail_kernel(n, dp_size, chunks, sub, wide, r):
    ex = Exchange(n, chunks, sub)
    small = Total(r.bufs, r.small_recv, r.small_sems, dp_size, n, wide)
    gs = GradSum(upper_arrays(r), r.grad_sems, dp_size)
    halo = Halo(r.halo_sems, dp_size)
    meet(ex.partners() + gs.partners() + halo.partners())
    r.near = r.full
    send_home(halo, r, chunks)
    sems = r.sems
    r.dv_sum[...] = jnp.zeros_like(r.dv_sum)
    r.sums[...] = jnp.zeros_like(r.sums)

    def pre(c):
        input_grad_chunk(ex, halo, r, c)

    def own(c):
        g = input_norm_own(ex, r, c, r.vec[0:1, :], r.sums)
        r.full[ex.me, c] = g.astype(BF16)
        ex.ag_send(r.full, sems.at[1], c, 0)
        if c == chunks - 1:
            r.bufs[0] = r.base[...]
            r.bufs[0, 0:8, :] = r.sums[...]
            r.bufs[0, wide : wide + 1, : r.dv_sum.shape[1]] = r.dv_sum[...]
            small.start(0)

    def post(c):
        ex.ag_wait(r.full, sems.at[1], c, ex.nbits - 1)
        for b in range(n):
            r.out[b, c] = r.full[b, c].astype(F32)
        r.store(N.out, (slice(None), c))

    made = [lambda: r.need(N.a1)] + grad_items(r.a1, r.dqkv, r.up3, 0)
    stages = [pre] + rs_stages(ex, r.part, r.recv, sems.at[0]) + [own] + ag_stages(ex, r.full, sems.at[1]) + [post]
    stages[1] = with_items(ex, stages[1], made)
    after_own = chunks * (2 + ex.nbits - 1)
    extra = [(3, lambda: r.need(N.keep1, N.got1, N.keep2, N.got2, N.up4))]
    extra += tail_sums(gs)

    def spread(c, p):
        if p == 0:
            r.need(N.result)
            r.full3[ex.me, c] = r.result[c]
        else:
            ex.ag_wait(r.full3, sems.at[2], c, p - 1)
        if p < ex.nbits:
            ex.ag_send(r.full3, sems.at[2], c, p)
        else:
            for b in range(n):
                r.out2[b, c] = r.full3[b, c].astype(F32)
            r.store(N.out2, (slice(None), c))

    for p in range(ex.nbits + 1):
        slot = after_own + chunks * ex.nbits if p == ex.nbits else chunks * (1 + 2 * p)
        extra += [(slot + c, functools.partial(spread, c, p)) for c in range(chunks)]
    extra += [(after_own + 1 + i, functools.partial(small.step, i)) for i in range(len(small.axes))]
    run_stages(ex, stages, extra)
    halo.drain()
    r.total[...] = r.bufs[len(small.axes)]
    ex.drain()
    small.drain()
    gs.drain()


def backward_tail(n, dp_size, collective_id, wide, source, above, vec, base, result):
    _, chunks, sub, width = source[N.dq].shape
    split = lambda cols: (n, chunks, sub, cols)
    steps = (n * dp_size).bit_length() - 1
    ins = list(source.items()) + list(above.items()) + [(N.vec, vec), (N.base, base), (N.result, result)]
    more, results = upper_buffers(above, width, dp_size)
    outs = [(N.out, split(D), F32, True), (N.out2, split(D), F32, True), (N.total, base.shape, F32, False)] + results
    scratch = comm_scratch(n, chunks, sub, "") + sem_scratch(3, n, chunks) + home_buffers(n, chunks, sub, width)
    scratch += [(N.full3, pltpu.VMEM(split(D), BF16))]
    scratch += [(N.full, pltpu.VMEM(split(D), BF16)), (N.sums, pltpu.VMEM((8, D), F32)), (N.dv_sum, pltpu.VMEM((1, width), F32))]
    scratch += [(N.bufs, pltpu.VMEM((steps + 1,) + base.shape, F32)), (N.small_recv, pltpu.VMEM((steps,) + base.shape, F32))]
    scratch += [(N.small_sems, pltpu.SemaphoreType.DMA((2, steps)))] + more
    return call(
        functools.partial(tail_kernel, n, dp_size, chunks, sub, wide),
        N.backward_tail,
        collective_id,
        [(k, a, lateness(k)) for k, a in ins],
        outs,
        scratch,
        2 * n * chunks * sub * D * 3 * width,
    )


def id_features(ids_col, query_side):
    lane = lax.broadcasted_iota(jnp.int32, (ids_col.shape[0], HD), 1)
    bit = (ids_col >> (lane & 15)) & 1
    first = lane < 16
    second = (lane >= 16) & (lane < 32)
    inv = 1 - bit
    if query_side:
        v = jnp.where(first, bit, jnp.where(second, inv, 0)).astype(F32) * (-BIG)
    else:
        v = jnp.where(first, inv, jnp.where(second, bit, 0)).astype(F32)
    return v

def each_tile(KB, t_lo, t_hi, kn_ref, vn_ref, k_ref, v_ref, fn):
    per = k_ref.shape[0] // KB
    for segment in range(3):
        def one(t, carry, segment=segment):
            here = pl.ds(pl.multiple_of((t - segment * per) * KB, KB), KB)
            if segment == 1:
                fn(t, here, k_ref[here, :], v_ref[here, :])
            else:
                fn(t, here, kn_ref[segment // 2, here, :], vn_ref[segment // 2, here, :])
            return carry
        lax.fori_loop(jnp.maximum(t_lo, segment * per), jnp.minimum(t_hi, (segment + 1) * per), one, 0)

def fwd_kernel(HH, QB, KB, KT, nq, lo_ref, hi_ref, q_ref, kn_ref, vn_ref, k_ref, v_ref, idq_ref, idk_ref, o_ref, lse_ref, kaug, vt, qaug):
    t_lo = lo_ref[nq]
    t_hi = hi_ref[nq]
    def prep(t, here, kk, vv):
        r = pl.ds(pl.multiple_of(t * KT, KT), KT)
        feat = id_features(idk_ref[r, :], False).astype(BF16)
        for h in range(HH):
            kaug[h, r, :] = jnp.concatenate([kk[:, h * HD:(h + 1) * HD], feat], axis=1)
        vt[:, r] = vv.T
    each_tile(KT, t_lo, t_hi, kn_ref, vn_ref, k_ref, v_ref, prep)
    def qprep(t, _):
        r = pl.ds(pl.multiple_of(t * QB, QB), QB)
        feat = id_features(idq_ref[r, :], True).astype(BF16)
        qq = (q_ref[r, :] * BF16(0.125))
        for h in range(HH):
            qaug[h, :, r] = jnp.concatenate([qq[:, h * HD:(h + 1) * HD], feat], axis=1).T
        return 0
    lax.fori_loop(0, nq, qprep, 0)
    def qloop(qb, _):
        rq = pl.ds(pl.multiple_of(qb * QB, QB), QB)
        lo = lo_ref[qb]
        qts = [qaug[h, :, rq] for h in range(HH)]
        def kloop(t, c):
            r = pl.ds(pl.multiple_of(lo * KT + t * KB, KT), KB)
            new = []
            for h in range(HH):
                m, l, acc = c[h]
                s = jnp.dot(kaug[h, r, :], qts[h], preferred_element_type=F32)
                mn = jnp.maximum(m, jnp.max(s, axis=0, keepdims=True))
                p = jnp.exp(s - mn)
                al = jnp.exp(m - mn)
                l = l * al + jnp.sum(p, axis=0, keepdims=True)
                acc = acc * al + jnp.dot(vt[h * HD:(h + 1) * HD, r], p.astype(BF16), preferred_element_type=F32)
                new.append((mn, l, acc))
            return tuple(new)
        z = (jnp.full((1, QB), -3e38, F32), jnp.zeros((1, QB), F32), jnp.zeros((HD, QB), F32))
        c = lax.fori_loop(0, (hi_ref[qb] - lo) // (KB // KT), kloop, (z,) * HH)
        both = jnp.concatenate([c[h][2] / c[h][1] for h in range(HH)], axis=0)
        o_ref[rq, :] = both.T.astype(BF16)
        for h in range(HH):
            lse_ref[0, h:h + 1, rq] = c[h][0] + jnp.log(c[h][1])
        return 0
    lax.fori_loop(0, nq, qloop, 0)

def attend_fwd(q, kn, vn, k, v, idq, idk, lo, hi, HH, QB, KB, KT):
    n, cols = q.shape
    w = 3 * n
    HH = min(HH, cols // HD)
    wide = HH * HD
    near = pl.BlockSpec((2, n, wide), lambda g, *_: (0, 0, g))
    pairs = cols // wide
    nq = n // QB
    return pl.pallas_call(
        functools.partial(fwd_kernel, HH, QB, KB, KT, nq),
        grid_spec=pltpu.PrefetchScalarGridSpec(
            num_scalar_prefetch=2, grid=(pairs,),
            in_specs=[pl.BlockSpec((n, wide), lambda g, *_: (0, g)), near, near, pl.BlockSpec((n, wide), lambda g, *_: (0, g)), pl.BlockSpec((n, wide), lambda g, *_: (0, g)),
                      pl.BlockSpec((n, 1), lambda g, *_: (0, 0)), pl.BlockSpec((w, 1), lambda g, *_: (0, 0))],
            out_specs=[pl.BlockSpec((n, wide), lambda g, *_: (0, g)), pl.BlockSpec((1, HH, n), lambda g, *_: (g, 0, 0))],
            scratch_shapes=[pltpu.VMEM((HH, w, 128), BF16), pltpu.VMEM((wide, w), BF16), pltpu.VMEM((HH, 128, n), BF16)]),
        out_shape=[jax.ShapeDtypeStruct((n, cols), BF16), jax.ShapeDtypeStruct((pairs, HH, n), F32)],
        compiler_params=pltpu.CompilerParams(vmem_limit_bytes=VMEM_LIMIT),
        cost_estimate=pl.CostEstimate(flops=5 * 10**10, bytes_accessed=10**8, transcendentals=0),
        name=N.attend_fwd,
    )(lo, hi, q, kn, vn, k, v, idq, idk)

def bwd_kernel(HH, QB, KB, KT, nq, lo_ref, hi_ref, q_ref, kn_ref, vn_ref, k_ref, v_ref, idq_ref, idk_ref, o_ref, g_ref, lse_ref, dq_ref, dkv_ref, qsum_ref, kaug, vaug, kt, qaug, gaug, acc):
    w = 3 * k_ref.shape[0]
    t_lo = lo_ref[nq]
    t_hi = hi_ref[nq]
    wide = HH * HD
    lane = lax.broadcasted_iota(jnp.int32, (KT, HD), 1)
    three = ((lane >= 32) & (lane < 35))
    def zero(t, _):
        r = pl.ds(pl.multiple_of(t * KT, KT), KT)
        for i in range(2):
            dkv_ref[i, r, :] = jnp.zeros((KT, wide), BF16)
        return 0
    lax.fori_loop(0, w // KT, zero, 0)
    def prep(t, here, kk, vv):
        r = pl.ds(pl.multiple_of(t * KT, KT), KT)
        feat = jnp.where(three, 1.0, id_features(idk_ref[r, :], False)).astype(BF16)
        ones = jnp.where(three, 1.0, 0.0).astype(BF16)
        for h in range(HH):
            kaug[h, r, :] = jnp.concatenate([kk[:, h * HD:(h + 1) * HD], feat], axis=1)
            vaug[h, r, :] = jnp.concatenate([vv[:, h * HD:(h + 1) * HD], ones], axis=1)
            acc[h, r, :] = jnp.zeros((KT, 128), F32)
        kt[:, r] = kk.T
    each_tile(KT, t_lo, t_hi, kn_ref, vn_ref, k_ref, v_ref, prep)
    qsum_ref[...] = jnp.zeros((1, wide), F32)
    def pieces(x):
        a = x.astype(BF16).astype(F32)
        b = (x - a).astype(BF16).astype(F32)
        return a, b, x - a - b
    def qprep(t, _):
        r = pl.ds(pl.multiple_of(t * QB, QB), QB)
        fid = id_features(idq_ref[r, :], True).T
        row = lax.broadcasted_iota(jnp.int32, (HD, QB), 0)
        qt = (q_ref[r, :] * BF16(0.125)).T
        gg = g_ref[r, :]
        gt = gg.T
        prod = (gg.astype(F32) * o_ref[r, :].astype(F32)).T
        for h in range(HH):
            a, b, c = pieces(-lse_ref[0, h:h + 1, r])
            f = jnp.where(row == 32, a, jnp.where(row == 33, b, jnp.where(row == 34, c, fid)))
            qaug[h, :, r] = jnp.concatenate([qt[h * HD:(h + 1) * HD, :], f.astype(BF16)], axis=0)
            d = -jnp.sum(prod[h * HD:(h + 1) * HD, :], axis=0, keepdims=True)
            a, b, c = pieces(d)
            f = jnp.where(row == 32, a, jnp.where(row == 33, b, jnp.where(row == 34, c, 0.0)))
            gaug[h, :, r] = jnp.concatenate([gt[h * HD:(h + 1) * HD, :], f.astype(BF16)], axis=0)
        return 0
    lax.fori_loop(0, nq, qprep, 0)
    def qloop(qb, _):
        rq = pl.ds(pl.multiple_of(qb * QB, QB), QB)
        qq = q_ref[rq, :] * BF16(0.125)
        gg = g_ref[rq, :]
        zz = jnp.zeros((QB, HD), BF16)
        lo = lo_ref[qb]
        qts = [qaug[h, :, rq] for h in range(HH)]
        gts = [gaug[h, :, rq] for h in range(HH)]
        rhs = [jnp.concatenate([jnp.concatenate([qq[:, h * HD:(h + 1) * HD], zz], axis=1), jnp.concatenate([zz, gg[:, h * HD:(h + 1) * HD]], axis=1)], axis=0) for h in range(HH)]
        def kloop(t, c):
            r = pl.ds(pl.multiple_of(lo * KT + t * KB, KT), KB)
            new = []
            for h in range(HH):
                s = jnp.dot(kaug[h, r, :], qts[h], preferred_element_type=F32)
                dp = jnp.dot(vaug[h, r, :], gts[h], preferred_element_type=F32)
                p = jnp.exp(s)
                ds = (p * dp).astype(BF16)
                both = jnp.concatenate([ds, p.astype(BF16)], axis=1)
                acc[h, r, :] += jnp.dot(both, rhs[h], preferred_element_type=F32)
                new.append(c[h] + jnp.dot(kt[h * HD:(h + 1) * HD, r], ds, preferred_element_type=F32))
            return tuple(new)
        z = jnp.zeros((HD, QB), F32)
        c = lax.fori_loop(0, (hi_ref[qb] - lo) // (KB // KT), kloop, (z,) * HH)
        dq = (jnp.concatenate(c, axis=0) * 0.125).T
        qsum_ref[...] += jnp.sum(dq, axis=0, keepdims=True)
        dq_ref[rq, :] = dq.astype(BF16)
        return 0
    lax.fori_loop(0, nq, qloop, 0)
    def fin(t, _):
        r = pl.ds(pl.multiple_of(t * KT, KT), KT)
        sums = [acc[h, r, :] for h in range(HH)]
        for i in range(2):
            dkv_ref[i, r, :] = jnp.concatenate([x[:, i * HD:(i + 1) * HD] for x in sums], axis=1).astype(BF16)
        return 0
    lax.fori_loop(t_lo, t_hi, fin, 0)

def attend_bwd(q, kn, vn, k, v, idq, idk, lo, hi, out, grad, lse, HH, QB, KB, KT):
    n, cols = q.shape
    w = 3 * n
    HH = min(HH, cols // HD)
    wide = HH * HD
    near = pl.BlockSpec((2, n, wide), lambda g, *_: (0, 0, g))
    pairs = cols // wide
    nq = n // QB
    rows = lambda m: pl.BlockSpec((m, wide), lambda g, *_: (0, g))
    return pl.pallas_call(
        functools.partial(bwd_kernel, HH, QB, KB, KT, nq),
        grid_spec=pltpu.PrefetchScalarGridSpec(
            num_scalar_prefetch=2, grid=(pairs,),
            in_specs=[rows(n), near, near, rows(n), rows(n), pl.BlockSpec((n, 1), lambda g, *_: (0, 0)), pl.BlockSpec((w, 1), lambda g, *_: (0, 0)), rows(n), rows(n), pl.BlockSpec((1, HH, n), lambda g, *_: (g, 0, 0))],
            out_specs=[rows(n), pl.BlockSpec((2, w, wide), lambda g, *_: (0, 0, g)), pl.BlockSpec((1, wide), lambda g, *_: (0, g))],
            scratch_shapes=[pltpu.VMEM((HH, w, 128), BF16), pltpu.VMEM((HH, w, 128), BF16), pltpu.VMEM((wide, w), BF16), pltpu.VMEM((HH, 128, n), BF16), pltpu.VMEM((HH, 128, n), BF16), pltpu.VMEM((HH, w, 128), F32)]),
        out_shape=[jax.ShapeDtypeStruct((n, cols), BF16), jax.ShapeDtypeStruct((2, w, cols), BF16), jax.ShapeDtypeStruct((1, cols), F32)],
        compiler_params=pltpu.CompilerParams(vmem_limit_bytes=VMEM_LIMIT),
        cost_estimate=pl.CostEstimate(flops=5 * 10**10, bytes_accessed=10**8, transcendentals=0),
        name=N.attend_bwd,
    )(lo, hi, q, kn, vn, k, v, idq, idk, out, grad, lse)

def reach(ids_win, n, QB, KB, KT, least, most):
    w = ids_win.shape[0]
    own = ids_win[n:2 * n].reshape(n // QB, QB)
    lo = (jnp.argmax(ids_win[None, :] == own[:, :1], axis=1) // KT).astype(jnp.int32)
    hi = ((w - jnp.argmax(ids_win[::-1][None, :] == own[:, -1:], axis=1) + KT - 1) // KT).astype(jnp.int32)
    need = -(lo - hi) % (KB // KT)
    need = jnp.where(need > 0, KB // KT - need, 0)
    up = jnp.minimum(most - hi, need)
    lo, hi = lo - (need - up), hi + up
    return jnp.append(lo, jnp.min(lo)), jnp.append(hi, jnp.max(hi))


def neighbours(axis):
    peers = lax.axis_size(axis)
    up = [(i, i + 1) for i in range(peers - 1)]
    return up, [(j, i) for i, j in up]


def with_halo(array):
    up, down = neighbours(N.dp)
    return jnp.concatenate(
        [lax.ppermute(array, N.dp, up), array, lax.ppermute(array, N.dp, down)], axis=0
    )


def near(array):
    up, down = neighbours(N.dp)
    return jnp.stack([lax.ppermute(array, N.dp, up), lax.ppermute(array, N.dp, down)])


def own_part(array, n):
    block, chunks, sub = sizes(array.shape[0], n)
    first = lax.axis_index(N.tensor) * block
    return lax.dynamic_slice_in_dim(array, first, block, 0).reshape(chunks, sub, array.shape[1])


def body(
    tokens, image_ids, cotangent, ln1_gain, ln1_bias, qkv_weight, qv_bias, proj_weight, proj_bias, scale_attn,
    ln2_gain, ln2_bias, fc1_weight, fc1_bias, fc2_weight, fc2_bias, scale_mlp,
):
    n = lax.axis_size(N.tensor)
    rows = tokens.shape[0]
    width, hidden = qkv_weight.shape[3], fc1_weight.shape[2]
    _, chunks, sub = sizes(rows, n)
    split = (n, chunks, sub)
    qkv2 = qkv_weight.reshape(LAYERS, D, 3 * width)
    ids_win = with_halo(image_ids + 1)
    per = rows // TILES[3]
    place, places = lax.axis_index(N.dp), lax.axis_size(N.dp)
    least, most = jnp.where(place == 0, per, 0), jnp.where(place == places - 1, 2 * per, 3 * per)
    lo, hi = reach(ids_win, rows, *TILES[1:], least, most)
    idq, idk = ids_win[rows : 2 * rows, None], ids_win[:, None]

    stream = tokens.astype(F32)
    hat, _ = normalised(stream)
    a1 = (hat * ln1_gain[0] + ln1_bias[0]).astype(BF16)
    first = jnp.dot(a1, qkv2[0], preferred_element_type=F32)
    q = (first[:, :width] + qv_bias[0, 0]).astype(BF16)
    k = first[:, width : 2 * width].astype(BF16)
    v = (first[:, 2 * width :] + qv_bias[0, 1]).astype(BF16)
    a1 = a1.reshape(split + (D,))
    own = own_part(tokens, n).astype(F32)
    hat1, sp1 = normalised(own)

    saved = []
    dp_size = lax.axis_size(N.dp)
    kn, vn = near(k), near(v)
    for level in range(LAYERS):
        kv = (kn, vn, k, v)
        attended, lse = attend_fwd(q, *kv, idq, idk, lo, hi, *TILES)
        last = level == LAYERS - 1
        after = 0 if last else level + 1
        vec = jnp.stack(
            [
                proj_bias[level], scale_attn[level], ln2_gain[level], ln2_bias[level], fc2_bias[level],
                scale_mlp[level], ln1_gain[after], ln1_bias[after],
            ]
        )
        extra = () if last else (qkv2[level + 1], qv_bias[level + 1])
        made = forward_block(
            n, dp_size, last, level, attended, proj_weight[level], fc1_weight[level], fc2_weight[level], fc1_bias[level][None],
            vec, own, *extra,
        )
        keep = {name: made[name] for name in (N.u1, N.hat2, N.sp2, N.u2, N.a2, N.act, N.slope)}
        keep[N.attended] = attended.reshape(split + (width,))
        saved.append((q, kv, attended, lse, a1, hat1, sp1, keep))
        if last:
            result = made[N.after]
        else:
            own, hat1, sp1, a1 = (made[name] for name in (N.after, N.hat1, N.sp1, N.a1))
            q, k, v = (made[name].reshape(rows, width) for name in N.qkv)
            kn, vn = (made[name].reshape(2, rows, width) for name in (N.k_near, N.v_near))

    cot = cotangent.astype(F32)
    source = {
        N.full: (cot * scale_mlp[LAYERS - 1]).astype(BF16).reshape(split + (D,)),
        N.gm: own_part(cotangent, n).astype(F32),
    }
    above, grads = {}, [None] * LAYERS
    sums, narrow, dv_sums = [None] * (LAYERS + 1), [None] * LAYERS, [None] * LAYERS
    up, down = neighbours(N.dp)
    for level in reversed(range(LAYERS)):
        q, kv, attended, lse, a1, hat1, sp1, keep = saved[level]
        upper = min(level + 1, LAYERS - 1)
        vec = jnp.stack([scale_mlp[level], ln2_gain[level], scale_attn[level], ln1_gain[upper]])
        outs = backward_block(
            n, dp_size, LAYERS + level, source, above, fc1_weight[level], fc2_weight[level], proj_weight[level], vec, keep,
        )
        datt, fc1b, sums[level + 1] = outs[N.datt], outs[N.fc1b], outs[N.sums]
        if above:
            grads[level + 1] = [outs["up%d_out" % (i + 1)] for i in range(4)]
            dv_sums[level + 1] = outs[N.dv_sum][0]
        flip = [(i, i ^ 2) for i in range(dp_size)]
        above = {N.up4: outs[N.g4]}
        for name in "12":
            above[N.keep + name] = outs[N.keep + name + N._out]
            above[N.got + name] = lax.ppermute(outs[N.send + name + N._out], N.dp, flip)
        dq, dkv, q_sum = attend_bwd(
            q, *kv, idq, idk, lo, hi, attended, datt.reshape(rows, width), lse, *TILES
        )
        narrow[level] = (fc1b[0], q_sum[0])
        dkv = dkv.reshape((2, 3) + split + (width,))
        source = {
            N.dkv_in: dkv, N.dq: dq.reshape(split + (width,)), N.qkv: qkv2[level], N.hat1: hat1,
            N.gm: outs[N.gm_out], N.a1: a1, N.sp1: sp1,
        }
    pad = jnp.zeros((D - width,), F32)
    flat = jnp.concatenate(
        [jnp.zeros((D,), F32)]
        + [x for i in range(1, LAYERS) for x in (dv_sums[i], pad)]
        + [x for i in range(LAYERS) for x in narrow[i]]
    )
    own_rows = -(-flat.shape[0] // (8 * D)) * 8
    flat = jnp.pad(flat, (0, own_rows * D - flat.shape[0])).reshape(own_rows, D)
    wide = 8 * (LAYERS + 1)
    base = jnp.concatenate([jnp.zeros((8, D), F32)] + sums[1:] + [flat])
    tail = backward_tail(n, dp_size, 2 * LAYERS, wide, source, above, ln1_gain[:1], base, result)
    grads[0] = [tail["up%d_out" % (i + 1)] for i in range(4)]
    grad_tokens, total = tail[N.out], tail[N.total]
    dv_total = total[wide : wide + LAYERS, :width]
    flat = total[wide + LAYERS :].reshape(-1)[: LAYERS * (hidden + width)].reshape(LAYERS, hidden + width)
    fc1b_total, qv_total = flat[:, :hidden], jnp.stack([flat[:, hidden:], dv_total], axis=1)
    stacked = lambda parts: jnp.stack([x.astype(F32) for x in parts])
    big = [
        stacked([x[2] for x in grads]),
        stacked([x[3][:width] for x in grads]),
        stacked([x[1] for x in grads]),
        stacked([x[0] for x in grads]),
    ]
    total = total[:wide].reshape(LAYERS + 1, 8, D)
    upper, lower = total[1:], total[:-1]
    return (
        tail[N.out2].reshape(rows, D),
        grad_tokens.reshape(rows, D),
        lower[:, 6],
        lower[:, 7],
        big[0].reshape(LAYERS, D, 3, width),
        qv_total,
        big[1],
        upper[:, 5],
        upper[:, 4],
        upper[:, 2],
        upper[:, 3],
        big[2],
        fc1b_total,
        big[3],
        upper[:, 1],
        upper[:, 0],
    )


def solution(mesh):
    cols, stack_rows = P(None, None, N.tensor), P(None, N.tensor, None)
    qkv = P(None, None, None, N.tensor)
    return jax.shard_map(
        body,
        mesh=mesh,
        in_specs=(
            P(N.dp, None), P(N.dp), P(N.dp, None), P(), P(), qkv, cols, stack_rows, P(), P(), P(), P(), cols,
            P(None, N.tensor), stack_rows, P(), P(),
        ),
        out_specs=(
            P(N.dp, None), P(N.dp, None), P(), P(), qkv, cols, stack_rows, P(), P(), P(), P(), cols,
            P(None, N.tensor), stack_rows, P(), P(),
        ),
        check_vma=False,
    )
```

time: 1280 us -> 874 us (0.68)
  waiting for transfers between devices: 352 us -> 1.12 us
  Pallas kernels: 650 us -> 741 us
  starting transfers between devices: 75.7 us -> 19.6 us
  matrix products: 46 us -> 2.66 us
  blocking collectives: 21.9 us -> 0 us
  between operations: 15.2 us -> 1.44 us
  other arithmetic: 53.8 us -> 40.8 us
    psum x2 -> x0, waiting for transfers between devices: 347 us -> none  [the longest x1 257 us: body(): lax.psum((weight_grad(a1, dqkv), weight_grad(attended.reshape(split + (wi...]
    pallas_call x9, Pallas kernels: 650 us -> 741 us  [the longest x5 561 us: call(): pl.pallas_call(entry, out_shape=[jax.ShapeDtypeStruct(shape, dtype) for _...]
    ppermute x18 -> x10, starting transfers between devices: 75.6 us -> 19.6 us  [the longest x2 6.41 us: near(): lax.ppermute(array, N.dp, up)]
    dot_general x8 -> x0, matrix products: 41.5 us -> none  [weight_grad(): lax.dot_general(left.reshape(rows, -1), right.reshape(rows, -1), (((0,),...]
    psum x1 -> x0, blocking collectives: 21.9 us -> none  [body(): lax.psum((jnp.stack([narrow[i][0] for i in range(LAYERS)]), jnp.stack([na...]
    concatenate x7 -> x3, other arithmetic: 15.9 us -> 2.62 us  [the longest x1 1.88 us: reach(): return (jnp.append(lo, jnp.min(lo)), jnp.append(hi, jnp.max(hi)))]
    unnamed x96 -> x98, local copies, waits for them, and re-layouts: 19.2 us -> 29 us
  transfers between devices with their start and end apart: 20 -> 10, of which waited for: 6 -> 1; matrix products, arithmetic and copies ran while one was open for 8% -> 6% of each run, Pallas kernels for 0% -> 12%
where the time goes in v2:
time: 874 us; the launch traced here: 865 us
  Pallas kernels  741 us (85%)
  local copies, waits for them, and re-layouts  58.2 us (7%)
  other arithmetic  40.8 us (5%)
  starting transfers between devices  19.6 us (2%)
    pallas_call x5, Pallas kernels, call(): pl.pallas_call(entry, out_shape=[jax.ShapeDtypeStruct(shape, dtype) for _...  561 us
    pallas_call x2, Pallas kernels, attend_bwd(): pl.pallas_call(functools.partial(bwd_kernel, HH, QB, KB, KT, nq), grid_sp...  101 us
    pallas_call x2, Pallas kernels, attend_fwd(): pl.pallas_call(functools.partial(fwd_kernel, HH, QB, KB, KT, nq), grid_sp...  78.8 us
    unnamed x98, local copies, waits for them, and re-layouts  29 us
  transfers between devices with their start and end apart: 10, of which 1 were waited for; matrix products, arithmetic and copies ran while one was open for 6% of the time, Pallas kernels for 12%

profile of v2, /device:TPU:17, one launch (start us, length us, event | category | flops | bytes accessed | tf_op | source)
XLA Modules:
  0.0 864.5 jit_solution(4088040368717171611)
XLA Ops:
  0.7 0.8 broadcast_add_fusion
  1.5 3.9 collective-permute-start
  5.4 1.9 collective-permute-start.1
  7.3 2.4 convert_reduce_fusion
  9.7 1.0 fusion.2
  10.7 0.9 copy-done.9
  11.6 1.9 fusion.16
  13.5 2.6 copy.124
  16.2 1.5 fusion.5
  17.7 2.7 fusion.29
  20.3 1.5 fusion.6
  21.8 2.5 collective-permute-start.5
  24.3 3.1 collective-permute-start.4
  27.4 1.0 slice.266.k_ref
  28.4 3.3 collective-permute-start.2
  32.9 3.1 slice_bitcast_fusion.4
  36.6 0.9 constant_dynamic-slice_fusion
  37.6 2.6 multiply_convert_fusion
  40.6 1.1 copy-done.7
  41.7 3.4 slice_bitcast_fusion
  45.1 1.4 subtract_multiply_fusion.refs_3_
  47.7 1.2 broadcast_in_dim.28.idq_ref
  48.9 1.6 copy.110.refs_2_
  50.5 0.9 copy.125
  51.4 1.6 copy.102.refs_7_.refs_2_
  53.0 1.3 convert.18.refs_1_
  54.3 0.8 copy.111.refs_6_
  55.7 0.7 stack.99.refs_6_
  57.0 1.9 collective-permute-start.3
  59.0 0.7 iota_reduce_fusion.1
  59.8 0.7 iota_reduce_fusion
  60.5 3.1 broadcast_in_dim.29.idk_ref
  64.9 1.9 pad_add_fusion.1
  66.7 2.7 pad_maximum_fusion.1.vn_ref
  69.4 1.1 collective-permute-done.3
  70.5 2.5 pad_maximum_fusion.kn_ref
  73.0 39.5 %attend_fwd.2 = (bf16[1536,256]{1,0:T(8,128)(2,1)}, f32[1,4,1536]{2,1,0:T(4,128)}) custom-call(s32[4]{0:T(128)} %get-tuple-element.267.lo_ref, s32[4]{0:T(128)} %get-tuple-element.268.hi_ref, bf16[1536,256]{1,0:T(8,128)(2,1)} %get-tuple-element.222.q_ref, bf16[2,1536,256]{2,1,0:T(8,128)(2,1)} %pad_maximum_fusion.kn_ref, ...), custom_call_target="tpu_custom_call" | custom-call | flops 49999998976 | bytes 100000000 | tf_op jit(solution)/shard_map/attend_fwd/pallas_call | solution.py:1266
  112.5 119.2 %forward_block.1 = (f32[3,128,1024]{2,1,0:T(8,128)}, f32[3,128,1024]{2,1,0:T(8,128)}, f32[3,128,1]{2,1,0:T(8,128)}, f32[3,128,1024]{2,1,0:T(8,128)}, bf16[4,3,12...) custom-call(bf16[4,3,128,256]{3,2,1,0:T(8,128)(2,1)} %bitcast.124, ...), custom_call_target="tpu_custom_call" | custom-call | flops 9663676416 | bytes 100000000 | tf_op jit(solution)/shard_map/forward_block/pallas_call | solution.py:431
  231.8 39.3 %attend_fwd.3 = (bf16[1536,256]{1,0:T(8,128)(2,1)}, f32[1,4,1536]{2,1,0:T(4,128)}) custom-call(s32[4]{0:T(128)} %get-tuple-element.267.lo_ref, s32[4]{0:T(128)} %get-tuple-element.268.hi_ref, bf16[1536,256]{1,0:T(8,128)(2,1)} %bitcast.152, bf16[2,1536,256]{2,1,0:T(8,128)(2,1)} %bitcast.148, bf16[2,1536,256]{2,1,0:T(8,128)(2,1)} %bitcast.150, ...), custom_call_target="tpu_custom_call" | custom-call | flops 49999998976 | bytes 100000000 | tf_op jit(solution)/shard_map/attend_fwd/pallas_call | solution.py:1266
  271.0 82.9 %forward_last.1 = (f32[3,128,1024]{2,1,0:T(8,128)}, f32[3,128,1024]{2,1,0:T(8,128)}, f32[3,128,1]{2,1,0:T(8,128)}, f32[3,128,1024]{2,1,0:T(8,128)}, bf16[4,3,128...) custom-call(bf16[4,3,128,256]{3,2,1,0:T(8,128)(2,1)} %bitcast.158, ...), custom_call_target="tpu_custom_call" | custom-call | flops 9663676416 | bytes 100000000 | tf_op jit(solution)/shard_map/forward_last/pallas_call | solution.py:431
  354.0 68.5 %backward_first.1 = (bf16[4,3,128,256]{3,2,1,0:T(8,128)(2,1)}, f32[3,128,1024]{2,1,0:T(8,128)}, f32[8,1024]{1,0:T(8,128)}, f32[1,1024]{1,0:T(1,128)}, bf16[256,1...) custom-call(bf16[4,3,128,1024]{3,2,1,0:T(8,128)(2,1)} %bitcast.117, ...), custom_call_target="tpu_custom_call" | custom-call | flops 9663676416 | bytes 100000000 | tf_op jit(solution)/shard_map/backward_first/pallas_call | solution.py:431
  422.5 1.5 collective-permute-start.7
  424.0 50.1 %attend_bwd.2 = (bf16[1536,256]{1,0:T(8,128)(2,1)}, bf16[2,4608,256]{2,1,0:T(8,128)(2,1)}, f32[1,256]{1,0:T(1,128)}) custom-call(s32[4]{0:T(128)} %get-tuple-element.267.lo_ref, s32[4]{0:T(128)} %get-tuple-element.268.hi_ref, bf16[1536,256]{1,0:T(8,128)(2,1)} %bitcast.153, bf16[2,1536,256]{2,1,0:T(8,128)(2,1)} %bitcast.149, bf16[2,1536,256]{2,1,0:T(8,128)(2,1)} %bitcast.151, ...), custom_call_target="tpu_custom_call" | custom-call | flops 49999998976 | bytes 100000000 | tf_op jit(solution)/shard_map/attend_bwd/pallas_call | solution.py:1371
  474.1 0.8 copy-done.14
  475.1 153.4 %backward_block.1 = (bf16[4,3,128,256]{3,2,1,0:T(8,128)(2,1)}, f32[3,128,1024]{2,1,0:T(8,128)}, f32[8,1024]{1,0:T(8,128)}, f32[1,1024]{1,0:T(1,128)}, bf16[256,1...) custom-call(bf16[2,3,4,3,128,256]{5,4,3,2,1,0:T(8,128)(2,1)} %bitcas, ...), custom_call_target="tpu_custom_call" | custom-call | flops 9663676416 | bytes 100000000 | tf_op jit(solution)/shard_map/backward_block/pallas_call | solution.py:431
  629.2 1.5 collective-permute-start.9
  630.7 0.7 constant_dynamic-update-slice_fusion.3
  631.3 50.5 %attend_bwd.3 = (bf16[1536,256]{1,0:T(8,128)(2,1)}, bf16[2,4608,256]{2,1,0:T(8,128)(2,1)}, f32[1,256]{1,0:T(1,128)}) custom-call(s32[4]{0:T(128)} %get-tuple-element.267.lo_ref, s32[4]{0:T(128)} %get-tuple-element.268.hi_ref, bf16[1536,256]{1,0:T(8,128)(2,1)} %get-tuple-element.222.q_ref, bf16[2,1536,256]{2,1,0:T(8,128)(2,1)} %pad_maximum_fusion.kn_ref, ...), custom_call_target="tpu_custom_call" | custom-call | flops 49999998976 | bytes 100000000 | tf_op jit(solution)/shard_map/attend_bwd/pallas_call | solution.py:1371
  681.8 0.7 constant_dynamic-update-slice_fusion.2
  682.6 1.7 copy.115
  684.4 0.7 pad_maximum_fusion.2.refs_13_
  685.1 137.3 %backward_tail.1 = (f32[4,3,128,1024]{3,2,1,0:T(8,128)}, f32[4,3,128,1024]{3,2,1,0:T(8,128)}, f32[32,1024]{1,0:T(8,128)}, bf16[1024,1024]{1,0:T(8,128)(2,1)}, bf...) custom-call(bf16[2,3,4,3,128,256]{5,4,3,2,1,0:T(8,128)(2,1)} %bitcast.114, ...), custom_call_target="tpu_custom_call" | custom-call | flops 2415919104 | bytes 100000000 | tf_op jit(solution)/shard_map/backward_tail/pallas_call | solution.py:431
  822.4 0.8 slice.217
  823.2 0.7 slice_bitcast_fusion.9
  823.9 0.9 slice_bitcast_fusion.6
  826.1 2.6 copy.114
  828.6 4.5 maximum_convert_fusion.2
  833.2 6.7 copy.122
  844.8 5.7 maximum_convert_fusion.1
  850.5 4.8 maximum_convert_fusion
  855.3 1.5 maximum_convert_fusion.3
  857.2 3.2 copy.158
  860.4 1.2 slice-done.1
  861.6 2.7 copy.159
  (135 shorter events, 13.7 us)
Async XLA Ops:
  0.6 9.1 %copy-start = (bf16[1536,1024]{1,0:T(8,128)(2,1)S(1)}, bf16[1536,1024]{1,0:T(8,128)(2,1)}, u32[]{:S(2)}) copy-start(bf16[1536,1024]{1,0:T(8,128)(2,1)} %param.17) | copy-start | bytes 9437188
  1.5 55.5 %collective-permute-start = (s32[1536]{0:T(1024)S(1)}, s32[1536]{0:T(1024)S(1)}, u32[]{:S(2)}, u32[]{:S(2)}) collective-permute-start(s32[1536]{0:T(1024)S(1)} %broadcast_add_fusion), channel_id=1, source_target_pairs={{0,4},{4,8},{8,12},{12,16},{16,20},{20,24},{24,28},{1,5},{5,9},{9,... | collective-permute-start | bytes 18440 | tf_op jit(solution)/shard_map/ppermute | solution.py:1405
  5.4 53.5 %collective-permute-start.1 = (s32[1536]{0:T(1024)S(1)}, s32[1536]{0:T(1024)S(1)}, u32[]{:S(2)}, u32[]{:S(2)}) collective-permute-start(s32[1536]{0:T(1024)S(1)} %broadcast_add_fusion), channel_id=1, source_target_pairs={{4,0},{8,4},{12,8},{16,12},{20,16},{24,20},{28,24},{5,1},{9,5},{13... | collective-permute-start | bytes 18440 | tf_op jit(solution)/shard_map/ppermute | solution.py:1405
  9.7 1.9 copy-start.9
  13.5 2.6 copy-start.31
  13.5 2.6 copy-start.23
  13.5 2.6 copy-start.24
  16.1 39.5 %copy-start.18 = (f32[1,1024]{1,0:T(1,128)}, f32[1,1024]{1,0:T(1,128)S(1)}, u32[]{:S(2)}) copy-start(f32[1,1024]{1,0:T(1,128)S(1)} %get-tuple-element.275.refs_12_) | copy-start | bytes 12292
  16.2 1.5 copy-start.3
  17.6 2.7 copy-start.1
  21.8 44.9 %collective-permute-start.5 = (bf16[1536,256]{1,0:T(8,128)(2,1)}, bf16[1536,256]{1,0:T(8,128)(2,1)}, u32[]{:S(2)}, u32[]{:S(2)}) collective-permute-start(bf16[1536,256]{1,0:T(8,128)(2,1)} %get-tuple-element.221.v_ref), channel_id=1, source_target_pairs={{4,0},{8,4},{12,8},{16,12},{20,16},{24,20},{28,24},{5,1},{9,5},{13... | collective-permute-start | bytes 2359304 | tf_op jit(solution)/shard_map/ppermute | solution.py:1411
  24.3 42.5 %collective-permute-start.4 = (bf16[1536,256]{1,0:T(8,128)(2,1)}, bf16[1536,256]{1,0:T(8,128)(2,1)}, u32[]{:S(2)}, u32[]{:S(2)}) collective-permute-start(bf16[1536,256]{1,0:T(8,128)(2,1)} %get-tuple-element.221.v_ref), channel_id=1, source_target_pairs={{0,4},{4,8},{8,12},{12,16},{16,20},{20,24},{24,28},{1,5},{5,9},{9,... | collective-permute-start | bytes 2359304 | tf_op jit(solution)/shard_map/ppermute | solution.py:1411
  28.4 41.0 %collective-permute-start.2 = (bf16[1536,256]{1,0:T(8,128)(2,1)}, bf16[1536,256]{1,0:T(8,128)(2,1)}, u32[]{:S(2)}, u32[]{:S(2)}) collective-permute-start(bf16[1536,256]{1,0:T(8,128)(2,1)} %slice.266.k_ref), channel_id=1, source_target_pairs={{0,4},{4,8},{8,12},{12,16},{16,20},{20,24},{24,28},{1,5},{5,9},{9,... | collective-permute-start | bytes 2359304 | tf_op jit(solution)/shard_map/ppermute | solution.py:1411
  32.3 3.7 copy-start.22
  32.3 4.3 copy-start.6
  32.4 12.6 %copy-start.2 = (f32[384,1024]{1,0:T(8,128)}, f32[384,1024]{1,0:T(8,128)S(1)}, u32[]{:S(2)}) copy-start(f32[384,1024]{1,0:T(8,128)S(1)} %dynamic-slice_convert_fusion) | copy-start | bytes 4718596
  32.5 5.1 copy-start.25
  32.5 5.1 copy-start.26
  36.6 4.1 copy-start.8
  37.5 3.0 copy-start.27
  37.6 3.0 copy-start.28
  37.6 3.0 copy-start.29
  37.6 3.0 copy-start.30
  37.6 4.1 copy-start.7
  45.1 3.9 copy-start.4
  46.5 4.0 copy-start.5
  51.4 1.6 copy-start.10
  57.0 13.5 %collective-permute-start.3 = (bf16[1536,256]{1,0:T(8,128)(2,1)}, bf16[1536,256]{1,0:T(8,128)(2,1)S(1)}, u32[]{:S(2)}, u32[]{:S(2)}) collective-permute-start(bf16[1536,256]{1,0:T(8,128)(2,1)} %slice.266.k_ref), channel_id=1, source_target_pairs={{4,0},{8,4},{12,8},{16,12},{20,16},{24,20},{28,24},{5,1},{9,5},{13... | collective-permute-start | bytes 2359304 | tf_op jit(solution)/shard_map/ppermute | solution.py:1411
  422.5 51.6 %collective-permute-start.6 = (bf16[256,1024]{1,0:T(8,128)(2,1)}, bf16[256,1024]{1,0:T(8,128)(2,1)S(1)}, u32[]{:S(2)}, u32[]{:S(2)}) collective-permute-start(bf16[256,1024]{1,0:T(8,128)(2,1)} %get-tuple-element.109), channel_id=1, source_target_pairs={{0,8},{4,12},{8,0},{12,4},{16,24},{20,28},{24,16},{28,20},{1,9},{5... | collective-permute-start | bytes 1572872 | tf_op jit(solution)/shard_map/ppermute | solution.py:1500
  422.5 51.6 %collective-permute-start.7 = (bf16[256,1024]{1,0:T(8,128)(2,1)}, bf16[256,1024]{1,0:T(8,128)(2,1)S(1)}, u32[]{:S(2)}, u32[]{:S(2)}) collective-permute-start(bf16[256,1024]{1,0:T(8,128)(2,1)} %get-tuple-element.111), channel_id=1, source_target_pairs={{0,8},{4,12},{8,0},{12,4},{16,24},{20,28},{24,16},{28,20},{1,9},{5... | collective-permute-start | bytes 1572872 | tf_op jit(solution)/shard_map/ppermute | solution.py:1500
  474.1 0.8 copy-start.14
  474.1 1.0 copy-start.15
  475.1 153.4 %copy-start.21 = (f32[4608]{0:T(1024)S(1)}, f32[4608]{0:T(1024)}, u32[]{:S(2)}) copy-start(f32[4608]{0:T(1024)} %constant_dynamic-update-slice_fusion.6) | copy-start | bytes 55300
  629.2 55.9 %collective-permute-start.8 = (bf16[256,1024]{1,0:T(8,128)(2,1)}, bf16[256,1024]{1,0:T(8,128)(2,1)}, u32[]{:S(2)}, u32[]{:S(2)}) collective-permute-start(bf16[256,1024]{1,0:T(8,128)(2,1)} %get-tuple-element.126), channel_id=1, source_target_pairs={{0,8},{4,12},{8,0},{12,4},{16,24},{20,28},{24,16},{28,20},{1,9},{5... | collective-permute-start | bytes 1572872 | tf_op jit(solution)/shard_map/ppermute | solution.py:1500
  629.2 55.9 %collective-permute-start.9 = (bf16[256,1024]{1,0:T(8,128)(2,1)}, bf16[256,1024]{1,0:T(8,128)(2,1)}, u32[]{:S(2)}, u32[]{:S(2)}) collective-permute-start(bf16[256,1024]{1,0:T(8,128)(2,1)} %get-tuple-element.128), channel_id=1, source_target_pairs={{0,8},{4,12},{8,0},{12,4},{16,24},{20,28},{24,16},{28,20},{1,9},{5... | collective-permute-start | bytes 1572872 | tf_op jit(solution)/shard_map/ppermute | solution.py:1500
  631.3 51.2 %copy-start.32 = (f32[1,1024]{1,0:T(1,128)S(1)}, f32[1,1024]{1,0:T(1,128)}, u32[]{:S(2)}) copy-start(f32[1,1024]{1,0:T(1,128)} %get-tuple-element.134) | copy-start | bytes 12292
  631.3 51.2 %copy-start.33 = (f32[1,256]{1,0:T(1,128)S(1)}, f32[1,256]{1,0:T(1,128)}, u32[]{:S(2)}) copy-start(f32[1,256]{1,0:T(1,128)} %get-tuple-element.135) | copy-start | bytes 3076
  681.8 2.5 copy-start.19
  681.8 2.5 copy-start.20
  681.8 2.5 copy-start.34
  833.2 11.6 %copy-start.12 = (bf16[1024,1024]{1,0:T(8,128)(2,1)S(1)}, bf16[1024,1024]{1,0:T(8,128)(2,1)}, u32[]{:S(2)}) copy-start(bf16[1024,1024]{1,0:T(8,128)(2,1)} %get-tuple-element.147) | copy-start | bytes 6291460
  844.8 5.7 copy-start.11
  844.8 5.7 copy-start.13
  850.4 6.3 slice-start.2
  850.5 4.8 copy-start.16
  850.5 4.8 copy-start.17
  850.5 6.7 slice-start.3
  855.3 5.1 slice-start
  857.2 4.4 slice-start.1

commit v3 on v2

--- a/solution.py
+++ b/solution.py
@@ -393,7 +393,11 @@
 
 
 def call(kernel, name, collective_id, ins, outs, scratch, flops):
-    late_in = [(k, a) for k, a, late in ins if late is True]
+    late_in = [
+        (k, jax.ShapeDtypeStruct(a.shape[1:] if type(late) is int else a.shape, a.dtype))
+        for k, a, late in ins
+        if late is True or type(late) is int
+    ]
     late_out = [(k, shape, dtype) for k, shape, dtype, late in outs if late is True]
 
     def entry(*refs):
@@ -409,9 +413,10 @@
             if late == N.far:
                 r.sources[k] = ref
                 continue
-            setattr(r, k, bufs[k] if late else ref)
-            if late:
-                cp = pltpu.make_async_copy(ref, bufs[k], load_sems.at[len(r.loads)])
+            fetched = late is True or type(late) is int
+            setattr(r, k, bufs[k] if fetched else ref)
+            if fetched:
+                cp = pltpu.make_async_copy(ref.at[late] if type(late) is int else ref, bufs[k], load_sems.at[len(r.loads)])
                 cp.start()
                 r.loads[k] = cp
         bufs = {k: b for (k, _, _), b in zip(late_out, out_bufs)}
@@ -427,7 +432,7 @@
         kernel(r)
         r.finish()
 
-    space = lambda late: pl.BlockSpec(memory_space=pl.ANY if late else pltpu.VMEM)
+    space = lambda late: pl.BlockSpec(memory_space=pltpu.VMEM if late is False else pl.ANY)
     result = pl.pallas_call(
         entry,
         out_shape=[jax.ShapeDtypeStruct(shape, dtype) for _, shape, dtype, _ in outs],
@@ -684,6 +689,8 @@
     full2 = None if last else r.a1
 
     def pre(c):
+        r.need(N.proj)
+
         def cols(j):
             y = matmul_nn(chunk_of(r.attended, c), r.proj, j)
             r.part1[:, c, :, j] = y.astype(BF16).reshape(n, sub, -1)
@@ -748,8 +755,8 @@
         r.need(N.qkv)
         x = chunk_of(full2, c)
         width = r.q.shape[3]
-        for i, name in enumerate((N.q, N.k, N.v)):
-            y = matmul_nn(x, r.qkv, slice(i * width, (i + 1) * width))
+        for i, name in ((1, N.k), (2, N.v), (0, N.q)):
+            y = jnp.dot(x, r.qkv[i], preferred_element_type=F32)
             if i != 1:
                 y = y + r.qv_bias[i // 2 : i // 2 + 1, :]
             getattr(r, name)[:, c] = y.astype(BF16).reshape(n, sub, width)
@@ -781,15 +788,74 @@
     ex.drain()
 
 
-def forward_block(n, dp_size, last, collective_id, attended, proj, fc1, fc2, fc1_bias, vec, stream, qkv=None, qv_bias=None):
+def first_kernel(n, dp_size, chunks, sub, r):
+    halo = Halo(r.halo_sems, dp_size)
+    meet(halo.partners())
+    me = lax.axis_index(N.tensor)
+    r.need(N.tokens, N.qkv)
+    width = r.q.shape[3]
+    for c in range(chunks):
+
+        def norm(b, carry, c=c):
+            hat, _ = normalised(r.tokens[b, c].astype(F32))
+            r.a1[b, c] = (hat * r.vec[0:1, :] + r.vec[1:2, :]).astype(BF16)
+            return carry
+
+        lax.fori_loop(0, n, norm, 0)
+        x = chunk_of(r.a1, c)
+        for i, name in ((1, N.k), (2, N.v), (0, N.q)):
+            y = jnp.dot(x, r.qkv[i], preferred_element_type=F32)
+            if i != 1:
+                y = y + r.qv_bias[i // 2 : i // 2 + 1, :]
+            getattr(r, name)[:, c] = y.astype(BF16).reshape(n, sub, width)
+            r.store(name, (slice(None), c))
+            if i:
+                for way in range(2):
+                    halo.send(
+                        getattr(r, name).at[:, c], r.targets[name + N._near].at[way, :, c], way, (i - 1) * chunks + c
+                    )
+        r.store(N.a1, (slice(None), c))
+        own = r.tokens[me, c].astype(F32)
+        r.after[c] = own
+        hat, spread = normalised(own)
+        r.hat1[c] = hat
+        r.sp1[c] = spread
+    for i, name in enumerate((N.k_near, N.v_near)):
+        for c in range(chunks):
+            for way in range(2):
+                halo.wait(r.targets[name].at[way, :, c], way, i * chunks + c)
+    halo.drain()
+
+
+def first_block(n, dp_size, collective_id, tokens, qkv, qv_bias, vec):
+    rows = tokens.shape[0]
+    _, chunks, sub = sizes(rows, n)
+    width = qv_bias.shape[1]
+    split = lambda cols: (n, chunks, sub, cols)
+    mine = (chunks, sub, D)
+    outs = [(N.after, mine, F32, False), (N.hat1, mine, F32, False), (N.sp1, (chunks, sub, 1), F32, False)]
+    outs += [(N.a1, split(D), BF16, True)] + [(k, split(width), BF16, True) for k in (N.q, N.k, N.v)]
+    outs += [(k, (2,) + split(width), BF16, N.far) for k in (N.k_near, N.v_near)]
+    return call(
+        functools.partial(first_kernel, n, dp_size, chunks, sub),
+        N.first_block,
+        collective_id,
+        [(N.tokens, tokens.reshape(split(D)), True), (N.qkv, qkv, 0), (N.qv_bias, qv_bias, False), (N.vec, vec, False)],
+        outs,
+        [(N.halo_sems, pltpu.SemaphoreType.DMA((2, 2, 2 * chunks)))],
+        2 * rows * D * 3 * width,
+    )
+
+
+def forward_block(n, dp_size, last, level, attended, proj, fc1, fc2, fc1_bias, vec, stream, qkv=None, qv_bias=None):
     rows, width = attended.shape
     block, chunks, sub = sizes(rows, n)
-    hidden = fc1.shape[1]
+    hidden = fc1.shape[2]
     split = lambda cols: (n, chunks, sub, cols)
     mine = (chunks, sub, D)
     ins = [
-        (N.attended, attended.reshape(split(width)), False), (N.proj, proj, False), (N.stream, stream.reshape(mine), True),
-        (N.fc1, fc1, True), (N.fc2, fc2, True), (N.fc1_bias, fc1_bias, False), (N.vec, vec, False),
+        (N.attended, attended.reshape(split(width)), False), (N.proj, proj, level), (N.stream, stream.reshape(mine), True),
+        (N.fc1, fc1, level), (N.fc2, fc2, level), (N.fc1_bias, fc1_bias, False), (N.vec, vec, False),
     ]
     outs = [
         (N.u1, mine, F32, True), (N.hat2, mine, F32, True), (N.sp2, (chunks, sub, 1), F32, False),
@@ -800,7 +866,7 @@
     if last:
         outs += [(N.after, mine, BF16, True)]
     else:
-        ins += [(N.qkv, qkv, True), (N.qv_bias, qv_bias, False)]
+        ins += [(N.qkv, qkv, level + 1), (N.qv_bias, qv_bias, False)]
         outs += [(N.after, mine, F32, True), (N.hat1, mine, F32, True), (N.sp1, (chunks, sub, 1), F32, False)]
         outs += [(N.a1, split(D), BF16, True)] + [(k, split(width), BF16, True) for k in N.qkv]
         outs += [(k, (2,) + split(width), BF16, N.far) for k in (N.k_near, N.v_near)]
@@ -808,7 +874,7 @@
     return call(
         functools.partial(forward_kernel, n, dp_size, chunks, sub, last),
         N.forward_last if last else N.forward_block,
-        collective_id,
+        level,
         ins,
         outs,
         scratch + sem_scratch(4, n, chunks),
@@ -870,7 +936,13 @@
             r.dqkv[b, c, :, cols] = total.astype(BF16)
 
     def cols(j):
-        y = matmul_nt(chunk_of(r.dqkv, c), r.qkv, j)
+        x = chunk_of(r.dqkv, c)
+        y = sum(
+            lax.dot_general(
+                x[:, i * width : (i + 1) * width], r.qkv[i, j, :], (((1,), (1,)), ((), ())), preferred_element_type=F32
+            )
+            for i in range(3)
+        )
         r.part[:, c, :, j] = y.astype(BF16).reshape(ex.n, ex.sub, -1)
 
     column_loop(D, 256, cols)
@@ -882,7 +954,7 @@
     sems, part, recv = r.sems, r.part, r.recv
     row = lambda i: r.vec[i : i + 1, :]
     if first:
-        meet(ex.partners() + [{N.dp: core_partner()}])
+        meet(ex.partners() + [{N.dp: dp_partner(0)}, {N.dp: dp_partner(1)}])
     else:
         halo = Halo(r.halo_sems, dp_size)
         gs = GradSum(upper_arrays(r), r.grad_sems, dp_size)
@@ -986,11 +1058,19 @@
         first_sum.wait(a, 0)
         names = ((N.keep1, N.send1), (N.keep2, N.send2))[a]
         first_sum.split(a, getattr(r, names[0] + N._out), getattr(r, names[1] + N._out))
-        for name in names:
-            r.store(name + N._out)
-
-    extra += [(behind - chunks, lambda: first_sum.send(0, 0)), (behind + 1, lambda: part_of(0))]
-    extra += [(behind + 1, lambda: first_sum.send(1, 0)), (behind + 3, lambda: part_of(1))]
+        r.store(names[0] + N._out)
+        if first:
+            got = r.targets[(N.got1_out, N.got2_out)[a]]
+            cp = first_sum.copy(getattr(r, names[1] + N._out), got, a, 1, 1)
+            cp.start()
+            first_sum.pending.append(cp)
+            arrivals.append(cp)
+        else:
+            r.store(names[1] + N._out)
+
+    arrivals = []
+    extra += [(behind - chunks, lambda: first_sum.send(0, 0)), (behind - chunks + 1, lambda: part_of(0))]
+    extra += [(behind, lambda: first_sum.send(1, 0)), (behind + 1, lambda: part_of(1))]
     run_stages(ex, stages, extra)
     r.need(N.attended)
     for item in grad_items(r.attended, r.e1, r.g4, 0):
@@ -998,13 +1078,15 @@
     if not first:
         gs.drain()
         halo.drain()
+    for cp in arrivals:
+        cp.wait_recv()
     first_sum.drain()
     ex.drain()
 
 
-def core_partner():
+def dp_partner(k):
     me = lax.axis_index(N.dp)
-    return me + 1 - 2 * bit_of(me, 0)
+    return me + (1 - 2 * bit_of(me, k)) * (1 << k)
 
 
 def tail_sums(gs):
@@ -1063,7 +1145,7 @@
 def backward_block(n, dp_size, collective_id, source, above, fc1, fc2, proj, vec, saved):
     first = not above
     _, chunks, sub, hidden = saved[N.slope].shape
-    width = proj.shape[0]
+    width = proj[0].shape[1]
     split = lambda cols: (n, chunks, sub, cols)
     mine = (chunks, sub, D)
     ins = list(source.items()) + list(above.items()) + [(N.fc2, fc2), (N.slope, saved[N.slope]), (N.fc1, fc1)]
@@ -1072,9 +1154,17 @@
         (N.datt, split(width), BF16, True), (N.gm_out, mine, F32, N.gm), (N.sums, (8, D), F32, False),
         (N.fc1b, (1, hidden), F32, False), (N.g4, (grad_rows(width, dp_size), D), BF16, False),
     ]
+    quarters = []
     for i, (rows, cols) in enumerate(((hidden, D), (D, hidden))):
-        outs += [(k % (i + 1), (rows // 4, cols), BF16, True) for k in ("keep%d_out", "send%d_out")]
-    scratch = comm_scratch(n, chunks, sub, "") + [(N.e1, pltpu.VMEM(split(D), BF16))] + sem_scratch(4, n, chunks)
+        keep, send, got = ((N.keep1_out, N.send1_out, N.got1_out), (N.keep2_out, N.send2_out, N.got2_out))[i]
+        quarter = (rows // 4, cols)
+        outs += [(keep, quarter, BF16, True)]
+        if first:
+            quarters += [(send, pltpu.VMEM(quarter, BF16))]
+            outs += [(got, quarter, BF16, N.far)]
+        else:
+            outs += [(send, quarter, BF16, True)]
+    scratch = quarters + comm_scratch(n, chunks, sub, "") + [(N.e1, pltpu.VMEM(split(D), BF16))] + sem_scratch(4, n, chunks)
     scratch += [(N.g1, pltpu.VMEM((hidden, D), BF16)), (N.g2, pltpu.VMEM((D, hidden), BF16))]
     scratch += [(N.core_recv0, pltpu.VMEM((hidden // 2, D), BF16)), (N.core_recv1, pltpu.VMEM((D // 2, hidden), BF16))]
     scratch += [(N.core_sems, pltpu.SemaphoreType.DMA((2, 2, 2 * (dp_size.bit_length() - 1))))]
@@ -1088,11 +1178,15 @@
         functools.partial(backward_kernel, n, dp_size, chunks, sub, first),
         N.backward_first if first else N.backward_block,
         collective_id,
-        [(k, a, N.far if k == N.act and not first else lateness(k)) for k, a in ins],
+        [placed_input(k, a) if first or k != N.act else (k, a, N.far) for k, a in ins],
         outs,
         scratch,
         2 * n * chunks * sub * D * (2 * hidden + 4 * width),
     )
+
+
+def placed_input(name, array):
+    return (name,) + (array if isinstance(array, tuple) else (array, lateness(name)))
 
 
 def lateness(name):
@@ -1128,8 +1222,6 @@
 
     def post(c):
         ex.ag_wait(r.full, sems.at[1], c, ex.nbits - 1)
-        for b in range(n):
-            r.out[b, c] = r.full[b, c].astype(F32)
         r.store(N.out, (slice(None), c))
 
     made = [lambda: r.need(N.a1)] + grad_items(r.a1, r.dqkv, r.up3, 0)
@@ -1148,8 +1240,6 @@
         if p < ex.nbits:
             ex.ag_send(r.full3, sems.at[2], c, p)
         else:
-            for b in range(n):
-                r.out2[b, c] = r.full3[b, c].astype(F32)
             r.store(N.out2, (slice(None), c))
 
     for p in range(ex.nbits + 1):
@@ -1170,7 +1260,7 @@
     steps = (n * dp_size).bit_length() - 1
     ins = list(source.items()) + list(above.items()) + [(N.vec, vec), (N.base, base), (N.result, result)]
     more, results = upper_buffers(above, width, dp_size)
-    outs = [(N.out, split(D), F32, True), (N.out2, split(D), F32, True), (N.total, base.shape, F32, False)] + results
+    outs = [(N.out, split(D), BF16, N.full), (N.out2, split(D), BF16, N.full3), (N.total, base.shape, F32, False)] + results
     scratch = comm_scratch(n, chunks, sub, "") + sem_scratch(3, n, chunks) + home_buffers(n, chunks, sub, width)
     scratch += [(N.full3, pltpu.VMEM(split(D), BF16))]
     scratch += [(N.full, pltpu.VMEM(split(D), BF16)), (N.sums, pltpu.VMEM((8, D), F32)), (N.dv_sum, pltpu.VMEM((1, width), F32))]
@@ -1180,7 +1270,7 @@
         functools.partial(tail_kernel, n, dp_size, chunks, sub, wide),
         N.backward_tail,
         collective_id,
-        [(k, a, lateness(k)) for k, a in ins],
+        [placed_input(k, a) for k, a in ins],
         outs,
         scratch,
         2 * n * chunks * sub * D * 3 * width,
@@ -1406,11 +1496,6 @@
     )
 
 
-def near(array):
-    up, down = neighbours(N.dp)
-    return jnp.stack([lax.ppermute(array, N.dp, up), lax.ppermute(array, N.dp, down)])
-
-
 def own_part(array, n):
     block, chunks, sub = sizes(array.shape[0], n)
     first = lax.axis_index(N.tensor) * block
@@ -1426,7 +1511,7 @@
     width, hidden = qkv_weight.shape[3], fc1_weight.shape[2]
     _, chunks, sub = sizes(rows, n)
     split = (n, chunks, sub)
-    qkv2 = qkv_weight.reshape(LAYERS, D, 3 * width)
+    planes = jnp.transpose(qkv_weight, (0, 2, 1, 3))
     ids_win = with_halo(image_ids + 1)
     per = rows // TILES[3]
     place, places = lax.axis_index(N.dp), lax.axis_size(N.dp)
@@ -1434,20 +1519,13 @@
     lo, hi = reach(ids_win, rows, *TILES[1:], least, most)
     idq, idk = ids_win[rows : 2 * rows, None], ids_win[:, None]
 
-    stream = tokens.astype(F32)
-    hat, _ = normalised(stream)
-    a1 = (hat * ln1_gain[0] + ln1_bias[0]).astype(BF16)
-    first = jnp.dot(a1, qkv2[0], preferred_element_type=F32)
-    q = (first[:, :width] + qv_bias[0, 0]).astype(BF16)
-    k = first[:, width : 2 * width].astype(BF16)
-    v = (first[:, 2 * width :] + qv_bias[0, 1]).astype(BF16)
-    a1 = a1.reshape(split + (D,))
-    own = own_part(tokens, n).astype(F32)
-    hat1, sp1 = normalised(own)
+    dp_size = lax.axis_size(N.dp)
+    made = first_block(n, dp_size, 2 * LAYERS + 1, tokens, planes, qv_bias[0], jnp.stack([ln1_gain[0], ln1_bias[0]]))
+    own, hat1, sp1, a1 = made[N.after], made[N.hat1], made[N.sp1], made[N.a1]
+    q, k, v = (made[name].reshape(rows, width) for name in (N.q, N.k, N.v))
+    kn, vn = (made[name].reshape(2, rows, width) for name in (N.k_near, N.v_near))
 
     saved = []
-    dp_size = lax.axis_size(N.dp)
-    kn, vn = near(k), near(v)
     for level in range(LAYERS):
         kv = (kn, vn, k, v)
         attended, lse = attend_fwd(q, *kv, idq, idk, lo, hi, *TILES)
@@ -1459,9 +1537,9 @@
                 scale_mlp[level], ln1_gain[after], ln1_bias[after],
             ]
         )
-        extra = () if last else (qkv2[level + 1], qv_bias[level + 1])
+        extra = () if last else (planes, qv_bias[level + 1])
         made = forward_block(
-            n, dp_size, last, level, attended, proj_weight[level], fc1_weight[level], fc2_weight[level], fc1_bias[level][None],
+            n, dp_size, last, level, attended, proj_weight, fc1_weight, fc2_weight, fc1_bias[level][None],
             vec, own, *extra,
         )
         keep = {name: made[name] for name in (N.u1, N.hat2, N.sp2, N.u2, N.a2, N.act, N.slope)}
@@ -1487,7 +1565,7 @@
         upper = min(level + 1, LAYERS - 1)
         vec = jnp.stack([scale_mlp[level], ln2_gain[level], scale_attn[level], ln1_gain[upper]])
         outs = backward_block(
-            n, dp_size, LAYERS + level, source, above, fc1_weight[level], fc2_weight[level], proj_weight[level], vec, keep,
+            n, dp_size, LAYERS + level, source, above, (fc1_weight, level), (fc2_weight, level), (proj_weight, level), vec, keep,
         )
         datt, fc1b, sums[level + 1] = outs[N.datt], outs[N.fc1b], outs[N.sums]
         if above:
@@ -1497,14 +1575,16 @@
         above = {N.up4: outs[N.g4]}
         for name in "12":
             above[N.keep + name] = outs[N.keep + name + N._out]
-            above[N.got + name] = lax.ppermute(outs[N.send + name + N._out], N.dp, flip)
+            got = N.got + name + N._out
+            send = N.send + name + N._out
+            above[N.got + name] = outs[got] if got in outs else lax.ppermute(outs[send], N.dp, flip)
         dq, dkv, q_sum = attend_bwd(
             q, *kv, idq, idk, lo, hi, attended, datt.reshape(rows, width), lse, *TILES
         )
         narrow[level] = (fc1b[0], q_sum[0])
         dkv = dkv.reshape((2, 3) + split + (width,))
         source = {
-            N.dkv_in: dkv, N.dq: dq.reshape(split + (width,)), N.qkv: qkv2[level], N.hat1: hat1,
+            N.dkv_in: dkv, N.dq: dq.reshape(split + (width,)), N.qkv: (planes, level), N.hat1: hat1,
             N.gm: outs[N.gm_out], N.a1: a1, N.sp1: sp1,
         }
     pad = jnp.zeros((D - width,), F32)
@@ -1525,7 +1605,10 @@
     fc1b_total, qv_total = flat[:, :hidden], jnp.stack([flat[:, hidden:], dv_total], axis=1)
     stacked = lambda parts: jnp.stack([x.astype(F32) for x in parts])
     big = [
-        stacked([x[2] for x in grads]),
+        jnp.transpose(
+            stacked([x[2][:, i * width : (i + 1) * width] for x in grads for i in range(3)]).reshape(LAYERS, 3, D, width),
+            (0, 2, 1, 3),
+        ),
         stacked([x[3][:width] for x in grads]),
         stacked([x[1] for x in grads]),
         stacked([x[0] for x in grads]),
@@ -1533,11 +1616,11 @@
     total = total[:wide].reshape(LAYERS + 1, 8, D)
     upper, lower = total[1:], total[:-1]
     return (
-        tail[N.out2].reshape(rows, D),
-        grad_tokens.reshape(rows, D),
+        tail[N.out2].reshape(rows, D).astype(F32),
+        grad_tokens.reshape(rows, D).astype(F32),
         lower[:, 6],
         lower[:, 7],
-        big[0].reshape(LAYERS, D, 3, width),
+        big[0],
         qv_total,
         big[1],
         upper[:, 5],

time: 874 us -> 834 us (0.954)
  local copies, waits for them, and re-layouts: 58.2 us -> 26.6 us
  Pallas kernels: 741 us -> 755 us
  starting transfers between devices: 19.6 us -> 7.14 us
    unnamed x98 -> x68, local copies, waits for them, and re-layouts: 29 us -> 12.4 us
    ppermute x8 -> x2, starting transfers between devices: 13.8 us -> 1.46 us  [body(): lax.ppermute(outs[send], N.dp, flip)]
    squeeze x5 -> x1, local copies, waits for them, and re-layouts: 10.2 us -> 1.28 us  [body(): extra = () if last else (planes, qv_bias[level + 1])]
    pallas_call x5 -> x6, Pallas kernels: 561 us -> 565 us  [call(): pl.pallas_call(entry, out_shape=[jax.ShapeDtypeStruct(shape, dtype) for _...]
  transfers between devices with their start and end apart: 10 -> 4, of which waited for: 1 -> 0; matrix products, arithmetic and copies ran while one was open for 6% -> 2% of each run, Pallas kernels for 12% -> 10%
where the time goes in v3:
time: 834 us; the launch traced here: 824 us
  Pallas kernels  755 us (91%)
  other arithmetic  33.3 us (4%)
  local copies, waits for them, and re-layouts  26.6 us (3%)
    pallas_call x6, Pallas kernels, call(): pl.pallas_call(entry, out_shape=[jax.ShapeDtypeStruct(shape, dtype) for _...  565 us
    pallas_call x2, Pallas kernels, attend_bwd(): pl.pallas_call(functools.partial(bwd_kernel, HH, QB, KB, KT, nq), grid_sp...  107 us
    pallas_call x2, Pallas kernels, attend_fwd(): pl.pallas_call(functools.partial(fwd_kernel, HH, QB, KB, KT, nq), grid_sp...  83.8 us
  transfers between devices with their start and end apart: 4, of which 0 were waited for; matrix products, arithmetic and copies ran while one was open for 2% of the time, Pallas kernels for 10%

profile of v3, /device:TPU:17, one launch (start us, length us, event | category | flops | bytes accessed | tf_op | source)
XLA Modules:
  0.0 823.6 jit_solution(727867740355411004)
XLA Ops:
  0.6 0.7 broadcast_add_fusion
  1.3 3.8 collective-permute-start
  5.1 1.9 collective-permute-start.1
  7.1 0.2 slice_reduce_fusion
  7.2 1.3 slice_bitcast_fusion.4
  8.5 1.4 fusion.12
  9.9 0.8 fusion.11
  10.7 1.2 constant_dynamic-slice_fusion
  11.9 0.0 copy-start.15
  12.0 4.5 multiply_convert_fusion
  16.5 0.6 pad_maximum_fusion.3.refs_3_
  17.1 27.2 %first_block.1 = (f32[3,128,1024]{2,1,0:T(8,128)}, f32[3,128,1024]{2,1,0:T(8,128)}, f32[3,128,1]{2,1,0:T(8,128)}, bf16[4,3,128,1024]{3,2,1,0:T(8,128)(2,1)}, bf1...) custom-call(bf16[4,3,128,1024]{3,2,1,0:T(8,128)(2,1)} %bitcast.128, ...), custom_call_target="tpu_custom_call" | custom-call | flops 2415919104 | bytes 100000000 | tf_op jit(solution)/shard_map/first_block/pallas_call | solution.py:436
  44.4 0.6 pad_maximum_fusion.1
  45.0 0.6 constant_dynamic-update-slice_fusion
  45.6 1.1 broadcast_in_dim.24.idq_ref
  46.7 1.3 convert.21.refs_1_
  48.1 0.5 pad.13.clone
  48.6 0.7 stack.96.refs_6_
  49.2 0.7 stack.95.refs_6_
  49.9 0.1 rev.3
  50.0 3.1 broadcast_in_dim.25.idk_ref
  53.1 0.7 iota_reduce_fusion.1
  53.8 0.7 iota_reduce_fusion
  54.6 0.7 fusion.2
  55.2 0.6 fusion.4
  55.9 1.9 pad_add_fusion.1
  57.7 41.8 %attend_fwd.2 = (bf16[1536,256]{1,0:T(8,128)(2,1)}, f32[1,4,1536]{2,1,0:T(4,128)}) custom-call(s32[4]{0:T(128)} %get-tuple-element.273.lo_ref, s32[4]{0:T(128)} %get-tuple-element.274.hi_ref, bf16[1536,256]{1,0:T(8,128)(2,1)} %bitcast.138, bf16[2,1536,256]{2,1,0:T(8,128)(2,1)} %bitcast.130, bf16[2,1536,256]{2,1,0:T(8,128)(2,1)} %bitcast.132, ...), custom_call_target="tpu_custom_call" | custom-call | flops 49999998976 | bytes 100000000 | tf_op jit(solution)/shard_map/attend_fwd/pallas_call | solution.py:1356
  99.5 117.6 %forward_block.1 = (f32[3,128,1024]{2,1,0:T(8,128)}, f32[3,128,1024]{2,1,0:T(8,128)}, f32[3,128,1]{2,1,0:T(8,128)}, f32[3,128,1024]{2,1,0:T(8,128)}, bf16[4,3,12...) custom-call(bf16[4,3,128,256]{3,2,1,0:T(8,128)(2,1)} %bitcast.109, ...), custom_call_target="tpu_custom_call" | custom-call | flops 9663676416 | bytes 100000000 | tf_op jit(solution)/shard_map/forward_block/pallas_call | solution.py:436
  217.1 42.0 %attend_fwd.3 = (bf16[1536,256]{1,0:T(8,128)(2,1)}, f32[1,4,1536]{2,1,0:T(4,128)}) custom-call(s32[4]{0:T(128)} %get-tuple-element.273.lo_ref, s32[4]{0:T(128)} %get-tuple-element.274.hi_ref, bf16[1536,256]{1,0:T(8,128)(2,1)} %bitcast.144, bf16[2,1536,256]{2,1,0:T(8,128)(2,1)} %bitcast.134, bf16[2,1536,256]{2,1,0:T(8,128)(2,1)} %bitcast.136, ...), custom_call_target="tpu_custom_call" | custom-call | flops 49999998976 | bytes 100000000 | tf_op jit(solution)/shard_map/attend_fwd/pallas_call | solution.py:1356
  259.2 79.6 %forward_last.1 = (f32[3,128,1024]{2,1,0:T(8,128)}, f32[3,128,1024]{2,1,0:T(8,128)}, f32[3,128,1]{2,1,0:T(8,128)}, f32[3,128,1024]{2,1,0:T(8,128)}, bf16[4,3,128...) custom-call(bf16[4,3,128,256]{3,2,1,0:T(8,128)(2,1)} %bitcast.150, ...), custom_call_target="tpu_custom_call" | custom-call | flops 9663676416 | bytes 100000000 | tf_op jit(solution)/shard_map/forward_last/pallas_call | solution.py:436
  338.8 64.6 %backward_first.1 = (bf16[4,3,128,256]{3,2,1,0:T(8,128)(2,1)}, f32[3,128,1024]{2,1,0:T(8,128)}, f32[8,1024]{1,0:T(8,128)}, f32[1,1024]{1,0:T(1,128)}, bf16[256,1...) custom-call(bf16[4,3,128,1024]{3,2,1,0:T(8,128)(2,1)} %bitcast.103, ...), custom_call_target="tpu_custom_call" | custom-call | flops 9663676416 | bytes 100000000 | tf_op jit(solution)/shard_map/backward_first/pallas_call | solution.py:436
  403.5 53.5 %attend_bwd.2 = (bf16[1536,256]{1,0:T(8,128)(2,1)}, bf16[2,4608,256]{2,1,0:T(8,128)(2,1)}, f32[1,256]{1,0:T(1,128)}) custom-call(s32[4]{0:T(128)} %get-tuple-element.273.lo_ref, s32[4]{0:T(128)} %get-tuple-element.274.hi_ref, bf16[1536,256]{1,0:T(8,128)(2,1)} %bitcast.145, bf16[2,1536,256]{2,1,0:T(8,128)(2,1)} %bitcast.135, bf16[2,1536,256]{2,1,0:T(8,128)(2,1)} %bitcast.137, ...), custom_call_target="tpu_custom_call" | custom-call | flops 49999998976 | bytes 100000000 | tf_op jit(solution)/shard_map/attend_bwd/pallas_call | solution.py:1461
  457.0 146.5 %backward_block.1 = (bf16[4,3,128,256]{3,2,1,0:T(8,128)(2,1)}, f32[3,128,1024]{2,1,0:T(8,128)}, f32[8,1024]{1,0:T(8,128)}, f32[1,1024]{1,0:T(1,128)}, bf16[256,1...) custom-call(bf16[2,3,4,3,128,256]{5,4,3,2,1,0:T(8,128)(2,1)} %bitcas, ...), custom_call_target="tpu_custom_call" | custom-call | flops 9663676416 | bytes 100000000 | tf_op jit(solution)/shard_map/backward_block/pallas_call | solution.py:436
  603.4 0.6 constant_dynamic-update-slice_fusion.6
  604.0 1.5 collective-permute-start.3
  605.5 0.7 constant_dynamic-update-slice_fusion.4
  606.2 53.2 %attend_bwd.3 = (bf16[1536,256]{1,0:T(8,128)(2,1)}, bf16[2,4608,256]{2,1,0:T(8,128)(2,1)}, f32[1,256]{1,0:T(1,128)}) custom-call(s32[4]{0:T(128)} %get-tuple-element.273.lo_ref, s32[4]{0:T(128)} %get-tuple-element.274.hi_ref, bf16[1536,256]{1,0:T(8,128)(2,1)} %bitcast.139, bf16[2,1536,256]{2,1,0:T(8,128)(2,1)} %bitcast.131, bf16[2,1536,256]{2,1,0:T(8,128)(2,1)} %bitcast.133, ...), custom_call_target="tpu_custom_call" | custom-call | flops 49999998976 | bytes 100000000 | tf_op jit(solution)/shard_map/attend_bwd/pallas_call | solution.py:1461
  659.5 0.7 constant_dynamic-update-slice_fusion.3
  660.2 0.7 pad_maximum_fusion.refs_13_
  661.0 0.8 copy-done.7
  661.8 0.2 copy-done.8
  661.9 129.1 %backward_tail.1 = (bf16[4,3,128,1024]{3,2,1,0:T(8,128)(2,1)}, bf16[4,3,128,1024]{3,2,1,0:T(8,128)(2,1)}, f32[32,1024]{1,0:T(8,128)}, bf16[1024,1024]{1,0:T(8,12...) custom-call(bf16[2,3,4,3,128,256]{5,4,3,2,1,0:T(8,128)(2,1)} %bitcast.100, ...), custom_call_target="tpu_custom_call" | custom-call | flops 2415919104 | bytes 100000000 | tf_op jit(solution)/shard_map/backward_tail/pallas_call | solution.py:436
  791.1 0.9 slice.182
  792.0 0.7 slice_bitcast_fusion.3
  792.7 0.9 slice_bitcast_fusion
  793.7 0.6 slice.205
  794.3 0.6 copy.92
  794.9 1.1 bitcast_dynamic-update-slice_fusion.5
  795.9 1.1 bitcast_dynamic-update-slice_fusion.4
  797.0 1.1 bitcast_dynamic-update-slice_fusion.3
  798.3 3.3 convert_bitcast_fusion
  801.5 3.7 bitcast_convert_fusion
  805.2 3.7 bitcast_convert_fusion.1
  808.9 0.6 copy.109
  809.5 0.6 copy.110
  810.1 0.6 copy.111
  810.7 0.6 copy.112
  811.3 0.6 copy.113
  811.9 0.6 copy.114
  812.5 0.6 copy.115
  813.1 0.6 copy.116
  813.8 4.2 maximum_convert_fusion.1
  817.9 3.9 maximum_convert_fusion
  821.9 1.5 maximum_convert_fusion.2
  (71 shorter events, 0.4 us)
Async XLA Ops:
  1.3 48.6 %collective-permute-start = (s32[1536]{0:T(1024)S(1)}, s32[1536]{0:T(1024)S(1)}, u32[]{:S(2)}, u32[]{:S(2)}) collective-permute-start(s32[1536]{0:T(1024)S(1)} %broadcast_add_fusion), channel_id=1, source_target_pairs={{0,4},{4,8},{8,12},{12,16},{16,20},{20,24},{24,28},{1,5},{5,9},{9,... | collective-permute-start | bytes 18440 | tf_op jit(solution)/shard_map/ppermute | solution.py:1495
  5.1 44.8 %collective-permute-start.1 = (s32[1536]{0:T(1024)S(1)}, s32[1536]{0:T(1024)S(1)}, u32[]{:S(2)}, u32[]{:S(2)}) collective-permute-start(s32[1536]{0:T(1024)S(1)} %broadcast_add_fusion), channel_id=1, source_target_pairs={{4,0},{8,4},{12,8},{16,12},{20,16},{24,20},{28,24},{5,1},{9,5},{13... | collective-permute-start | bytes 18440 | tf_op jit(solution)/shard_map/ppermute | solution.py:1495
  11.9 4.5 copy-start.15
  11.9 4.5 copy-start.16
  11.9 5.2 copy-start.17
  11.9 5.2 copy-start.18
  11.9 5.2 copy-start.19
  11.9 5.2 copy-start.20
  16.5 32.1 %copy-start.11 = (f32[1,1024]{1,0:T(1,128)}, f32[1,1024]{1,0:T(1,128)S(1)}, u32[]{:S(2)}) copy-start(f32[1,1024]{1,0:T(1,128)S(1)} %get-tuple-element.271.refs_12_) | copy-start | bytes 12292
  456.9 146.5 %copy-start.14 = (f32[4608]{0:T(1024)S(1)}, f32[4608]{0:T(1024)}, u32[]{:S(2)}) copy-start(f32[4608]{0:T(1024)} %constant_dynamic-update-slice_fusion) | copy-start | bytes 55300
  604.0 56.9 %collective-permute-start.2 = (bf16[256,1024]{1,0:T(8,128)(2,1)}, bf16[256,1024]{1,0:T(8,128)(2,1)S(1)}, u32[]{:S(2)}, u32[]{:S(2)}) collective-permute-start(bf16[256,1024]{1,0:T(8,128)(2,1)} %get-tuple-element.144), channel_id=1, source_target_pairs={{0,8},{4,12},{8,0},{12,4},{16,24},{20,28},{24,16},{28,20},{1,9},{5... | collective-permute-start | bytes 1572872 | tf_op jit(solution)/shard_map/ppermute | solution.py:1580
  604.0 56.9 %collective-permute-start.3 = (bf16[256,1024]{1,0:T(8,128)(2,1)}, bf16[256,1024]{1,0:T(8,128)(2,1)S(1)}, u32[]{:S(2)}, u32[]{:S(2)}) collective-permute-start(bf16[256,1024]{1,0:T(8,128)(2,1)} %get-tuple-element.146), channel_id=1, source_target_pairs={{0,8},{4,12},{8,0},{12,4},{16,24},{20,28},{24,16},{28,20},{1,9},{5... | collective-permute-start | bytes 1572872 | tf_op jit(solution)/shard_map/ppermute | solution.py:1580
  606.2 53.9 %copy-start.21 = (f32[1,1024]{1,0:T(1,128)S(1)}, f32[1,1024]{1,0:T(1,128)}, u32[]{:S(2)}) copy-start(f32[1,1024]{1,0:T(1,128)} %get-tuple-element.152) | copy-start | bytes 12292
  606.2 53.9 %copy-start.22 = (f32[1,256]{1,0:T(1,128)S(1)}, f32[1,256]{1,0:T(1,128)}, u32[]{:S(2)}) copy-start(f32[1,256]{1,0:T(1,128)} %get-tuple-element.153) | copy-start | bytes 3076
  606.2 54.0 %copy-start.12 = (f32[8,1024]{1,0:T(8,128)S(1)}, f32[8,1024]{1,0:T(8,128)}, u32[]{:S(2)}) copy-start(f32[8,1024]{1,0:T(8,128)} %get-tuple-element.148) | copy-start | bytes 98308
  606.2 54.0 %copy-start.13 = (f32[8,1024]{1,0:T(8,128)S(1)}, f32[8,1024]{1,0:T(8,128)}, u32[]{:S(2)}) copy-start(f32[8,1024]{1,0:T(8,128)} %get-tuple-element.147) | copy-start | bytes 98308
  606.2 54.0 %copy-start.23 = (f32[32]{0:T(128)S(1)}, f32[32]{0:T(128)}, u32[]{:S(2)}) copy-start(f32[32]{0:T(128)} %pad.13.clone) | copy-start | bytes 388
  661.0 0.8 copy-start.7
  661.0 1.0 copy-start.8
  791.1 7.0 copy-start.6
  798.2 3.3 copy-start.1
  801.5 3.7 copy-start
  805.2 8.6 %copy-start.3 = (bf16[1024,1024]{1,0:T(8,128)(2,1)S(1)}, bf16[1024,1024]{1,0:T(8,128)(2,1)}, u32[]{:S(2)}) copy-start(bf16[1024,1024]{1,0:T(8,128)(2,1)} %get-tuple-element.165) | copy-start | bytes 6291460
  805.2 8.6 %copy-start.5 = (bf16[1024,1024]{1,0:T(8,128)(2,1)S(1)}, bf16[1024,1024]{1,0:T(8,128)(2,1)}, u32[]{:S(2)}) copy-start(bf16[1024,1024]{1,0:T(8,128)(2,1)} %get-tuple-element.164) | copy-start | bytes 6291460
  813.8 4.2 copy-start.2
  813.8 4.2 copy-start.4
  817.9 3.9 copy-start.9
  817.9 4.0 copy-start.10

commit v4 on v3

--- a/solution.py
+++ b/solution.py
@@ -983,11 +983,18 @@
         ex.ag_send(r.full, sems.at[1], c, 0)
 
     def mid(c):
-        r.need(N.fc1, N.fc2, N.slope, N.full, N.u2, N.gm)
+        r.need(N.full, N.fc2, N.slope, N.fc1, N.u2, N.gm)
         if not first and c == 0:
             ex.drain()
         if first:
-            g = r.gm[c]
+            g = r.full[ex.me, c].astype(F32)
+            r.gm[c] = g
+
+            def scaled(b, carry):
+                r.full[b, c] = (r.full[b, c].astype(F32) * row(0)).astype(BF16)
+                return carry
+
+            lax.fori_loop(0, n, scaled, 0)
             add_rows(r.sums, 0, g * r.u2[c])
             add_rows(r.sums, 1, g * row(0))
         else:
@@ -1168,7 +1175,9 @@
     scratch += [(N.g1, pltpu.VMEM((hidden, D), BF16)), (N.g2, pltpu.VMEM((D, hidden), BF16))]
     scratch += [(N.core_recv0, pltpu.VMEM((hidden // 2, D), BF16)), (N.core_recv1, pltpu.VMEM((D // 2, hidden), BF16))]
     scratch += [(N.core_sems, pltpu.SemaphoreType.DMA((2, 2, 2 * (dp_size.bit_length() - 1))))]
-    if not first:
+    if first:
+        scratch += [(N.gm, pltpu.VMEM(mine, F32))]
+    else:
         scratch += [(N.act_sem, pltpu.SemaphoreType.DMA)]
         scratch += [(N.full, pltpu.VMEM(split(D), BF16))] + home_buffers(n, chunks, sub, width)
         more, results = upper_buffers(above, width, dp_size)
@@ -1496,12 +1505,6 @@
     )
 
 
-def own_part(array, n):
-    block, chunks, sub = sizes(array.shape[0], n)
-    first = lax.axis_index(N.tensor) * block
-    return lax.dynamic_slice_in_dim(array, first, block, 0).reshape(chunks, sub, array.shape[1])
-
-
 def body(
     tokens, image_ids, cotangent, ln1_gain, ln1_bias, qkv_weight, qv_bias, proj_weight, proj_bias, scale_attn,
     ln2_gain, ln2_bias, fc1_weight, fc1_bias, fc2_weight, fc2_bias, scale_mlp,
@@ -1552,11 +1555,7 @@
             q, k, v = (made[name].reshape(rows, width) for name in N.qkv)
             kn, vn = (made[name].reshape(2, rows, width) for name in (N.k_near, N.v_near))
 
-    cot = cotangent.astype(F32)
-    source = {
-        N.full: (cot * scale_mlp[LAYERS - 1]).astype(BF16).reshape(split + (D,)),
-        N.gm: own_part(cotangent, n).astype(F32),
-    }
+    source = {N.full: cotangent.reshape(split + (D,))}
     above, grads = {}, [None] * LAYERS
     sums, narrow, dv_sums = [None] * (LAYERS + 1), [None] * LAYERS, [None] * LAYERS
     up, down = neighbours(N.dp)

time: 834 us -> 829 us (level)
    pallas_call x6, Pallas kernels: 565 us -> 582 us  [call(): pl.pallas_call(entry, out_shape=[jax.ShapeDtypeStruct(shape, dtype) for _...]
  transfers between devices with their start and end apart: 4 -> 4, of which waited for: 0 -> 0; matrix products, arithmetic and copies ran while one was open for 2% -> 2% of each run, Pallas kernels for 10% -> 9%
where the time goes in v4:
time: 829 us; the launch traced here: 825 us
  Pallas kernels  762 us (92%)
  local copies, waits for them, and re-layouts  27.8 us (3%)
  other arithmetic  27.5 us (3%)
    pallas_call x6, Pallas kernels, call(): pl.pallas_call(entry, out_shape=[jax.ShapeDtypeStruct(shape, dtype) for _...  582 us
    pallas_call x2, Pallas kernels, attend_bwd(): pl.pallas_call(functools.partial(bwd_kernel, HH, QB, KB, KT, nq), grid_sp...  100 us
    pallas_call x2, Pallas kernels, attend_fwd(): pl.pallas_call(functools.partial(fwd_kernel, HH, QB, KB, KT, nq), grid_sp...  78.7 us
  transfers between devices with their start and end apart: 4, of which 0 were waited for; matrix products, arithmetic and copies ran while one was open for 2% of the time, Pallas kernels for 9%

profile of v4, /device:TPU:17, one launch (start us, length us, event | category | flops | bytes accessed | tf_op | source)
XLA Modules:
  0.0 825.2 jit_solution(18395646328874546035)
XLA Ops:
  0.6 0.7 broadcast_add_fusion
  1.3 3.8 collective-permute-start
  5.1 1.9 collective-permute-start.1
  7.0 0.2 slice_reduce_fusion
  7.2 1.3 slice_bitcast_fusion.4
  8.5 1.4 fusion.13
  9.9 0.8 fusion.14
  10.7 0.6 pad_maximum_fusion.3.refs_3_
  11.3 0.8 fusion.7
  12.1 0.8 fusion.11
  12.9 0.8 fusion.9
  13.7 27.1 %first_block.1 = (f32[3,128,1024]{2,1,0:T(8,128)}, f32[3,128,1024]{2,1,0:T(8,128)}, f32[3,128,1]{2,1,0:T(8,128)}, bf16[4,3,128,1024]{3,2,1,0:T(8,128)(2,1)}, bf1...) custom-call(bf16[4,3,128,1024]{3,2,1,0:T(8,128)(2,1)} %bitcast.122, ...), custom_call_target="tpu_custom_call" | custom-call | flops 2415919104 | bytes 100000000 | tf_op jit(solution)/shard_map/first_block/pallas_call | solution.py:436
  40.8 0.6 pad_maximum_fusion.1
  41.5 0.6 constant_dynamic-update-slice_fusion
  42.1 1.1 broadcast_in_dim.24.idq_ref
  43.2 0.5 pad.13.clone
  43.7 0.7 stack.96.refs_6_
  44.4 0.7 stack.95.refs_6_
  45.1 0.1 rev.3
  45.2 3.1 broadcast_in_dim.25.idk_ref
  48.3 0.7 iota_reduce_fusion.1
  49.0 0.7 iota_reduce_fusion
  49.7 0.7 fusion.2
  50.4 0.6 fusion.4
  51.0 1.9 pad_add_fusion.1
  52.9 39.2 %attend_fwd.2 = (bf16[1536,256]{1,0:T(8,128)(2,1)}, f32[1,4,1536]{2,1,0:T(4,128)}) custom-call(s32[4]{0:T(128)} %get-tuple-element.273.lo_ref, s32[4]{0:T(128)} %get-tuple-element.274.hi_ref, bf16[1536,256]{1,0:T(8,128)(2,1)} %bitcast.133, bf16[2,1536,256]{2,1,0:T(8,128)(2,1)} %bitcast.125, bf16[2,1536,256]{2,1,0:T(8,128)(2,1)} %bitcast.127, ...), custom_call_target="tpu_custom_call" | custom-call | flops 49999998976 | bytes 100000000 | tf_op jit(solution)/shard_map/attend_fwd/pallas_call | solution.py:1365
  92.1 118.6 %forward_block.1 = (f32[3,128,1024]{2,1,0:T(8,128)}, f32[3,128,1024]{2,1,0:T(8,128)}, f32[3,128,1]{2,1,0:T(8,128)}, f32[3,128,1024]{2,1,0:T(8,128)}, bf16[4,3,12...) custom-call(bf16[4,3,128,256]{3,2,1,0:T(8,128)(2,1)} %bitcast.104, ...), custom_call_target="tpu_custom_call" | custom-call | flops 9663676416 | bytes 100000000 | tf_op jit(solution)/shard_map/forward_block/pallas_call | solution.py:436
  210.7 39.5 %attend_fwd.3 = (bf16[1536,256]{1,0:T(8,128)(2,1)}, f32[1,4,1536]{2,1,0:T(4,128)}) custom-call(s32[4]{0:T(128)} %get-tuple-element.273.lo_ref, s32[4]{0:T(128)} %get-tuple-element.274.hi_ref, bf16[1536,256]{1,0:T(8,128)(2,1)} %bitcast.139, bf16[2,1536,256]{2,1,0:T(8,128)(2,1)} %bitcast.129, bf16[2,1536,256]{2,1,0:T(8,128)(2,1)} %bitcast.131, ...), custom_call_target="tpu_custom_call" | custom-call | flops 49999998976 | bytes 100000000 | tf_op jit(solution)/shard_map/attend_fwd/pallas_call | solution.py:1365
  250.2 83.7 %forward_last.1 = (f32[3,128,1024]{2,1,0:T(8,128)}, f32[3,128,1024]{2,1,0:T(8,128)}, f32[3,128,1]{2,1,0:T(8,128)}, f32[3,128,1024]{2,1,0:T(8,128)}, bf16[4,3,128...) custom-call(bf16[4,3,128,256]{3,2,1,0:T(8,128)(2,1)} %bitcast.145, ...), custom_call_target="tpu_custom_call" | custom-call | flops 9663676416 | bytes 100000000 | tf_op jit(solution)/shard_map/forward_last/pallas_call | solution.py:436
  333.9 67.3 %backward_first.1 = (bf16[4,3,128,256]{3,2,1,0:T(8,128)(2,1)}, f32[3,128,1024]{2,1,0:T(8,128)}, f32[8,1024]{1,0:T(8,128)}, f32[1,1024]{1,0:T(1,128)}, bf16[256,1...) custom-call(bf16[4,3,128,1024]{3,2,1,0:T(8,128)(2,1)} %bitcast.123, ...), custom_call_target="tpu_custom_call" | custom-call | flops 9663676416 | bytes 100000000 | tf_op jit(solution)/shard_map/backward_first/pallas_call | solution.py:436
  401.2 50.3 %attend_bwd.2 = (bf16[1536,256]{1,0:T(8,128)(2,1)}, bf16[2,4608,256]{2,1,0:T(8,128)(2,1)}, f32[1,256]{1,0:T(1,128)}) custom-call(s32[4]{0:T(128)} %get-tuple-element.273.lo_ref, s32[4]{0:T(128)} %get-tuple-element.274.hi_ref, bf16[1536,256]{1,0:T(8,128)(2,1)} %bitcast.140, bf16[2,1536,256]{2,1,0:T(8,128)(2,1)} %bitcast.130, bf16[2,1536,256]{2,1,0:T(8,128)(2,1)} %bitcast.132, ...), custom_call_target="tpu_custom_call" | custom-call | flops 49999998976 | bytes 100000000 | tf_op jit(solution)/shard_map/attend_bwd/pallas_call | solution.py:1470
  451.6 154.9 %backward_block.1 = (bf16[4,3,128,256]{3,2,1,0:T(8,128)(2,1)}, f32[3,128,1024]{2,1,0:T(8,128)}, f32[8,1024]{1,0:T(8,128)}, f32[1,1024]{1,0:T(1,128)}, bf16[256,1...) custom-call(bf16[2,3,4,3,128,256]{5,4,3,2,1,0:T(8,128)(2,1)} %bitcas, ...), custom_call_target="tpu_custom_call" | custom-call | flops 9663676416 | bytes 100000000 | tf_op jit(solution)/shard_map/backward_block/pallas_call | solution.py:436
  606.5 0.7 constant_dynamic-update-slice_fusion.6
  607.2 1.5 collective-permute-start.3
  608.7 0.7 constant_dynamic-update-slice_fusion.4
  609.4 0.0 copy-start.17
  609.4 50.1 %attend_bwd.3 = (bf16[1536,256]{1,0:T(8,128)(2,1)}, bf16[2,4608,256]{2,1,0:T(8,128)(2,1)}, f32[1,256]{1,0:T(1,128)}) custom-call(s32[4]{0:T(128)} %get-tuple-element.273.lo_ref, s32[4]{0:T(128)} %get-tuple-element.274.hi_ref, bf16[1536,256]{1,0:T(8,128)(2,1)} %bitcast.134, bf16[2,1536,256]{2,1,0:T(8,128)(2,1)} %bitcast.126, bf16[2,1536,256]{2,1,0:T(8,128)(2,1)} %bitcast.128, ...), custom_call_target="tpu_custom_call" | custom-call | flops 49999998976 | bytes 100000000 | tf_op jit(solution)/shard_map/attend_bwd/pallas_call | solution.py:1470
  659.4 0.7 constant_dynamic-update-slice_fusion.3
  660.2 0.7 pad_maximum_fusion.refs_13_
  661.0 0.8 copy-done.7
  661.8 0.2 copy-done.8
  661.9 130.8 %backward_tail.1 = (bf16[4,3,128,1024]{3,2,1,0:T(8,128)(2,1)}, bf16[4,3,128,1024]{3,2,1,0:T(8,128)(2,1)}, f32[32,1024]{1,0:T(8,128)}, bf16[1024,1024]{1,0:T(8,12...) custom-call(bf16[2,3,4,3,128,256]{5,4,3,2,1,0:T(8,128)(2,1)} %bitcast.97, ...), custom_call_target="tpu_custom_call" | custom-call | flops 2415919104 | bytes 100000000 | tf_op jit(solution)/shard_map/backward_tail/pallas_call | solution.py:436
  792.7 0.9 slice.181
  793.6 0.7 slice_bitcast_fusion.3
  794.3 0.9 slice_bitcast_fusion
  795.3 0.6 slice.204
  795.9 0.6 copy.92
  796.5 1.1 bitcast_dynamic-update-slice_fusion.5
  797.6 1.1 bitcast_dynamic-update-slice_fusion.4
  798.7 1.1 bitcast_dynamic-update-slice_fusion.3
  799.9 3.3 convert_bitcast_fusion
  803.2 3.7 bitcast_convert_fusion
  806.8 3.7 bitcast_convert_fusion.1
  810.5 0.6 copy.109
  811.2 0.6 copy.110
  811.8 0.6 copy.111
  812.4 0.6 copy.112
  813.0 0.6 copy.113
  813.6 0.6 copy.114
  814.2 0.6 copy.115
  814.8 0.6 copy.116
  815.4 4.2 maximum_convert_fusion.1
  819.6 3.9 maximum_convert_fusion
  823.5 1.5 maximum_convert_fusion.2
  (56 shorter events, 0.3 us)
Async XLA Ops:
  1.3 43.7 %collective-permute-start = (s32[1536]{0:T(1024)S(1)}, s32[1536]{0:T(1024)S(1)}, u32[]{:S(2)}, u32[]{:S(2)}) collective-permute-start(s32[1536]{0:T(1024)S(1)} %broadcast_add_fusion), channel_id=1, source_target_pairs={{0,4},{4,8},{8,12},{12,16},{16,20},{20,24},{24,28},{1,5},{5,9},{9,... | collective-permute-start | bytes 18440 | tf_op jit(solution)/shard_map/ppermute | solution.py:1504
  5.1 40.0 %collective-permute-start.1 = (s32[1536]{0:T(1024)S(1)}, s32[1536]{0:T(1024)S(1)}, u32[]{:S(2)}, u32[]{:S(2)}) collective-permute-start(s32[1536]{0:T(1024)S(1)} %broadcast_add_fusion), channel_id=1, source_target_pairs={{4,0},{8,4},{12,8},{16,12},{20,16},{24,20},{28,24},{5,1},{9,5},{13... | collective-permute-start | bytes 18440 | tf_op jit(solution)/shard_map/ppermute | solution.py:1504
  10.7 33.0 %copy-start.11 = (f32[1,1024]{1,0:T(1,128)}, f32[1,1024]{1,0:T(1,128)S(1)}, u32[]{:S(2)}) copy-start(f32[1,1024]{1,0:T(1,128)S(1)} %get-tuple-element.271.refs_12_) | copy-start | bytes 12292
  451.6 154.9 %copy-start.14 = (f32[4608]{0:T(1024)S(1)}, f32[4608]{0:T(1024)}, u32[]{:S(2)}) copy-start(f32[4608]{0:T(1024)} %constant_dynamic-update-slice_fusion) | copy-start | bytes 55300
  607.2 53.8 %collective-permute-start.2 = (bf16[256,1024]{1,0:T(8,128)(2,1)}, bf16[256,1024]{1,0:T(8,128)(2,1)S(1)}, u32[]{:S(2)}, u32[]{:S(2)}) collective-permute-start(bf16[256,1024]{1,0:T(8,128)(2,1)} %get-tuple-element.144), channel_id=1, source_target_pairs={{0,8},{4,12},{8,0},{12,4},{16,24},{20,28},{24,16},{28,20},{1,9},{5... | collective-permute-start | bytes 1572872 | tf_op jit(solution)/shard_map/ppermute | solution.py:1579
  607.2 53.8 %collective-permute-start.3 = (bf16[256,1024]{1,0:T(8,128)(2,1)}, bf16[256,1024]{1,0:T(8,128)(2,1)S(1)}, u32[]{:S(2)}, u32[]{:S(2)}) collective-permute-start(bf16[256,1024]{1,0:T(8,128)(2,1)} %get-tuple-element.146), channel_id=1, source_target_pairs={{0,8},{4,12},{8,0},{12,4},{16,24},{20,28},{24,16},{28,20},{1,9},{5... | collective-permute-start | bytes 1572872 | tf_op jit(solution)/shard_map/ppermute | solution.py:1579
  609.3 50.8 %copy-start.15 = (f32[1,1024]{1,0:T(1,128)S(1)}, f32[1,1024]{1,0:T(1,128)}, u32[]{:S(2)}) copy-start(f32[1,1024]{1,0:T(1,128)} %get-tuple-element.152) | copy-start | bytes 12292
  609.3 50.8 %copy-start.16 = (f32[1,256]{1,0:T(1,128)S(1)}, f32[1,256]{1,0:T(1,128)}, u32[]{:S(2)}) copy-start(f32[1,256]{1,0:T(1,128)} %get-tuple-element.153) | copy-start | bytes 3076
  609.3 50.9 %copy-start.12 = (f32[8,1024]{1,0:T(8,128)S(1)}, f32[8,1024]{1,0:T(8,128)}, u32[]{:S(2)}) copy-start(f32[8,1024]{1,0:T(8,128)} %get-tuple-element.148) | copy-start | bytes 98308
  609.4 50.9 %copy-start.13 = (f32[8,1024]{1,0:T(8,128)S(1)}, f32[8,1024]{1,0:T(8,128)}, u32[]{:S(2)}) copy-start(f32[8,1024]{1,0:T(8,128)} %get-tuple-element.147) | copy-start | bytes 98308
  609.4 50.9 %copy-start.17 = (f32[32]{0:T(128)S(1)}, f32[32]{0:T(128)}, u32[]{:S(2)}) copy-start(f32[32]{0:T(128)} %pad.13.clone) | copy-start | bytes 388
  661.0 0.8 copy-start.7
  661.0 1.0 copy-start.8
  792.7 7.0 copy-start.6
  799.9 3.3 copy-start.1
  803.2 3.7 copy-start
  806.8 8.6 %copy-start.3 = (bf16[1024,1024]{1,0:T(8,128)(2,1)S(1)}, bf16[1024,1024]{1,0:T(8,128)(2,1)}, u32[]{:S(2)}) copy-start(bf16[1024,1024]{1,0:T(8,128)(2,1)} %get-tuple-element.165) | copy-start | bytes 6291460
  806.8 8.6 %copy-start.5 = (bf16[1024,1024]{1,0:T(8,128)(2,1)S(1)}, bf16[1024,1024]{1,0:T(8,128)(2,1)}, u32[]{:S(2)}) copy-start(bf16[1024,1024]{1,0:T(8,128)(2,1)} %get-tuple-element.164) | copy-start | bytes 6291460
  815.4 4.2 copy-start.2
  815.4 4.2 copy-start.4
  819.6 3.9 copy-start.9
  819.6 4.0 copy-start.10

commit v5 on v4

--- a/solution.py
+++ b/solution.py
@@ -1066,14 +1066,11 @@
         names = ((N.keep1, N.send1), (N.keep2, N.send2))[a]
         first_sum.split(a, getattr(r, names[0] + N._out), getattr(r, names[1] + N._out))
         r.store(names[0] + N._out)
-        if first:
-            got = r.targets[(N.got1_out, N.got2_out)[a]]
-            cp = first_sum.copy(getattr(r, names[1] + N._out), got, a, 1, 1)
-            cp.start()
-            first_sum.pending.append(cp)
-            arrivals.append(cp)
-        else:
-            r.store(names[1] + N._out)
+        got = r.targets[(N.got1_out, N.got2_out)[a]]
+        cp = first_sum.copy(getattr(r, names[1] + N._out), got, a, 1, 1)
+        cp.start()
+        first_sum.pending.append(cp)
+        arrivals.append(cp)
 
     arrivals = []
     extra += [(behind - chunks, lambda: first_sum.send(0, 0)), (behind - chunks + 1, lambda: part_of(0))]
@@ -1166,11 +1163,8 @@
         keep, send, got = ((N.keep1_out, N.send1_out, N.got1_out), (N.keep2_out, N.send2_out, N.got2_out))[i]
         quarter = (rows // 4, cols)
         outs += [(keep, quarter, BF16, True)]
-        if first:
-            quarters += [(send, pltpu.VMEM(quarter, BF16))]
-            outs += [(got, quarter, BF16, N.far)]
-        else:
-            outs += [(send, quarter, BF16, True)]
+        quarters += [(send, pltpu.VMEM(quarter, BF16))]
+        outs += [(got, quarter, BF16, N.far)]
     scratch = quarters + comm_scratch(n, chunks, sub, "") + [(N.e1, pltpu.VMEM(split(D), BF16))] + sem_scratch(4, n, chunks)
     scratch += [(N.g1, pltpu.VMEM((hidden, D), BF16)), (N.g2, pltpu.VMEM((D, hidden), BF16))]
     scratch += [(N.core_recv0, pltpu.VMEM((hidden // 2, D), BF16)), (N.core_recv1, pltpu.VMEM((D // 2, hidden), BF16))]
@@ -1570,13 +1564,10 @@
         if above:
             grads[level + 1] = [outs["up%d_out" % (i + 1)] for i in range(4)]
             dv_sums[level + 1] = outs[N.dv_sum][0]
-        flip = [(i, i ^ 2) for i in range(dp_size)]
         above = {N.up4: outs[N.g4]}
         for name in "12":
             above[N.keep + name] = outs[N.keep + name + N._out]
-            got = N.got + name + N._out
-            send = N.send + name + N._out
-            above[N.got + name] = outs[got] if got in outs else lax.ppermute(outs[send], N.dp, flip)
+            above[N.got + name] = outs[N.got + name + N._out]
         dq, dkv, q_sum = attend_bwd(
             q, *kv, idq, idk, lo, hi, attended, datt.reshape(rows, width), lse, *TILES
         )

time: 829 us -> 832 us (level)
  transfers between devices with their start and end apart: 4 -> 2, of which waited for: 0 -> 0; matrix products, arithmetic and copies ran while one was open for 2% -> 1% of each run, Pallas kernels for 9% -> 3%
where the time goes in v5:
time: 832 us; the launch traced here: 822 us
  Pallas kernels  760 us (91%)
  other arithmetic  27.5 us (3%)
  local copies, waits for them, and re-layouts  26.9 us (3%)
    pallas_call x6, Pallas kernels, call(): pl.pallas_call(entry, out_shape=[jax.ShapeDtypeStruct(shape, dtype) for _...  581 us
    pallas_call x2, Pallas kernels, attend_bwd(): pl.pallas_call(functools.partial(bwd_kernel, HH, QB, KB, KT, nq), grid_sp...  100 us
    pallas_call x2, Pallas kernels, attend_fwd(): pl.pallas_call(functools.partial(fwd_kernel, HH, QB, KB, KT, nq), grid_sp...  78.7 us
  transfers between devices with their start and end apart: 2, of which 0 were waited for; matrix products, arithmetic and copies ran while one was open for 1% of the time, Pallas kernels for 3%

profile of v5, /device:TPU:17, one launch (start us, length us, event | category | flops | bytes accessed | tf_op | source)
XLA Modules:
  0.0 821.5 jit_solution(10593739850239994034)
XLA Ops:
  0.6 0.7 broadcast_add_fusion
  1.3 3.8 collective-permute-start
  5.1 1.9 collective-permute-start.1
  7.0 0.2 slice_reduce_fusion
  7.2 1.3 slice_bitcast_fusion.4
  8.5 1.4 fusion.13
  9.9 0.8 fusion.14
  10.7 0.0 copy-start.9
  10.7 0.6 pad_maximum_fusion.3.refs_3_
  11.3 0.8 fusion.7
  12.1 0.8 fusion.11
  12.9 0.8 fusion.9
  13.7 27.2 %first_block.1 = (f32[3,128,1024]{2,1,0:T(8,128)}, f32[3,128,1024]{2,1,0:T(8,128)}, f32[3,128,1]{2,1,0:T(8,128)}, bf16[4,3,128,1024]{3,2,1,0:T(8,128)(2,1)}, bf1...) custom-call(bf16[4,3,128,1024]{3,2,1,0:T(8,128)(2,1)} %bitcast.122, ...), custom_call_target="tpu_custom_call" | custom-call | flops 2415919104 | bytes 100000000 | tf_op jit(solution)/shard_map/first_block/pallas_call | solution.py:436
  40.9 0.6 pad_maximum_fusion.1
  41.5 0.6 constant_dynamic-update-slice_fusion
  42.1 1.1 broadcast_in_dim.24.idq_ref
  43.3 0.5 pad.13.clone
  43.8 0.7 stack.96.refs_6_
  44.5 0.7 stack.95.refs_6_
  45.1 0.0 collective-permute-done
  45.1 0.0 collective-permute-done.1
  45.1 0.1 rev.3
  45.2 3.1 broadcast_in_dim.25.idk_ref
  48.3 0.7 iota_reduce_fusion.1
  49.1 0.7 iota_reduce_fusion
  49.8 0.7 fusion.2
  50.4 0.6 fusion.4
  51.1 1.9 pad_add_fusion.1
  53.0 39.2 %attend_fwd.2 = (bf16[1536,256]{1,0:T(8,128)(2,1)}, f32[1,4,1536]{2,1,0:T(4,128)}) custom-call(s32[4]{0:T(128)} %get-tuple-element.273.lo_ref, s32[4]{0:T(128)} %get-tuple-element.274.hi_ref, bf16[1536,256]{1,0:T(8,128)(2,1)} %bitcast.133, bf16[2,1536,256]{2,1,0:T(8,128)(2,1)} %bitcast.125, bf16[2,1536,256]{2,1,0:T(8,128)(2,1)} %bitcast.127, ...), custom_call_target="tpu_custom_call" | custom-call | flops 49999998976 | bytes 100000000 | tf_op jit(solution)/shard_map/attend_fwd/pallas_call | solution.py:1359
  92.2 118.6 %forward_block.1 = (f32[3,128,1024]{2,1,0:T(8,128)}, f32[3,128,1024]{2,1,0:T(8,128)}, f32[3,128,1]{2,1,0:T(8,128)}, f32[3,128,1024]{2,1,0:T(8,128)}, bf16[4,3,12...) custom-call(bf16[4,3,128,256]{3,2,1,0:T(8,128)(2,1)} %bitcast.104, ...), custom_call_target="tpu_custom_call" | custom-call | flops 9663676416 | bytes 100000000 | tf_op jit(solution)/shard_map/forward_block/pallas_call | solution.py:436
  210.8 39.5 %attend_fwd.3 = (bf16[1536,256]{1,0:T(8,128)(2,1)}, f32[1,4,1536]{2,1,0:T(4,128)}) custom-call(s32[4]{0:T(128)} %get-tuple-element.273.lo_ref, s32[4]{0:T(128)} %get-tuple-element.274.hi_ref, bf16[1536,256]{1,0:T(8,128)(2,1)} %bitcast.139, bf16[2,1536,256]{2,1,0:T(8,128)(2,1)} %bitcast.129, bf16[2,1536,256]{2,1,0:T(8,128)(2,1)} %bitcast.131, ...), custom_call_target="tpu_custom_call" | custom-call | flops 49999998976 | bytes 100000000 | tf_op jit(solution)/shard_map/attend_fwd/pallas_call | solution.py:1359
  250.3 84.8 %forward_last.1 = (f32[3,128,1024]{2,1,0:T(8,128)}, f32[3,128,1024]{2,1,0:T(8,128)}, f32[3,128,1]{2,1,0:T(8,128)}, f32[3,128,1024]{2,1,0:T(8,128)}, bf16[4,3,128...) custom-call(bf16[4,3,128,256]{3,2,1,0:T(8,128)(2,1)} %bitcast.145, ...), custom_call_target="tpu_custom_call" | custom-call | flops 9663676416 | bytes 100000000 | tf_op jit(solution)/shard_map/forward_last/pallas_call | solution.py:436
  335.1 66.0 %backward_first.1 = (bf16[4,3,128,256]{3,2,1,0:T(8,128)(2,1)}, f32[3,128,1024]{2,1,0:T(8,128)}, f32[8,1024]{1,0:T(8,128)}, f32[1,1024]{1,0:T(1,128)}, bf16[256,1...) custom-call(bf16[4,3,128,1024]{3,2,1,0:T(8,128)(2,1)} %bitcast.123, ...), custom_call_target="tpu_custom_call" | custom-call | flops 9663676416 | bytes 100000000 | tf_op jit(solution)/shard_map/backward_first/pallas_call | solution.py:436
  401.0 50.4 %attend_bwd.2 = (bf16[1536,256]{1,0:T(8,128)(2,1)}, bf16[2,4608,256]{2,1,0:T(8,128)(2,1)}, f32[1,256]{1,0:T(1,128)}) custom-call(s32[4]{0:T(128)} %get-tuple-element.273.lo_ref, s32[4]{0:T(128)} %get-tuple-element.274.hi_ref, bf16[1536,256]{1,0:T(8,128)(2,1)} %bitcast.140, bf16[2,1536,256]{2,1,0:T(8,128)(2,1)} %bitcast.130, bf16[2,1536,256]{2,1,0:T(8,128)(2,1)} %bitcast.132, ...), custom_call_target="tpu_custom_call" | custom-call | flops 49999998976 | bytes 100000000 | tf_op jit(solution)/shard_map/attend_bwd/pallas_call | solution.py:1464
  451.4 151.7 %backward_block.1 = (bf16[4,3,128,256]{3,2,1,0:T(8,128)(2,1)}, f32[3,128,1024]{2,1,0:T(8,128)}, f32[8,1024]{1,0:T(8,128)}, f32[1,1024]{1,0:T(1,128)}, bf16[256,1...) custom-call(bf16[2,3,4,3,128,256]{5,4,3,2,1,0:T(8,128)(2,1)} %bitcas, ...), custom_call_target="tpu_custom_call" | custom-call | flops 9663676416 | bytes 100000000 | tf_op jit(solution)/shard_map/backward_block/pallas_call | solution.py:436
  603.1 0.7 constant_dynamic-update-slice_fusion.6
  603.8 0.7 constant_dynamic-update-slice_fusion.4
  604.5 0.0 copy-start.15
  604.5 50.1 %attend_bwd.3 = (bf16[1536,256]{1,0:T(8,128)(2,1)}, bf16[2,4608,256]{2,1,0:T(8,128)(2,1)}, f32[1,256]{1,0:T(1,128)}) custom-call(s32[4]{0:T(128)} %get-tuple-element.273.lo_ref, s32[4]{0:T(128)} %get-tuple-element.274.hi_ref, bf16[1536,256]{1,0:T(8,128)(2,1)} %bitcast.134, bf16[2,1536,256]{2,1,0:T(8,128)(2,1)} %bitcast.126, bf16[2,1536,256]{2,1,0:T(8,128)(2,1)} %bitcast.128, ...), custom_call_target="tpu_custom_call" | custom-call | flops 49999998976 | bytes 100000000 | tf_op jit(solution)/shard_map/attend_bwd/pallas_call | solution.py:1464
  654.5 0.7 constant_dynamic-update-slice_fusion.3
  655.3 0.7 pad_maximum_fusion.refs_13_
  656.1 132.9 %backward_tail.1 = (bf16[4,3,128,1024]{3,2,1,0:T(8,128)(2,1)}, bf16[4,3,128,1024]{3,2,1,0:T(8,128)(2,1)}, f32[32,1024]{1,0:T(8,128)}, bf16[1024,1024]{1,0:T(8,12...) custom-call(bf16[2,3,4,3,128,256]{5,4,3,2,1,0:T(8,128)(2,1)} %bitcast.97, ...), custom_call_target="tpu_custom_call" | custom-call | flops 2415919104 | bytes 100000000 | tf_op jit(solution)/shard_map/backward_tail/pallas_call | solution.py:436
  789.0 0.9 slice.181
  789.9 0.7 slice_bitcast_fusion.3
  790.6 0.9 slice_bitcast_fusion
  791.6 0.6 slice.204
  792.2 0.6 copy.92
  792.8 1.1 bitcast_dynamic-update-slice_fusion.5
  793.9 1.1 bitcast_dynamic-update-slice_fusion.4
  794.9 1.1 bitcast_dynamic-update-slice_fusion.3
  796.2 3.3 convert_bitcast_fusion
  799.5 3.7 bitcast_convert_fusion
  803.1 3.7 bitcast_convert_fusion.1
  806.8 0.6 copy.109
  807.4 0.6 copy.110
  808.0 0.6 copy.111
  808.6 0.6 copy.112
  809.2 0.6 copy.113
  809.8 0.6 copy.114
  810.5 0.6 copy.115
  811.1 0.6 copy.116
  811.7 4.2 maximum_convert_fusion.1
  815.9 3.9 maximum_convert_fusion
  819.8 1.5 maximum_convert_fusion.2
  (48 shorter events, 0.3 us)
Async XLA Ops:
  1.3 43.8 %collective-permute-start = (s32[1536]{0:T(1024)S(1)}, s32[1536]{0:T(1024)S(1)}, u32[]{:S(2)}, u32[]{:S(2)}) collective-permute-start(s32[1536]{0:T(1024)S(1)} %broadcast_add_fusion), channel_id=1, source_target_pairs={{0,4},{4,8},{8,12},{12,16},{16,20},{20,24},{24,28},{1,5},{5,9},{9,... | collective-permute-start | bytes 18440 | tf_op jit(solution)/shard_map/ppermute | solution.py:1498
  5.1 40.0 %collective-permute-start.1 = (s32[1536]{0:T(1024)S(1)}, s32[1536]{0:T(1024)S(1)}, u32[]{:S(2)}, u32[]{:S(2)}) collective-permute-start(s32[1536]{0:T(1024)S(1)} %broadcast_add_fusion), channel_id=1, source_target_pairs={{4,0},{8,4},{12,8},{16,12},{20,16},{24,20},{28,24},{5,1},{9,5},{13... | collective-permute-start | bytes 18440 | tf_op jit(solution)/shard_map/ppermute | solution.py:1498
  10.7 33.1 %copy-start.9 = (f32[1,1024]{1,0:T(1,128)}, f32[1,1024]{1,0:T(1,128)S(1)}, u32[]{:S(2)}) copy-start(f32[1,1024]{1,0:T(1,128)S(1)} %get-tuple-element.271.refs_12_) | copy-start | bytes 12292
  451.4 151.7 %copy-start.12 = (f32[4608]{0:T(1024)S(1)}, f32[4608]{0:T(1024)}, u32[]{:S(2)}) copy-start(f32[4608]{0:T(1024)} %constant_dynamic-update-slice_fusion) | copy-start | bytes 55300
  604.4 50.8 %copy-start.13 = (f32[1,1024]{1,0:T(1,128)S(1)}, f32[1,1024]{1,0:T(1,128)}, u32[]{:S(2)}) copy-start(f32[1,1024]{1,0:T(1,128)} %get-tuple-element.152) | copy-start | bytes 12292
  604.4 50.8 %copy-start.14 = (f32[1,256]{1,0:T(1,128)S(1)}, f32[1,256]{1,0:T(1,128)}, u32[]{:S(2)}) copy-start(f32[1,256]{1,0:T(1,128)} %get-tuple-element.153) | copy-start | bytes 3076
  604.4 50.9 %copy-start.10 = (f32[8,1024]{1,0:T(8,128)S(1)}, f32[8,1024]{1,0:T(8,128)}, u32[]{:S(2)}) copy-start(f32[8,1024]{1,0:T(8,128)} %get-tuple-element.148) | copy-start | bytes 98308
  604.4 50.9 %copy-start.11 = (f32[8,1024]{1,0:T(8,128)S(1)}, f32[8,1024]{1,0:T(8,128)}, u32[]{:S(2)}) copy-start(f32[8,1024]{1,0:T(8,128)} %get-tuple-element.147) | copy-start | bytes 98308
  604.5 50.9 %copy-start.15 = (f32[32]{0:T(128)S(1)}, f32[32]{0:T(128)}, u32[]{:S(2)}) copy-start(f32[32]{0:T(128)} %pad.13.clone) | copy-start | bytes 388
  789.0 7.0 copy-start.6
  796.2 3.3 copy-start.1
  799.5 3.7 copy-start
  803.1 8.6 %copy-start.3 = (bf16[1024,1024]{1,0:T(8,128)(2,1)S(1)}, bf16[1024,1024]{1,0:T(8,128)(2,1)}, u32[]{:S(2)}) copy-start(bf16[1024,1024]{1,0:T(8,128)(2,1)} %get-tuple-element.165) | copy-start | bytes 6291460
  803.1 8.6 %copy-start.5 = (bf16[1024,1024]{1,0:T(8,128)(2,1)S(1)}, bf16[1024,1024]{1,0:T(8,128)(2,1)}, u32[]{:S(2)}) copy-start(bf16[1024,1024]{1,0:T(8,128)(2,1)} %get-tuple-element.164) | copy-start | bytes 6291460
  811.7 4.2 copy-start.2
  811.7 4.2 copy-start.4
  815.9 3.9 copy-start.7
  815.9 4.0 copy-start.8
